TPU v7x, 512 devices: a whole 4x4x16 slice. The times are simulated.
512 devices in a mesh: group: 16 (over x, y), sub: 32 (over z, core).
Axes of the slice: x: 4, y: 4, z: 16, core: 2. Of those that a mesh axis runs over, the one named last changes fastest.
Arguments:
- source: float32 [128, 1024, 256], P('group', 'sub'), may hold values from -70 to 70
- perm: float32 [128, 1024, 256], P('group', 'sub'), may hold values from 0.2 to 5
- storage: float32 [128, 1024, 256], P('group', 'sub'), may hold values from 0.05 to 0.5
Outputs:
- pressure: float32 [128, 1024, 256], P('group', 'sub')
- preconditioned: float32 [128, 1024, 256], P('group', 'sub')
All inputs are finite; a program needn't handle non-finite values.
Results may differ from a plain program's by a relative error of at most 0.0003.
Values sent between devices are 32-bit elements; how exact they have to be, the bound alone decides.
No kernel may reach another device: no remote copies, remote signals or barrier semaphores. Data moves between devices by JAX's collectives and lax.ppermute only.
A program may use at most 64 MiB of HBM per device.

v0:
```python
import jax
import jax.numpy as jnp
from jax import lax
from jax.sharding import PartitionSpec as P

SWEEPS = 4
ITERS = 2


OMEGA = 0.8


def with_halo(shard, sides, width):
    for axis, dim in sides:
        peers, length = (lax.axis_size(axis), shard.shape[dim])
        up = [(i, (i + 1) % peers) for i in range(peers)]
        down = [(j, i) for i, j in up]
        last = lax.slice_in_dim(shard, length - width, length, axis=dim)
        leading = lax.slice_in_dim(shard, 0, width, axis=dim)
        before = lax.ppermute(last, axis, up)
        after = lax.ppermute(leading, axis, down)
        shard = jnp.concatenate([before, shard, after], axis=dim)
    return shard


def harmonic(left, right):
    return 2.0 * left * right / (left + right)


def assemble(diag_all, off_all):
    count = diag_all.shape[0]
    index = jnp.arange(count)
    following = (index + 1) % count
    rows = index[:, None]
    cols = index[None, :]
    matrix = jnp.where(rows == cols, diag_all[:, None], jnp.float32(0.0))
    matrix = matrix + jnp.where(cols == following[:, None], off_all[:, None], jnp.float32(0.0))
    matrix = matrix + jnp.where(rows == following[None, :], off_all[None, :], jnp.float32(0.0))
    return matrix


def solve_coarse(factor, sums):
    return jax.scipy.linalg.cho_solve((factor, True), sums)


def shards(source, perm, storage):
    padded = with_halo(perm, (("group", 0), ("sub", 1)), 1)
    east_face = harmonic(perm, padded[2:, 1:-1])
    west_face = harmonic(padded[:-2, 1:-1], perm)
    north_face = harmonic(perm, padded[1:-1, 2:])
    south_face = harmonic(padded[1:-1, :-2], perm)
    upper_face = harmonic(perm, jnp.roll(perm, -1, 2))
    lower_face = jnp.roll(upper_face, 1, 2)
    diagonal = storage + east_face + west_face + north_face + south_face + upper_face + lower_face

    def local_operator(field):
        east_value = jnp.pad(field[1:], ((0, 1), (0, 0), (0, 0)))
        west_value = jnp.pad(field[:-1], ((1, 0), (0, 0), (0, 0)))
        north_value = jnp.pad(field[:, 1:], ((0, 0), (0, 1), (0, 0)))
        south_value = jnp.pad(field[:, :-1], ((0, 0), (1, 0), (0, 0)))
        total = diagonal * field
        total = total - east_face * east_value - west_face * west_value
        total = total - north_face * north_value - south_face * south_value
        total = total - upper_face * jnp.roll(field, -1, 2) - lower_face * jnp.roll(field, 1, 2)
        return total

    members = lax.axis_size("sub")
    north_sum = jnp.sum(north_face[:, -1])
    south_sum = jnp.sum(south_face[:, 0])
    coarse_diag = jnp.sum(storage) / members + members * (north_sum + south_sum)
    coarse_off = -members * north_sum
    diag_all, off_all = (
        lax.all_gather(coarse_diag[None], "sub", axis=0, tiled=True),
        lax.all_gather(coarse_off[None], "sub", axis=0, tiled=True),
    )
    factor = jnp.linalg.cholesky(assemble(diag_all, off_all))
    selector = (jnp.arange(diag_all.shape[0]) == lax.axis_index("sub")).astype(jnp.float32)

    def precondition(resid, wanted):
        smooth = OMEGA * resid / diagonal
        for sweep in range(SWEEPS - 1):
            smooth = smooth + OMEGA * (resid - local_operator(smooth)) / diagonal
        sums = lax.all_gather(jnp.sum(resid)[None], "sub", axis=0, tiled=True)
        coarse = solve_coarse(factor, sums)
        result = smooth + jnp.sum(selector * coarse)
        inner = lax.psum(jnp.sum(resid * result), ("group", "sub")) if wanted else None
        return (result, inner)

    pressure = jnp.zeros_like(source)
    resid = source
    precond, inner_now = precondition(resid, True)
    direction = precond
    for step in range(ITERS):
        halo_field = with_halo(direction, (("group", 0), ("sub", 1)), 1)
        operate_total = storage * direction
        operate_total = (
            operate_total
            + east_face * (direction - halo_field[2:, 1:-1])
            + west_face * (direction - halo_field[:-2, 1:-1])
        )
        operate_total = (
            operate_total
            + north_face * (direction - halo_field[1:-1, 2:])
            + south_face * (direction - halo_field[1:-1, :-2])
        )
        operate_total = (
            operate_total
            + upper_face * (direction - jnp.roll(direction, -1, 2))
            + lower_face * (direction - jnp.roll(direction, 1, 2))
        )
        step_size = inner_now / lax.psum(jnp.sum(direction * operate_total), ("group", "sub"))
        pressure = pressure + step_size * direction
        resid = resid - step_size * operate_total
        wanted = step + 1 < ITERS
        precond, inner_next = precondition(resid, wanted)
        if wanted:
            direction = precond + inner_next / inner_now * direction
            inner_now = inner_next
    return (pressure, precond)


def solution(mesh):
    in_specs = (P("group", "sub", None), P("group", "sub", None), P("group", "sub", None))
    out_specs = (P("group", "sub", None), P("group", "sub", None))
    return jax.shard_map(shards, mesh=mesh, in_specs=in_specs, out_specs=out_specs, check_vma=False)
```

profile of v0, /device:TPU:1, one launch (start us, length us, event | category | flops | bytes accessed | tf_op | source)
XLA Modules:
  0.0 547.8 jit_solution(2187185016459888428)
XLA Ops:
  0.6 0.8 fusion.164
  1.5 4.0 collective-permute-start.1
  5.5 5.6 %collective-permute-start = (f32[1,32,256]{2,1,0:T(8,128)S(1)}, f32[1,32,256]{2,1,0:T(8,128)S(1)}, u32[]{:S(2)}, u32[]{:S(2)}) collective-permute-start(f32[1,32,256]{2,1,0:T(8,128)S(1)} %get-tuple-element.118), channel_id=1, source_target_pairs={{32,0},{64,32},{96,64},{128,96},{160,128},{192,160},{224,192},{256... | collective-permute-start | bytes 98312 | tf_op jit(solution)/shard_map/ppermute | solution.py:21
  12.2 7.0 %collective-permute-start.2 = (f32[10,1,256]{2,1,0:T(1,128)S(1)}, f32[10,1,256]{2,1,0:T(1,128)S(1)}, u32[]{:S(2)}, u32[]{:S(2)}) collective-permute-start(f32[10,1,256]{2,1,0:T(1,128)S(1)} %get-tuple-element.28), channel_id=1, source_target_pairs={{1,0},{2,1},{3,2},{4,3},{5,4},{6,5},{7,6},{8,7},{9,8},{10,9},{11,1... | collective-permute-start | bytes 30728 | tf_op jit(solution)/shard_map/ppermute | solution.py:21
  19.1 1.2 dynamic-slice
  20.5 2.0 collective-permute-done.3
  31.7 1.2 dynamic-update-slice.5
  32.9 48.8 %all-reduce.42 = (f32[32]{0:T(128)S(1)}, f32[32]{0:T(128)S(1)}, f32[32]{0:T(128)S(1)}) all-reduce(f32[32]{0:T(128)S(1)} %dynamic-update-slice.3, f32[32]{0:T(128)S(1)} %dynamic-update-slice.4, f32[32]{0:T(128)S(1)} %dynamic-update-slice.5), channel_id=1, replica_groups=mesh['group'=16,'sub'=32] {'sub'}, use_global_device_ids=true, to_apply=%add.36 | all-reduce | flops 96 | bytes 768
  81.8 2.9 cholesky.19
  86.0 2.4 custom-call.10
  89.3 2.1 fusion.102
  91.5 6.9 %collective-permute-start.4 = (f32[1,32,256]{2,1,0:T(8,128)S(1)}, f32[1,32,256]{2,1,0:T(8,128)S(1)}, u32[]{:S(2)}, u32[]{:S(2)}) collective-permute-start(f32[1,32,256]{2,1,0:T(8,128)S(1)} %get-tuple-element.84), channel_id=1, source_target_pairs={{32,0},{64,32},{96,64},{128,96},{160,128},{192,160},{224,192},{256... | collective-permute-start | bytes 98312 | tf_op jit(solution)/shard_map/ppermute | solution.py:21
  98.4 1.9 collective-permute-start.5
  100.4 5.9 %collective-permute-done.5 = f32[1,32,256]{2,1,0:T(8,128)S(1)} collective-permute-done((f32[1,32,256]{2,1,0:T(8,128)S(1)}, f32[1,32,256]{2,1,0:T(8,128)S(1)}, u32[]{:S(2)}, u32[]{:S(2)}) %collective-permute-start.5) | collective-permute-done | bytes 32800 | tf_op jit(solution)/shard_map/ppermute | solution.py:20
  106.6 1.9 collective-permute-start.6
  109.7 1.0 multiply_reduce_fusion.2
  110.7 102.9 %all-reduce.41 = (f32[]{:T(128)}, f32[]{:T(128)}) all-reduce(f32[]{:T(128)} %get-tuple-element.4, f32[]{:T(128)} %get-tuple-element.3), channel_id=1, replica_groups=mesh['group'=16,'sub'=32] {'group','sub'}, use_global_device_ids=true, to_apply=%region_8.10 | all-reduce | flops 2 | bytes 16 | tf_op jit(solution)/shard_map/psum | solution.py:86
  219.9 1.3 dynamic-update-slice.6
  221.2 45.8 %all-reduce.39 = f32[32]{0:T(128)S(1)} all-reduce(f32[32]{0:T(128)S(1)} %dynamic-update-slice.6), channel_id=1, replica_groups=mesh['group'=16,'sub'=32] {'sub'}, use_global_device_ids=true, to_apply=%add.39 | all-reduce | flops 32 | bytes 256
  267.9 3.5 multiply_reduce_fusion.1
  271.4 98.6 %psum.30 = f32[]{:T(128)} all-reduce(f32[]{:T(128)} %get-tuple-element.14), channel_id=1, replica_groups=mesh['group'=16,'sub'=32] {'group','sub'}, use_global_device_ids=true, to_apply=%region_14.16 | all-reduce | flops 1 | bytes 8 | tf_op jit(solution)/shard_map/psum | solution.py:86
  371.3 1.0 multiply_add_fusion.1
  372.3 3.5 collective-permute-start.8
  375.8 1.9 collective-permute-start.9
  377.9 5.9 %collective-permute-done.9 = f32[1,32,256]{2,1,0:T(8,128)S(1)} collective-permute-done((f32[1,32,256]{2,1,0:T(8,128)S(1)}, f32[1,32,256]{2,1,0:T(8,128)S(1)}, u32[]{:S(2)}, u32[]{:S(2)}) %collective-permute-start.9) | collective-permute-done | bytes 32800 | tf_op jit(solution)/shard_map/ppermute | solution.py:20
  383.8 3.3 collective-permute-start.11
  388.0 2.3 collective-permute-done.10
  390.3 1.0 multiply_reduce_fusion
  391.2 99.6 %psum.31 = f32[]{:T(128)} all-reduce(f32[]{:T(128)} %get-tuple-element.12), channel_id=1, replica_groups=mesh['group'=16,'sub'=32] {'group','sub'}, use_global_device_ids=true, to_apply=%region_16.18 | all-reduce | flops 1 | bytes 8 | tf_op jit(solution)/shard_map/psum | solution.py:111
  497.1 1.3 dynamic-update-slice.7
  498.4 45.8 %all-reduce.40 = f32[32]{0:T(128)S(1)} all-reduce(f32[32]{0:T(128)S(1)} %dynamic-update-slice.7), channel_id=1, replica_groups=mesh['group'=16,'sub'=32] {'sub'}, use_global_device_ids=true, to_apply=%add.40 | all-reduce | flops 32 | bytes 256
  545.1 2.8 fusion.100
  (100 shorter events, 24.3 us)
Async XLA Ops:
  0.6 10.4 %copy-start = (f32[8,32,256]{2,1,0:T(8,128)S(1)}, f32[8,32,256]{2,1,0:T(8,128)}, u32[]{:S(2)}) copy-start(f32[8,32,256]{2,1,0:T(8,128)} %param.6) | copy-start | bytes 786436
  1.5 9.7 %collective-permute-start.1 = (f32[1,32,256]{2,1,0:T(8,128)S(1)}, f32[1,32,256]{2,1,0:T(8,128)S(1)}, u32[]{:S(2)}, u32[]{:S(2)}) collective-permute-start(f32[1,32,256]{2,1,0:T(8,128)S(1)} %get-tuple-element.117), channel_id=1, source_target_pairs={{0,32},{32,64},{64,96},{96,128},{128,160},{160,192},{192,224},{224... | collective-permute-start | bytes 98312 | tf_op jit(solution)/shard_map/ppermute | solution.py:20
  5.5 6.6 %collective-permute-start = (f32[1,32,256]{2,1,0:T(8,128)S(1)}, f32[1,32,256]{2,1,0:T(8,128)S(1)}, u32[]{:S(2)}, u32[]{:S(2)}) collective-permute-start(f32[1,32,256]{2,1,0:T(8,128)S(1)} %get-tuple-element.118), channel_id=1, source_target_pairs={{32,0},{64,32},{96,64},{128,96},{160,128},{192,160},{224,192},{256... | collective-permute-start | bytes 98312 | tf_op jit(solution)/shard_map/ppermute | solution.py:21
  11.1 0.9 slice-start
  12.0 10.5 %copy-start.2 = (f32[8,32,256]{2,1,0:T(8,128)S(1)}, f32[8,32,256]{2,1,0:T(8,128)}, u32[]{:S(2)}) copy-start(f32[8,32,256]{2,1,0:T(8,128)} %param.5) | copy-start | bytes 786436
  12.1 10.4 %copy-start.1 = (f32[8,32,256]{2,1,0:T(8,128)S(1)}, f32[8,32,256]{2,1,0:T(8,128)}, u32[]{:S(2)}) copy-start(f32[8,32,256]{2,1,0:T(8,128)} %param.7) | copy-start | bytes 786436
  12.2 8.3 %collective-permute-start.2 = (f32[10,1,256]{2,1,0:T(1,128)S(1)}, f32[10,1,256]{2,1,0:T(1,128)S(1)}, u32[]{:S(2)}, u32[]{:S(2)}) collective-permute-start(f32[10,1,256]{2,1,0:T(1,128)S(1)} %get-tuple-element.28), channel_id=1, source_target_pairs={{1,0},{2,1},{3,2},{4,3},{5,4},{6,5},{7,6},{8,7},{9,8},{10,9},{11,1... | collective-permute-start | bytes 30728 | tf_op jit(solution)/shard_map/ppermute | solution.py:21
  19.1 3.3 collective-permute-start.3
  91.5 9.0 %collective-permute-start.4 = (f32[1,32,256]{2,1,0:T(8,128)S(1)}, f32[1,32,256]{2,1,0:T(8,128)S(1)}, u32[]{:S(2)}, u32[]{:S(2)}) collective-permute-start(f32[1,32,256]{2,1,0:T(8,128)S(1)} %get-tuple-element.84), channel_id=1, source_target_pairs={{32,0},{64,32},{96,64},{128,96},{160,128},{192,160},{224,192},{256... | collective-permute-start | bytes 98312 | tf_op jit(solution)/shard_map/ppermute | solution.py:21
  98.4 8.0 %collective-permute-start.5 = (f32[1,32,256]{2,1,0:T(8,128)S(1)}, f32[1,32,256]{2,1,0:T(8,128)S(1)}, u32[]{:S(2)}, u32[]{:S(2)}) collective-permute-start(f32[1,32,256]{2,1,0:T(8,128)S(1)} %get-tuple-element.83), channel_id=1, source_target_pairs={{0,32},{32,64},{64,96},{96,128},{128,160},{160,192},{192,224},{224... | collective-permute-start | bytes 98312 | tf_op jit(solution)/shard_map/ppermute | solution.py:20
  106.4 2.8 collective-permute-start.7
  106.6 3.1 collective-permute-start.6
  372.3 5.6 %collective-permute-start.8 = (f32[1,32,256]{2,1,0:T(8,128)S(1)}, f32[1,32,256]{2,1,0:T(8,128)S(1)}, u32[]{:S(2)}, u32[]{:S(2)}) collective-permute-start(f32[1,32,256]{2,1,0:T(8,128)S(1)} %get-tuple-element.54), channel_id=1, source_target_pairs={{32,0},{64,32},{96,64},{128,96},{160,128},{192,160},{224,192},{256... | collective-permute-start | bytes 98312 | tf_op jit(solution)/shard_map/ppermute | solution.py:21
  375.8 8.0 %collective-permute-start.9 = (f32[1,32,256]{2,1,0:T(8,128)S(1)}, f32[1,32,256]{2,1,0:T(8,128)S(1)}, u32[]{:S(2)}, u32[]{:S(2)}) collective-permute-start(f32[1,32,256]{2,1,0:T(8,128)S(1)} %get-tuple-element.53), channel_id=1, source_target_pairs={{0,32},{32,64},{64,96},{96,128},{128,160},{160,192},{192,224},{224... | collective-permute-start | bytes 98312 | tf_op jit(solution)/shard_map/ppermute | solution.py:20
  383.8 4.2 collective-permute-start.11
  387.2 3.1 collective-permute-start.10
where the time goes:
time: 549 us; the launch traced here: 548 us
  blocking collectives  441 us (80%)
  starting transfers between devices  36.3 us (7%)
  other arithmetic  25 us (5%)
  waiting for transfers between devices  17.9 us (3%)
  local copies, waits for them, and re-layouts  17.1 us (3%)
  between operations  7.46 us (1%)
    psum x2, blocking collectives, precondition(): lax.psum(jnp.sum(resid * result), ('group', 'sub'))  202 us
    unnamed x3, blocking collectives  140 us
    psum x1, blocking collectives, shards(): lax.psum(jnp.sum(direction * operate_total), ('group', 'sub'))  99.6 us
    ppermute x6, starting transfers between devices, with_halo(): after = lax.ppermute(leading, axis, down)  24.8 us
    ppermute x6, waiting for transfers between devices, with_halo(): before = lax.ppermute(last, axis, up)  15 us
    ppermute x6, starting transfers between devices, with_halo(): before = lax.ppermute(last, axis, up)  11.5 us
  transfers between devices with their start and end apart: 12, of which 7 were waited for; matrix products, arithmetic and copies ran while one was open for 0% of the time, Pallas kernels for 0%

commit v1 on v0

v1 whole, which is shorter than its diff:
```python
import functools

import jax
import jax.numpy as jnp
from jax import lax
from jax.experimental import pallas as pl
from jax.experimental.pallas import tpu as pltpu
from jax.sharding import PartitionSpec as P

OMEGA = 0.8
LANES = 128
VMEM = 24 * 2**20
STORED, COUPLING, SOURCE, PARTIAL, NORTH, SOUTH, EAST, WEST, EAST_T, WEST_T = range(10)
FROM_EAST, FROM_WEST = 16, 32


def harmonic(left, right):
    return 2.0 * left * right / (left + right)


def shift(value, by, axis):
    return pltpu.roll(value, by % value.shape[axis], axis)


def rows_of(shape):
    return lax.broadcasted_iota(jnp.int32, shape, 0)


def fold(value):
    total = None
    for y in range(0, value.shape[0], 8):
        for z in range(0, value.shape[1], LANES):
            tile = value[y : y + 8, z : z + LANES]
            total = tile if total is None else total + tile
    return total


def total_of(value):
    return jnp.sum(value, axis=(0, 1), keepdims=True)


def placed(totals):
    lane = lax.broadcasted_iota(jnp.int32, (1, LANES), 1)
    row = jnp.zeros((1, LANES), jnp.float32)
    for at, total in totals:
        row = jnp.where(lane == at, total, row)
    return row


def smooth(first, work, weights):
    cx = first.shape[0]
    east, west, north, south, upper, lower = weights

    def sweep(src, dst):
        def slab(x, carry):
            s = src[x + 1]
            total = (1.0 - OMEGA) * s + first[x]
            total = total + east[x] * src[x + 2] + west[x] * src[x]
            total = total + north[x] * shift(s, -1, 0) + south[x] * shift(s, 1, 0)
            total = total + upper[x] * shift(s, -1, 1) + lower[x] * shift(s, 1, 1)
            dst[x + 1] = total
            return carry

        lax.fori_loop(0, cx, slab, 0)

    sweep(work.at[0], work.at[1])
    sweep(work.at[1], work.at[0])
    sweep(work.at[0], work.at[1])


def apply(padded, north_halo, south_halo, storage, faces, out):
    cx, cy = storage.shape[:2]
    east_t, north_t, south_t, upper_t, lower_t = faces

    def slab(x, carry):
        u = padded[x + 1]
        row = rows_of(u.shape)
        north = jnp.where(row == cy - 1, north_halo[pl.ds(x, 1)], shift(u, -1, 0))
        south = jnp.where(row == 0, south_halo[pl.ds(x, 1)], shift(u, 1, 0))
        total = storage[x] * u
        total = total + east_t[x + 1] * (u - padded[x + 2]) + east_t[x] * (u - padded[x])
        total = total + north_t[x] * (u - north) + south_t[x] * (u - south)
        total = total + upper_t[x] * (u - shift(u, -1, 1)) + lower_t[x] * (u - shift(u, 1, 1))
        out[x] = total
        return carry

    lax.fori_loop(0, cx, slab, 0)


def assemble_kernel(
    source, perm, storage, perm_east, perm_west, perm_north, perm_south,
    east_t, north_t, south_t, upper_t, lower_t, scale, w_east, w_west, w_north, w_south, w_upper, w_lower,
    result, to_east, to_west, to_north, to_south, own, first, work,
):
    cx, cy, cz = source.shape
    row = rows_of((cy, cz))
    stored = total_r = inside = jnp.zeros((8, LANES), jnp.float32)
    coupling = jnp.zeros((1, cz), jnp.float32)
    east_t[0] = harmonic(perm_west[...], perm[0])
    for x in range(cx):
        k, w, r = perm[x], storage[x], source[x]
        east = harmonic(k, perm[x + 1] if x + 1 < cx else perm_east[...])
        west = east_t[x]
        north = harmonic(k, jnp.where(row == cy - 1, perm_north[x : x + 1], shift(k, -1, 0)))
        south = jnp.where(row == 0, harmonic(perm_south[x : x + 1], k[0:1]), shift(north, 1, 0))
        upper = harmonic(k, shift(k, -1, 1))
        lower = shift(upper, 1, 1)
        diagonal = w + east + west + north + south + upper + lower
        q = OMEGA / diagonal
        east_t[x + 1] = east
        north_t[x] = north
        south_t[x] = south
        upper_t[x] = upper
        lower_t[x] = lower
        scale[x] = q
        w_east[x] = q * east
        w_west[x] = q * west
        w_north[x] = jnp.where(row == cy - 1, 0.0, q * north)
        w_south[x] = jnp.where(row == 0, 0.0, q * south)
        w_upper[x] = q * upper
        w_lower[x] = q * lower
        s = q * r
        first[x] = s
        work[0, x + 1] = s
        stored = stored + fold(w)
        total_r = total_r + fold(r)
        coupling = coupling + north[cy - 1 : cy]
    outside = jnp.zeros((cy, cz), jnp.float32)
    for at in range(2):
        work[at, 0] = outside
        work[at, cx + 1] = outside
    smooth(first, work, (w_east, w_west, w_north, w_south, w_upper, w_lower))
    flux_north = flux_south = jnp.zeros((1, cz), jnp.float32)
    for x in range(cx):
        s = work[1, x + 1]
        result[x] = s
        inside = inside + fold(storage[x] * s)
        top, bottom = s[cy - 1 : cy], s[0:1]
        to_north[x : x + 1] = top
        to_south[x : x + 1] = bottom
        flux_north = flux_north + north_t[x, cy - 1 : cy] * top
        flux_south = flux_south + south_t[x, 0:1] * bottom
    flux_east = total_of(fold(east_t[cx] * work[1, cx]))
    flux_west = total_of(fold(east_t[0] * work[1, 1]))
    flux_north = total_of(flux_north)
    flux_south = total_of(flux_south)
    totals = (
        (STORED, total_of(stored)),
        (COUPLING, total_of(coupling)),
        (SOURCE, total_of(total_r)),
        (PARTIAL, total_of(inside) + flux_east + flux_west + flux_north + flux_south),
        (NORTH, flux_north),
        (SOUTH, flux_south),
        (EAST, flux_east),
        (WEST, flux_west),
        (EAST_T, total_of(fold(east_t[cx]))),
        (WEST_T, total_of(fold(east_t[0]))),
    )
    scalars = placed(totals)
    own[...] = scalars
    tail = rows_of((8, cz)) == 0
    for out, layer, at in ((to_east, cx, FROM_WEST), (to_west, 1, FROM_EAST)):
        out[0:cy] = work[1, layer]
        moved = pltpu.roll(scalars, at, 1)
        moved = jnp.concatenate([moved] + [jnp.zeros_like(moved)] * (cz // LANES - 1), axis=1)
        out[cy : cy + 8] = jnp.where(tail, moved, 0.0)


def reduce_rows(margin, coupling, steps):
    before, after = shift(coupling, 1, 0), coupling
    factors = []
    for step in range(steps):
        h = 2**step
        inverse = 1.0 / (margin + before + after)
        from_before = before * shift(inverse, h, 0)
        from_after = after * shift(inverse, -h, 0)
        margin = margin + from_before * shift(margin, h, 0) + from_after * shift(margin, -h, 0)
        before, after = from_before * shift(before, h, 0), from_after * shift(after, -h, 0)
        factors.append((from_before, from_after))
    return factors, 1.0 / margin


def solve_rows(factors, last, right):
    for step, (from_before, from_after) in enumerate(factors):
        h = 2**step
        right = right + from_before * shift(right, h, 0) + from_after * shift(right, -h, 0)
    return right * last


def first_kernel(
    steps, axis, table, halo_east, halo_west, halo_north, halo_south, source, storage,
    east_t, north_t, south_t, upper_t, lower_t, scale, w_east, w_west, w_north, w_south, w_upper, w_lower, result,
    u0_ref, u1_ref, to_east, to_west, to_north, to_south, dots, solver, padded, image, first, work, edges,
):
    cx, cy, cz = source.shape
    members = table.shape[0]
    me = lax.axis_index(axis)
    t = table[...]

    def column(at):
        return shift(t, -at, 1)

    factors, last = reduce_rows(column(STORED) / members, column(COUPLING) * members, steps)
    for step, pair in enumerate(factors):
        solver[2 * step] = pair[0]
        solver[2 * step + 1] = pair[1]
    solver[2 * steps] = last
    c0 = solve_rows(factors, last, column(SOURCE))
    c_east, c_west = shift(c0, -FROM_EAST, 1), shift(c0, -FROM_WEST, 1)
    c_north, c_south = shift(c0, -1, 0), shift(c0, 1, 0)
    after = column(COUPLING)
    sums = (
        column(PARTIAL) - shift(column(SOUTH), -1, 0) - shift(column(NORTH), 1, 0)
        - column(FROM_EAST + WEST) - column(FROM_WEST + EAST)
        + column(STORED) * c0 + after * (c0 - c_north) + shift(after, 1, 0) * (c0 - c_south)
        + column(EAST_T) * (c0 - c_east) + column(WEST_T) * (c0 - c_west)
    )
    c1 = solve_rows(factors, last, sums)
    mine = (rows_of(t.shape) == me) & (lax.broadcasted_iota(jnp.int32, t.shape, 1) == 0)

    def pick(value):
        return total_of(jnp.where(mine, value, 0.0))

    here, east, west, north, south, c1 = (pick(c) for c in (c0, c_east, c_west, c_north, c_south, c1))

    padded[0] = halo_west[0:cy] + west
    padded[cx + 1] = halo_east[0:cy] + east
    edges[0] = halo_north[...] + north
    edges[1] = halo_south[...] + south
    for x in range(cx):
        u = result[x] + here
        padded[x + 1] = u
        u0_ref[x] = u
    apply(padded, edges.at[0], edges.at[1], storage, (east_t, north_t, south_t, upper_t, lower_t), image)
    outside = jnp.zeros((cy, cz), jnp.float32)
    for at in range(2):
        work[at, 0] = outside
        work[at, cx + 1] = outside
    for x in range(cx):
        s = scale[x] * image[x]
        first[x] = s
        work[0, x + 1] = s
    smooth(first, work, (w_east, w_west, w_north, w_south, w_upper, w_lower))
    r_u0 = u0_v0 = v0_u1 = r_u1 = jnp.zeros((8, LANES), jnp.float32)
    for x in range(cx):
        u0, v0, r = padded[x + 1], image[x], source[x]
        u1 = work[1, x + 1] + c1
        u1_ref[x] = u1
        to_north[x : x + 1] = u1[cy - 1 : cy]
        to_south[x : x + 1] = u1[0:1]
        r_u0 = r_u0 + fold(r * u0)
        u0_v0 = u0_v0 + fold(u0 * v0)
        v0_u1 = v0_u1 + fold(v0 * u1)
        r_u1 = r_u1 + fold(r * u1)
    to_east[...] = u1_ref[cx - 1]
    to_west[...] = u1_ref[0]
    dots[...] = placed(((1, total_of(r_u0)), (2, total_of(u0_v0)), (3, total_of(v0_u1)), (4, total_of(r_u1))))


def second_kernel(
    halo_east, halo_west, halo_north, halo_south, u0_ref, u1_ref, dots, storage,
    east_t, north_t, south_t, upper_t, lower_t, scale, w_east, w_west, w_north, w_south, w_upper, w_lower,
    result, out, padded, image, first, work,
):
    cx, cy, cz = storage.shape
    padded[0] = halo_west[...]
    padded[cx + 1] = halo_east[...]
    for x in range(cx):
        padded[x + 1] = u1_ref[x]
    apply(padded, halo_north, halo_south, storage, (east_t, north_t, south_t, upper_t, lower_t), image)
    outside = jnp.zeros((cy, cz), jnp.float32)
    for at in range(2):
        work[at, 0] = outside
        work[at, cx + 1] = outside
    total = u1_v1 = u0_v1 = jnp.zeros((8, LANES), jnp.float32)
    for x in range(cx):
        v1 = image[x]
        s = scale[x] * v1
        first[x] = s
        work[0, x + 1] = s
        total = total + fold(v1)
        u1_v1 = u1_v1 + fold(u1_ref[x] * v1)
        u0_v1 = u0_v1 + fold(u0_ref[x] * v1)
    smooth(first, work, (w_east, w_west, w_north, w_south, w_upper, w_lower))
    for x in range(cx):
        result[x] = work[1, x + 1]
    out[...] = dots[...] + placed(((0, total_of(total)), (5, total_of(u1_v1)), (6, total_of(u0_v1))))


def last_kernel(steps, axis, table, solver, u0_ref, u1_ref, result, pressure, precond):
    t = table[...]
    me = lax.axis_index(axis)
    lane = lax.broadcasted_iota(jnp.int32, t.shape, 1)
    factors = [(solver[2 * step], solver[2 * step + 1]) for step in range(steps)]
    c2 = solve_rows(factors, solver[2 * steps], t)
    c2 = total_of(jnp.where((rows_of(t.shape) == me) & (lane == 0), c2, 0.0))
    sums = jnp.sum(t, axis=0, keepdims=True)
    r_u0, u0_v0, v0_u1, r_u1, u1_v1, u0_v1 = (sums[:, at : at + 1] for at in range(1, 7))
    a0 = r_u0 / u0_v0
    rz = r_u0 - a0 * r_u1 - a0 * u0_v0 + a0 * a0 * v0_u1
    keep = 1.0 + rz / r_u0
    a1 = rz / (keep * keep * u0_v0 - keep * a0 * (u0_v1 + v0_u1) + a0 * a0 * u1_v1)
    p0 = a0 + a1 * keep
    p1 = a1 * a0
    z1 = a0 + a1 * keep
    z2 = a1 * a0
    for x in range(u0_ref.shape[0]):
        u0, u1 = u0_ref[x], u1_ref[x]
        pressure[x] = p0 * u0 - p1 * u1
        precond[x] = u0 - z1 * u1 + z2 * (result[x] + c2)


def call(body, outs, scratch, *operands):
    space = pl.BlockSpec(memory_space=pltpu.VMEM)
    return pl.pallas_call(
        body,
        out_shape=[jax.ShapeDtypeStruct(s, jnp.float32) for s in outs],
        in_specs=[space] * len(operands),
        out_specs=[space] * len(outs),
        scratch_shapes=[pltpu.VMEM(s, jnp.float32) for s in scratch],
        compiler_params=pltpu.CompilerParams(vmem_limit_bytes=VMEM),
    )(*operands)


def exchange(to_east, to_west, to_north, to_south):
    def ring(axis):
        peers = lax.axis_size(axis)
        up = [(i, (i + 1) % peers) for i in range(peers)]
        return up, [(j, i) for i, j in up]

    up, down = ring("group")
    west = lax.ppermute(to_east, "group", up)
    east = lax.ppermute(to_west, "group", down)
    up, down = ring("sub")
    south = lax.ppermute(to_north, "sub", up)
    north = lax.ppermute(to_south, "sub", down)
    return east, west, north, south


def gather(row, axis):
    peers = lax.axis_size(axis)
    return lax.all_to_all(jnp.broadcast_to(row[None], (peers, 1, LANES)), axis, 0, 0).reshape(peers, LANES)


def shards(source, perm, storage):
    cx, cy, cz = source.shape
    members = lax.axis_size("sub")
    steps = members.bit_length() - 1
    full, wide, tall, layer, edge = (cx, cy, cz), (cx + 2, cy, cz), (cy + 8, cz), (cy, cz), (cx, cz)
    halos = exchange(perm[-1], perm[0], perm[:, -1], perm[:, 0])
    *shared, result, to_east, to_west, to_north, to_south, own = call(
        assemble_kernel,
        [(cx + 1, cy, cz)] + [full] * 12 + [tall, tall, edge, edge, (1, LANES)],
        [full, (2,) + wide],
        source, perm, storage, *halos,
    )
    halos = exchange(to_east, to_west, to_north, to_south)
    table = gather(own + halos[0][cy : cy + 1, :LANES] + halos[1][cy : cy + 1, :LANES], "sub")
    u0, u1, to_east, to_west, to_north, to_south, dots, solver = call(
        functools.partial(first_kernel, steps, "sub"),
        [full, full, layer, layer, edge, edge, (1, LANES), (2 * steps + 1, members, LANES)],
        [wide, full, full, (2,) + wide, (2,) + edge],
        table, *halos, source, storage, *shared, result,
    )
    halos = exchange(to_east, to_west, to_north, to_south)
    result, row = call(
        second_kernel,
        [full, (1, LANES)],
        [wide, full, full, (2,) + wide],
        *halos, u0, u1, dots, storage, *shared,
    )
    over_groups = jnp.sum(gather(row, "group"), axis=0, keepdims=True)
    row = jnp.where(jnp.arange(LANES)[None] == 0, row, over_groups)
    return tuple(
        call(functools.partial(last_kernel, steps, "sub"), [full, full], [], gather(row, "sub"), solver, u0, u1, result)
    )


def solution(mesh):
    spec = P("group", "sub", None)
    return jax.shard_map(shards, mesh=mesh, in_specs=(spec,) * 3, out_specs=(spec,) * 2, check_vma=False)
```

time: 549 us -> 119 us (0.22)
  blocking collectives: 441 us -> 29.2 us
  other arithmetic: 25 us -> 0.03 us
  Pallas kernels: 0 us -> 10.9 us
  between operations: 7.46 us -> 0.81 us
  starting transfers between devices: 36.3 us -> 42.1 us
    psum x3 -> x0, blocking collectives: 301 us -> none  [the longest x2 202 us: precondition(): lax.psum(jnp.sum(resid * result), ('group', 'sub'))]
    unnamed x3 -> x0, blocking collectives: 140 us -> none
    all_to_all x0 -> x2, blocking collectives: none -> 29.2 us  [gather(): lax.all_to_all(jnp.broadcast_to(row[None], (peers, 1, LANES)), axis, 0, 0)]
    all_to_all x0 -> x1, starting transfers between devices: none -> 12 us  [gather(): lax.all_to_all(jnp.broadcast_to(row[None], (peers, 1, LANES)), axis, 0, 0)]
    pallas_call x0 -> x4, Pallas kernels: none -> 10.9 us  [call(): pl.pallas_call(body, out_shape=[jax.ShapeDtypeStruct(s, jnp.float32) for...]
    slice x48 -> x1, local copies, waits for them, and re-layouts: 10.7 us -> 0.89 us  [shards(): halos = exchange(perm[-1], perm[0], perm[:, -1], perm[:, 0])]
    add x10 -> x0, other arithmetic: 9.62 us -> none  [the longest x2 4.89 us: precondition(): result = smooth + jnp.sum(selector * coarse)]
    all_to_all x0 -> x1, waiting for transfers between devices: none -> 7.75 us  [gather(): lax.all_to_all(jnp.broadcast_to(row[None], (peers, 1, LANES)), axis, 0, 0)]
  transfers between devices with their start and end apart: 12 -> 13, of which waited for: 7 -> 8; matrix products, arithmetic and copies ran while one was open for 0% -> 1% of each run, Pallas kernels for 0% -> 0%
where the time goes in v1:
time: 119 us
  starting transfers between devices  42.1 us (35%)
  blocking collectives  29.2 us (25%)
  waiting for transfers between devices  22.8 us (19%)
  local copies, waits for them, and re-layouts  12.8 us (11%)
  Pallas kernels  10.9 us (9%)
    all_to_all x2, blocking collectives, gather(): lax.all_to_all(jnp.broadcast_to(row[None], (peers, 1, LANES)), axis, 0, 0)  29.2 us
    all_to_all x1, starting transfers between devices, gather(): lax.all_to_all(jnp.broadcast_to(row[None], (peers, 1, LANES)), axis, 0, 0)  12 us
    pallas_call x4, Pallas kernels, call(): pl.pallas_call(body, out_shape=[jax.ShapeDtypeStruct(s, jnp.float32) for...  10.9 us
    ppermute x3, starting transfers between devices, exchange(): east = lax.ppermute(to_west, 'group', down)  10.8 us
    unnamed x34, local copies, waits for them, and re-layouts  10.5 us
    ppermute x3, starting transfers between devices, exchange(): west = lax.ppermute(to_east, 'group', up)  9.3 us
    ppermute x3, starting transfers between devices, exchange(): north = lax.ppermute(to_south, 'sub', down)  8.2 us
    all_to_all x1, waiting for transfers between devices, gather(): lax.all_to_all(jnp.broadcast_to(row[None], (peers, 1, LANES)), axis, 0, 0)  7.75 us
  transfers between devices with their start and end apart: 13, of which 8 were waited for; matrix products, arithmetic and copies ran while one was open for 1% of the time, Pallas kernels for 0%

profile of v1, /device:TPU:1, one launch (start us, length us, event | category | flops | bytes accessed | tf_op | source)
XLA Modules:
  0.0 118.7 jit_solution(5096890809390877394)
XLA Ops:
  1.4 4.0 %collective-permute-start.1 = (f32[32,256]{1,0:T(8,128)S(1)}, f32[32,256]{1,0:T(8,128)S(1)}, u32[]{:S(2)}, u32[]{:S(2)}) collective-permute-start(f32[32,256]{1,0:T(8,128)S(1)} %get-tuple-element.60), channel_id=1, source_target_pairs={{0,32},{32,64},{64,96},{96,128},{128,160},{160,192},{192,224},{224... | collective-permute-start | bytes 98312 | tf_op jit(solution)/shard_map/ppermute | solution.py:332
  5.4 5.6 %collective-permute-start = (f32[32,256]{1,0:T(8,128)S(1)}, f32[32,256]{1,0:T(8,128)S(1)}, u32[]{:S(2)}, u32[]{:S(2)}) collective-permute-start(f32[32,256]{1,0:T(8,128)S(1)} %get-tuple-element.61), channel_id=1, source_target_pairs={{32,0},{64,32},{96,64},{128,96},{160,128},{192,160},{224,192},{256... | collective-permute-start | bytes 98312 | tf_op jit(solution)/shard_map/ppermute | solution.py:333
  11.0 0.9 fusion.2
  11.9 6.5 %collective-permute-start.2 = (f32[8,256]{1,0:T(8,128)S(1)}, f32[8,256]{1,0:T(8,128)S(1)}, u32[]{:S(2)}, u32[]{:S(2)}) collective-permute-start(f32[8,256]{1,0:T(8,128)S(1)} %bitcast.24), channel_id=1, source_target_pairs={{1,0},{2,1},{3,2},{4,3},{5,4},{6,5},{7,6},{8,7},{9,8},{10,9},{11,1... | collective-permute-start | bytes 24584 | tf_op jit(solution)/shard_map/ppermute | solution.py:336
  19.2 3.0 %collective-permute-done.3.perm_south = f32[8,256]{1,0:T(8,128)S(1)} collective-permute-done((f32[8,256]{1,0:T(8,128)S(1)}, f32[8,256]{1,0:T(8,128)S(1)}, u32[]{:S(2)}, u32[]{:S(2)}) %collective-permute-start.3) | collective-permute-done | bytes 8224 | tf_op jit(solution)/shard_map/ppermute | solution.py:335
  22.2 0.9 copy-done
  23.2 0.9 copy-done.2
  24.1 0.9 copy-done.8
  25.1 3.3 %shard_map.50 = (f32[9,32,256]{2,1,0:T(8,128)S(1)}, f32[8,32,256]{2,1,0:T(8,128)S(1)}, f32[8,32,256]{2,1,0:T(8,128)S(1)}, f32[8,32,256]{2,1,0:T(8,128)S(1)}, f32...) custom-call(f32[8,32,256]{2,1,0:T(8,128)S(1)} %copy-done.2, ...), custom_call_target="tpu_custom_call" | custom-call | tf_op jit(solution)/shard_map/pallas_call | solution.py:315
  29.7 3.4 %collective-permute-start.4 = (f32[40,256]{1,0:T(8,128)S(1)}, f32[40,256]{1,0:T(8,128)S(1)}, u32[]{:S(2)}, u32[]{:S(2)}) collective-permute-start(f32[40,256]{1,0:T(8,128)S(1)} %get-tuple-element.31), channel_id=1, source_target_pairs={{32,0},{64,32},{96,64},{128,96},{160,128},{192,160},{224,192},{256... | collective-permute-start | bytes 122888 | tf_op jit(solution)/shard_map/ppermute | solution.py:333
  33.0 1.9 %collective-permute-start.5 = (f32[40,256]{1,0:T(8,128)S(1)}, f32[40,256]{1,0:T(8,128)S(1)}, u32[]{:S(2)}, u32[]{:S(2)}) collective-permute-start(f32[40,256]{1,0:T(8,128)S(1)} %get-tuple-element.32), channel_id=1, source_target_pairs={{0,32},{32,64},{64,96},{96,128},{128,160},{160,192},{192,224},{224... | collective-permute-start | bytes 122888 | tf_op jit(solution)/shard_map/ppermute | solution.py:332
  35.0 6.1 %collective-permute-done.5.halo_west = f32[40,256]{1,0:T(8,128)S(1)} collective-permute-done((f32[40,256]{1,0:T(8,128)S(1)}, f32[40,256]{1,0:T(8,128)S(1)}, u32[]{:S(2)}, u32[]{:S(2)}) %collective-permute-start.5) | collective-permute-done | bytes 40992 | tf_op jit(solution)/shard_map/ppermute | solution.py:332
  41.7 12.0 %all-to-all-start = ((f32[32,1,128]{2,1,0:T(1,128)}), f32[32,1,128]{2,1,0:T(1,128)S(1)}, u32[]{:S(2)}, u32[]{:S(2)}) async-start(f32[32,1,128]{2,1,0:T(1,128)} %broadcast_in_dim.29), calls=%async_computation | async-start | bytes 32768 | tf_op jit(solution)/shard_map/all_to_all | solution.py:342
  54.0 1.5 %collective-permute-start.7 = (f32[8,256]{1,0:T(8,128)}, f32[8,256]{1,0:T(8,128)S(1)}, u32[]{:S(2)}, u32[]{:S(2)}) collective-permute-start(f32[8,256]{1,0:T(8,128)} %copy-done.15), channel_id=1, source_target_pairs={{0,1},{1,2},{2,3},{3,4},{4,5},{5,6},{6,7},{7,8},{8,9},{9,10},{10,1... | collective-permute-start | bytes 24584 | tf_op jit(solution)/shard_map/ppermute | solution.py:335
  55.5 1.8 %collective-permute-done.6.halo_north = f32[8,256]{1,0:T(8,128)S(1)} collective-permute-done((f32[8,256]{1,0:T(8,128)}, f32[8,256]{1,0:T(8,128)S(1)}, u32[]{:S(2)}, u32[]{:S(2)}) %collective-permute-start.6) | collective-permute-done | bytes 8224 | tf_op jit(solution)/shard_map/ppermute | solution.py:336
  57.7 7.8 %all-to-all-done = f32[32,1,128]{2,1,0:T(1,128)S(1)} async-done(((f32[32,1,128]{2,1,0:T(1,128)}), f32[32,1,128]{2,1,0:T(1,128)S(1)}, u32[]{:S(2)}, u32[]{:S(2)}) %all-to-all-start) | async-done | bytes 16416 | tf_op jit(solution)/shard_map/all_to_all | solution.py:342
  65.5 0.9 copy-done.3
  66.4 0.9 copy-done.10
  67.4 3.5 %shard_map.51 = (f32[8,32,256]{2,1,0:T(8,128)S(1)}, f32[8,32,256]{2,1,0:T(8,128)S(1)}, f32[32,256]{1,0:T(8,128)S(1)}, f32[32,256]{1,0:T(8,128)S(1)}, f32[8,256]{...) custom-call(f32[32,128]{1,0:T(8,128)S(1)} %bitcast.20, ...), custom_call_target="tpu_custom_call" | custom-call | tf_op jit(solution)/shard_map/pallas_call | solution.py:315
  70.9 1.9 %collective-permute-start.8 = (f32[32,256]{1,0:T(8,128)S(1)}, f32[32,256]{1,0:T(8,128)S(1)}, u32[]{:S(2)}, u32[]{:S(2)}) collective-permute-start(f32[32,256]{1,0:T(8,128)S(1)} %get-tuple-element.48), channel_id=1, source_target_pairs={{32,0},{64,32},{96,64},{128,96},{160,128},{192,160},{224,192},{256... | collective-permute-start | bytes 98312 | tf_op jit(solution)/shard_map/ppermute | solution.py:333
  72.8 3.4 %collective-permute-start.9 = (f32[32,256]{1,0:T(8,128)S(1)}, f32[32,256]{1,0:T(8,128)S(1)}, u32[]{:S(2)}, u32[]{:S(2)}) collective-permute-start(f32[32,256]{1,0:T(8,128)S(1)} %get-tuple-element.49), channel_id=1, source_target_pairs={{0,32},{32,64},{64,96},{96,128},{128,160},{160,192},{192,224},{224... | collective-permute-start | bytes 98312 | tf_op jit(solution)/shard_map/ppermute | solution.py:332
  76.2 1.5 %collective-permute-start.10 = (f32[8,256]{1,0:T(8,128)S(1)}, f32[8,256]{1,0:T(8,128)S(1)}, u32[]{:S(2)}, u32[]{:S(2)}) collective-permute-start(f32[8,256]{1,0:T(8,128)S(1)} %get-tuple-element.50), channel_id=1, source_target_pairs={{1,0},{2,1},{3,2},{4,3},{5,4},{6,5},{7,6},{8,7},{9,8},{10,9},{11,1... | collective-permute-start | bytes 24584 | tf_op jit(solution)/shard_map/ppermute | solution.py:336
  78.0 1.3 %collective-permute-done.10.halo_north = f32[8,256]{1,0:T(8,128)S(1)} collective-permute-done((f32[8,256]{1,0:T(8,128)S(1)}, f32[8,256]{1,0:T(8,128)S(1)}, u32[]{:S(2)}, u32[]{:S(2)}) %collective-permute-start.10) | collective-permute-done | bytes 8224 | tf_op jit(solution)/shard_map/ppermute | solution.py:336
  79.3 1.5 %collective-permute-done.9.halo_west = f32[32,256]{1,0:T(8,128)S(1)} collective-permute-done((f32[32,256]{1,0:T(8,128)S(1)}, f32[32,256]{1,0:T(8,128)S(1)}, u32[]{:S(2)}, u32[]{:S(2)}) %collective-permute-start.9) | collective-permute-done | bytes 32800 | tf_op jit(solution)/shard_map/ppermute | solution.py:332
  80.8 3.0 %shard_map.52 = (f32[8,32,256]{2,1,0:T(8,128)S(1)}, f32[1,128]{1,0:T(1,128)S(1)}) custom-call(f32[32,256]{1,0:T(8,128)S(1)} %collective-permute-done.8.halo_east, f32[32,256]{1,0:T(8,128)S(1)} %collective-permute-done.9.halo_west, f32[8,256]{1,0:T(8,128)S(1)} %collective-permute-done.10.halo_north, f32[8,256]{1,0:T(8,128)S(1)} %collective-permute-done.11.halo_south, ...), custom_call_target="tpu_custom_call" | custom-call | tf_op jit(solution)/shard_map/pallas_call | solution.py:315
  84.6 9.4 %all_to_all.15 = f32[16,1,128]{2,1,0:T(1,128)S(1)} all-to-all(f32[16,1,128]{2,1,0:T(1,128)S(1)} %broadcast_in_dim.31), channel_id=1, replica_groups=mesh['group'=16,'sub'=32] {'group'}, dimensions={0} | all-to-all | bytes 16384 | tf_op jit(solution)/shard_map/all_to_all | solution.py:342
  94.0 19.8 %all_to_all.16 = f32[32,1,128]{2,1,0:T(1,128)S(1)} all-to-all(f32[32,1,128]{2,1,0:T(1,128)S(1)} %broadcast_in_dim.34), channel_id=1, replica_groups=mesh['group'=16,'sub'=32] {'sub'}, dimensions={0} | all-to-all | bytes 32768 | tf_op jit(solution)/shard_map/all_to_all | solution.py:342
  113.8 0.9 copy-done.5
  114.8 0.9 copy-done.7
  115.7 0.9 copy-done.12
  116.7 0.9 copy-done.14
  117.6 1.1 shard_map.53
  (42 shorter events, 5.2 us)
Async XLA Ops:
  1.4 20.8 %collective-permute-start.1 = (f32[32,256]{1,0:T(8,128)S(1)}, f32[32,256]{1,0:T(8,128)S(1)}, u32[]{:S(2)}, u32[]{:S(2)}) collective-permute-start(f32[32,256]{1,0:T(8,128)S(1)} %get-tuple-element.60), channel_id=1, source_target_pairs={{0,32},{32,64},{64,96},{96,128},{128,160},{160,192},{192,224},{224... | collective-permute-start | bytes 98312 | tf_op jit(solution)/shard_map/ppermute | solution.py:332
  5.4 16.8 %collective-permute-start = (f32[32,256]{1,0:T(8,128)S(1)}, f32[32,256]{1,0:T(8,128)S(1)}, u32[]{:S(2)}, u32[]{:S(2)}) collective-permute-start(f32[32,256]{1,0:T(8,128)S(1)} %get-tuple-element.61), channel_id=1, source_target_pairs={{32,0},{64,32},{96,64},{128,96},{160,128},{192,160},{224,192},{256... | collective-permute-start | bytes 98312 | tf_op jit(solution)/shard_map/ppermute | solution.py:333
  11.9 7.3 %collective-permute-start.2 = (f32[8,256]{1,0:T(8,128)S(1)}, f32[8,256]{1,0:T(8,128)S(1)}, u32[]{:S(2)}, u32[]{:S(2)}) collective-permute-start(f32[8,256]{1,0:T(8,128)S(1)} %bitcast.24), channel_id=1, source_target_pairs={{1,0},{2,1},{3,2},{4,3},{5,4},{6,5},{7,6},{8,7},{9,8},{10,9},{11,1... | collective-permute-start | bytes 24584 | tf_op jit(solution)/shard_map/ppermute | solution.py:336
  18.4 3.8 %collective-permute-start.3 = (f32[8,256]{1,0:T(8,128)S(1)}, f32[8,256]{1,0:T(8,128)S(1)}, u32[]{:S(2)}, u32[]{:S(2)}) collective-permute-start(f32[8,256]{1,0:T(8,128)S(1)} %bitcast.25), channel_id=1, source_target_pairs={{0,1},{1,2},{2,3},{3,4},{4,5},{5,6},{6,7},{7,8},{8,9},{9,10},{10,1... | collective-permute-start | bytes 24584 | tf_op jit(solution)/shard_map/ppermute | solution.py:335
  22.2 1.0 copy-start
  23.2 0.9 copy-start.2
  24.1 0.9 copy-start.8
  25.1 40.4 %copy-start.1 = (f32[8,32,256]{2,1,0:T(8,128)S(1)}, f32[8,32,256]{2,1,0:T(8,128)}, u32[]{:S(2)}) copy-start(f32[8,32,256]{2,1,0:T(8,128)} %storage.5) | copy-start | bytes 786436
  28.4 0.7 copy-start.9
  29.1 0.6 copy-start.15
  29.7 5.3 %collective-permute-start.4 = (f32[40,256]{1,0:T(8,128)S(1)}, f32[40,256]{1,0:T(8,128)S(1)}, u32[]{:S(2)}, u32[]{:S(2)}) collective-permute-start(f32[40,256]{1,0:T(8,128)S(1)} %get-tuple-element.31), channel_id=1, source_target_pairs={{32,0},{64,32},{96,64},{128,96},{160,128},{192,160},{224,192},{256... | collective-permute-start | bytes 122888 | tf_op jit(solution)/shard_map/ppermute | solution.py:333
  33.0 8.1 %collective-permute-start.5 = (f32[40,256]{1,0:T(8,128)S(1)}, f32[40,256]{1,0:T(8,128)S(1)}, u32[]{:S(2)}, u32[]{:S(2)}) collective-permute-start(f32[40,256]{1,0:T(8,128)S(1)} %get-tuple-element.32), channel_id=1, source_target_pairs={{0,32},{32,64},{64,96},{96,128},{128,160},{160,192},{192,224},{224... | collective-permute-start | bytes 122888 | tf_op jit(solution)/shard_map/ppermute | solution.py:332
  41.7 23.8 %all-to-all-start = ((f32[32,1,128]{2,1,0:T(1,128)}), f32[32,1,128]{2,1,0:T(1,128)S(1)}, u32[]{:S(2)}, u32[]{:S(2)}) async-start(f32[32,1,128]{2,1,0:T(1,128)} %broadcast_in_dim.29), calls=%async_computation | async-start | bytes 32768 | tf_op jit(solution)/shard_map/all_to_all | solution.py:342
  53.8 3.6 %collective-permute-start.6 = (f32[8,256]{1,0:T(8,128)}, f32[8,256]{1,0:T(8,128)S(1)}, u32[]{:S(2)}, u32[]{:S(2)}) collective-permute-start(f32[8,256]{1,0:T(8,128)} %get-tuple-element.33), channel_id=1, source_target_pairs={{1,0},{2,1},{3,2},{4,3},{5,4},{6,5},{7,6},{8,7},{9,8},{10,9},{11,1... | collective-permute-start | bytes 24584 | tf_op jit(solution)/shard_map/ppermute | solution.py:336
  54.0 3.7 %collective-permute-start.7 = (f32[8,256]{1,0:T(8,128)}, f32[8,256]{1,0:T(8,128)S(1)}, u32[]{:S(2)}, u32[]{:S(2)}) collective-permute-start(f32[8,256]{1,0:T(8,128)} %copy-done.15), channel_id=1, source_target_pairs={{0,1},{1,2},{2,3},{3,4},{4,5},{5,6},{6,7},{7,8},{8,9},{9,10},{10,1... | collective-permute-start | bytes 24584 | tf_op jit(solution)/shard_map/ppermute | solution.py:335
  65.5 1.0 copy-start.3
  66.4 0.9 copy-start.10
  70.9 13.0 %copy-start.4 = (f32[8,32,256]{2,1,0:T(8,128)}, f32[8,32,256]{2,1,0:T(8,128)S(1)}, u32[]{:S(2)}) copy-start(f32[8,32,256]{2,1,0:T(8,128)S(1)} %get-tuple-element.52.u0_ref) | copy-start | bytes 786436
  70.9 13.0 %copy-start.6 = (f32[8,32,256]{2,1,0:T(8,128)}, f32[8,32,256]{2,1,0:T(8,128)S(1)}, u32[]{:S(2)}) copy-start(f32[8,32,256]{2,1,0:T(8,128)S(1)} %get-tuple-element.53.u1_ref) | copy-start | bytes 786436
  70.9 13.0 %copy-start.13 = (f32[11,32,128]{2,1,0:T(8,128)}, f32[11,32,128]{2,1,0:T(8,128)S(1)}, u32[]{:S(2)}) copy-start(f32[11,32,128]{2,1,0:T(8,128)S(1)} %get-tuple-element.56.solver) | copy-start | bytes 540676
  70.9 8.4 %collective-permute-start.8 = (f32[32,256]{1,0:T(8,128)S(1)}, f32[32,256]{1,0:T(8,128)S(1)}, u32[]{:S(2)}, u32[]{:S(2)}) collective-permute-start(f32[32,256]{1,0:T(8,128)S(1)} %get-tuple-element.48), channel_id=1, source_target_pairs={{32,0},{64,32},{96,64},{128,96},{160,128},{192,160},{224,192},{256... | collective-permute-start | bytes 98312 | tf_op jit(solution)/shard_map/ppermute | solution.py:333
  72.8 8.0 %collective-permute-start.9 = (f32[32,256]{1,0:T(8,128)S(1)}, f32[32,256]{1,0:T(8,128)S(1)}, u32[]{:S(2)}, u32[]{:S(2)}) collective-permute-start(f32[32,256]{1,0:T(8,128)S(1)} %get-tuple-element.49), channel_id=1, source_target_pairs={{0,32},{32,64},{64,96},{96,128},{128,160},{160,192},{192,224},{224... | collective-permute-start | bytes 98312 | tf_op jit(solution)/shard_map/ppermute | solution.py:332
  76.2 3.1 %collective-permute-start.10 = (f32[8,256]{1,0:T(8,128)S(1)}, f32[8,256]{1,0:T(8,128)S(1)}, u32[]{:S(2)}, u32[]{:S(2)}) collective-permute-start(f32[8,256]{1,0:T(8,128)S(1)} %get-tuple-element.50), channel_id=1, source_target_pairs={{1,0},{2,1},{3,2},{4,3},{5,4},{6,5},{7,6},{8,7},{9,8},{10,9},{11,1... | collective-permute-start | bytes 24584 | tf_op jit(solution)/shard_map/ppermute | solution.py:336
  77.7 1.6 %collective-permute-start.11 = (f32[8,256]{1,0:T(8,128)S(1)}, f32[8,256]{1,0:T(8,128)S(1)}, u32[]{:S(2)}, u32[]{:S(2)}) collective-permute-start(f32[8,256]{1,0:T(8,128)S(1)} %get-tuple-element.51), channel_id=1, source_target_pairs={{0,1},{1,2},{2,3},{3,4},{4,5},{5,6},{6,7},{7,8},{8,9},{9,10},{10,1... | collective-permute-start | bytes 24584 | tf_op jit(solution)/shard_map/ppermute | solution.py:335
  83.9 0.7 copy-start.11
  113.8 1.0 copy-start.5
  114.8 0.9 copy-start.7
  115.7 0.9 copy-start.12
  116.7 0.9 copy-start.14

commit v2 on v1

v2 whole, which is shorter than its diff:
```python
import functools

import jax
import jax.numpy as jnp
from jax import lax
from jax.experimental import pallas as pl
from jax.experimental.pallas import tpu as pltpu
from jax.sharding import PartitionSpec as P

OMEGA = 0.8
LANES = 128
VMEM = 16 * 2**20
UNROLL = 1
STORED, COUPLING, SOURCE, PARTIAL, NORTH, SOUTH, EAST, WEST, EAST_T, WEST_T = range(10)
FROM_EAST, FROM_WEST = 16, 32


def harmonic(left, right):
    return 2.0 * left * right / (left + right)


def shift(value, by, axis):
    return pltpu.roll(value, by % value.shape[axis], axis)


def rows_of(shape):
    return lax.broadcasted_iota(jnp.int32, shape, 0)


def fold(value):
    total = None
    for y in range(0, value.shape[0], 8):
        for z in range(0, value.shape[1], LANES):
            tile = value[y : y + 8, z : z + LANES]
            total = tile if total is None else total + tile
    return total


def total_of(value):
    return jnp.sum(value, axis=(0, 1), keepdims=True)


def placed(totals):
    lane = lax.broadcasted_iota(jnp.int32, (1, LANES), 1)
    row = jnp.zeros((1, LANES), jnp.float32)
    for at, total in totals:
        row = jnp.where(lane == at, total, row)
    return row


def smooth(first, work, weights):
    cx = first.shape[0]
    east, west, north, south, upper, lower = weights

    def sweep(src, dst):
        def slab(x, carry):
            s = src[x + 1]
            total = (1.0 - OMEGA) * s + first[x]
            total = total + east[x] * src[x + 2] + west[x] * src[x]
            total = total + north[x] * shift(s, -1, 0) + south[x] * shift(s, 1, 0)
            total = total + upper[x] * shift(s, -1, 1) + lower[x] * shift(s, 1, 1)
            dst[x + 1] = total
            return carry

        lax.fori_loop(0, cx, slab, 0, unroll=UNROLL)

    sweep(work.at[0], work.at[1])
    sweep(work.at[1], work.at[0])
    sweep(work.at[0], work.at[1])


def clear_ends(work):
    for at in range(2):
        for end in (0, work.shape[1] - 1):
            work[at, end] = jnp.zeros(work.shape[2:], jnp.float32)


def apply(padded, north_halo, south_halo, storage, inner, edges, out):
    cx, cy = storage.shape[:2]
    east_t, north_t, south_t, upper_t, lower_t = inner
    edge_east, edge_west, edge_north, edge_south = edges

    def slab(x, carry):
        u = padded[x + 1]
        row = rows_of(u.shape)
        total = storage[x] * u
        total = total + east_t[x + 1] * (u - padded[x + 2]) + east_t[x] * (u - padded[x])
        total = total + north_t[x] * (u - shift(u, -1, 0)) + south_t[x] * (u - shift(u, 1, 0))
        total = total + upper_t[x] * (u - shift(u, -1, 1)) + lower_t[x] * (u - shift(u, 1, 1))
        one = pl.ds(x, 1)
        north = jnp.where(row == cy - 1, edge_north[one] * (u - north_halo[one]), 0.0)
        total = total + jnp.where(row == 0, edge_south[one] * (u - south_halo[one]), north)
        out[x] = total
        return carry

    lax.fori_loop(0, cx, slab, 0, unroll=UNROLL)
    out[0] = out[0] + edge_west[...] * (padded[1] - padded[0])
    out[cx - 1] = out[cx - 1] + edge_east[...] * (padded[cx] - padded[cx + 1])


def inner_kernel(perm, storage, east_t, north_t, south_t, upper_t, lower_t, diagonal):
    cx, cy, cz = perm.shape
    row = rows_of((cy, cz))
    west = jnp.zeros((cy, cz), jnp.float32)
    for x in range(cx):
        k = perm[x]
        east = harmonic(k, perm[x + 1]) if x + 1 < cx else jnp.zeros((cy, cz), jnp.float32)
        north = jnp.where(row == cy - 1, 0.0, harmonic(k, shift(k, -1, 0)))
        south = shift(north, 1, 0)
        upper = harmonic(k, shift(k, -1, 1))
        lower = shift(upper, 1, 1)
        east_t[x + 1] = east
        north_t[x] = north
        south_t[x] = south
        upper_t[x] = upper
        lower_t[x] = lower
        diagonal[x] = storage[x] + east + west + north + south + upper + lower
        west = east
    east_t[0] = jnp.zeros((cy, cz), jnp.float32)


def sums_kernel(source, storage, out):
    stored = total_r = jnp.zeros((8, LANES), jnp.float32)
    for x in range(source.shape[0]):
        stored = stored + fold(storage[x])
        total_r = total_r + fold(source[x])
    out[...] = placed(((STORED, total_of(stored)), (SOURCE, total_of(total_r))))


def assemble_kernel(
    perm_a, perm_b, perm_north, perm_south, source, perm, storage, sums,
    east_in, north_in, south_in, upper_t, lower_t, diagonal,
    edge_east, edge_west, edge_north, edge_south,
    scale, w_east, w_west, w_north, w_south, w_upper, w_lower, result, to_a, to_b, to_north, to_south, own, first, work,
):
    cx, cy, cz = source.shape
    odd = lax.axis_index("group") % 2 == 1
    row = rows_of((cy, cz))
    a, b = perm_a[...], perm_b[...]
    edge_east[...] = harmonic(perm[cx - 1], jnp.where(odd, b, a))
    edge_west[...] = harmonic(jnp.where(odd, a, b), perm[0])
    top = jnp.concatenate([perm[x, cy - 1 : cy] for x in range(cx)], axis=0)
    bottom = jnp.concatenate([perm[x, 0:1] for x in range(cx)], axis=0)
    edge_north[...] = harmonic(top, perm_north[...])
    edge_south[...] = harmonic(perm_south[...], bottom)
    for x in range(cx):
        d = diagonal[x]
        d = d + jnp.where(row == cy - 1, edge_north[x : x + 1], jnp.where(row == 0, edge_south[x : x + 1], 0.0))
        if x == 0:
            d = d + edge_west[...]
        if x == cx - 1:
            d = d + edge_east[...]
        q = OMEGA / d
        scale[x] = q
        w_east[x] = q * east_in[x + 1]
        w_west[x] = q * east_in[x]
        w_north[x] = q * north_in[x]
        w_south[x] = q * south_in[x]
        w_upper[x] = q * upper_t[x]
        w_lower[x] = q * lower_t[x]
        s = q * source[x]
        first[x] = s
        work[0, x + 1] = s
    clear_ends(work)
    smooth(first, work, (w_east, w_west, w_north, w_south, w_upper, w_lower))
    inside = jnp.zeros((8, LANES), jnp.float32)
    for x in range(cx):
        s = work[1, x + 1]
        result[x] = s
        inside = inside + fold(storage[x] * s)
        to_north[x : x + 1] = s[cy - 1 : cy]
        to_south[x : x + 1] = s[0:1]
    flux_east = total_of(fold(edge_east[...] * work[1, cx]))
    flux_west = total_of(fold(edge_west[...] * work[1, 1]))
    flux_north = total_of(edge_north[...] * to_north[...])
    flux_south = total_of(edge_south[...] * to_south[...])
    totals = (
        (COUPLING, total_of(edge_north[...])),
        (PARTIAL, total_of(inside) + flux_east + flux_west + flux_north + flux_south),
        (NORTH, flux_north),
        (SOUTH, flux_south),
        (EAST, flux_east),
        (WEST, flux_west),
        (EAST_T, total_of(fold(edge_east[...]))),
        (WEST_T, total_of(fold(edge_west[...]))),
    )
    scalars = sums[...] + placed(totals)
    own[...] = scalars
    tail = rows_of((8, cz)) == 0

    def message(layer, at):
        moved = pltpu.roll(scalars, at, 1)
        moved = jnp.concatenate([moved] + [jnp.zeros_like(moved)] * (cz // LANES - 1), axis=1)
        return layer, jnp.where(tail, moved, 0.0)

    east, west = message(work[1, cx], FROM_WEST), message(work[1, 1], FROM_EAST)
    for part, place in ((0, slice(0, cy)), (1, slice(cy, cy + 8))):
        to_a[place] = jnp.where(odd, west[part], east[part])
        to_b[place] = jnp.where(odd, east[part], west[part])


def reduce_rows(margin, coupling, steps):
    before, after = shift(coupling, 1, 0), coupling
    factors = []
    for step in range(steps):
        h = 2**step
        inverse = 1.0 / (margin + before + after)
        from_before = before * shift(inverse, h, 0)
        from_after = after * shift(inverse, -h, 0)
        margin = margin + from_before * shift(margin, h, 0) + from_after * shift(margin, -h, 0)
        before, after = from_before * shift(before, h, 0), from_after * shift(after, -h, 0)
        factors.append((from_before, from_after))
    return factors, 1.0 / margin


def solve_rows(factors, last, right):
    for step, (from_before, from_after) in enumerate(factors):
        h = 2**step
        right = right + from_before * shift(right, h, 0) + from_after * shift(right, -h, 0)
    return right * last


def first_kernel(
    steps, table, halo_a, halo_b, halo_north, halo_south, storage,
    east_t, north_t, south_t, upper_t, lower_t, edge_east, edge_west, edge_north, edge_south,
    scale, w_east, w_west, w_north, w_south, w_upper, w_lower, result,
    u0_ref, image, u1_ref, to_a, to_b, to_north, to_south, solver, padded, first, work, edges,
):
    cx, cy, cz = storage.shape
    members = table.shape[0]
    me = lax.axis_index("sub")
    odd = lax.axis_index("group") % 2 == 1
    t = table[...]

    def column(at):
        return shift(t, -at, 1)

    factors, last = reduce_rows(column(STORED) / members, column(COUPLING) * members, steps)
    for step, pair in enumerate(factors):
        solver[2 * step] = pair[0]
        solver[2 * step + 1] = pair[1]
    solver[2 * steps] = last
    c0 = solve_rows(factors, last, column(SOURCE))
    c_east, c_west = shift(c0, -FROM_EAST, 1), shift(c0, -FROM_WEST, 1)
    c_north, c_south = shift(c0, -1, 0), shift(c0, 1, 0)
    after = column(COUPLING)
    sums = (
        column(PARTIAL) - shift(column(SOUTH), -1, 0) - shift(column(NORTH), 1, 0)
        - column(FROM_EAST + WEST) - column(FROM_WEST + EAST)
        + column(STORED) * c0 + after * (c0 - c_north) + shift(after, 1, 0) * (c0 - c_south)
        + column(EAST_T) * (c0 - c_east) + column(WEST_T) * (c0 - c_west)
    )
    c1 = solve_rows(factors, last, sums)
    mine = (rows_of(t.shape) == me) & (lax.broadcasted_iota(jnp.int32, t.shape, 1) == 0)

    def pick(value):
        return total_of(jnp.where(mine, value, 0.0))

    here, east, west, north, south, c1 = (pick(c) for c in (c0, c_east, c_west, c_north, c_south, c1))

    a, b = halo_a[0:cy], halo_b[0:cy]
    padded[0] = jnp.where(odd, a, b) + west
    padded[cx + 1] = jnp.where(odd, b, a) + east
    edges[0] = halo_north[...] + north
    edges[1] = halo_south[...] + south
    for x in range(cx):
        u = result[x] + here
        padded[x + 1] = u
        u0_ref[x] = u
    inner, outer = (east_t, north_t, south_t, upper_t, lower_t), (edge_east, edge_west, edge_north, edge_south)
    apply(padded, edges.at[0], edges.at[1], storage, inner, outer, image)
    for x in range(cx):
        s = scale[x] * image[x]
        first[x] = s
        work[0, x + 1] = s
    clear_ends(work)
    smooth(first, work, (w_east, w_west, w_north, w_south, w_upper, w_lower))
    for x in range(cx):
        u1 = work[1, x + 1] + c1
        u1_ref[x] = u1
        to_north[x : x + 1] = u1[cy - 1 : cy]
        to_south[x : x + 1] = u1[0:1]
    east, west = u1_ref[cx - 1], u1_ref[0]
    to_a[...] = jnp.where(odd, west, east)
    to_b[...] = jnp.where(odd, east, west)


def dots_kernel(source, u0_ref, image, u1_ref, out):
    r_u0 = u0_v0 = v0_u1 = r_u1 = jnp.zeros((8, LANES), jnp.float32)
    for x in range(source.shape[0]):
        r, u0, v0, u1 = source[x], u0_ref[x], image[x], u1_ref[x]
        r_u0 = r_u0 + fold(r * u0)
        u0_v0 = u0_v0 + fold(u0 * v0)
        v0_u1 = v0_u1 + fold(v0 * u1)
        r_u1 = r_u1 + fold(r * u1)
    out[...] = placed(((1, total_of(r_u0)), (2, total_of(u0_v0)), (3, total_of(v0_u1)), (4, total_of(r_u1))))


def second_kernel(
    halo_a, halo_b, halo_north, halo_south, u0_ref, u1_ref, dots, storage,
    east_t, north_t, south_t, upper_t, lower_t, edge_east, edge_west, edge_north, edge_south,
    scale, w_east, w_west, w_north, w_south, w_upper, w_lower,
    result, out, padded, image, first, work,
):
    cx = storage.shape[0]
    odd = lax.axis_index("group") % 2 == 1
    a, b = halo_a[...], halo_b[...]
    padded[0] = jnp.where(odd, a, b)
    padded[cx + 1] = jnp.where(odd, b, a)
    for x in range(cx):
        padded[x + 1] = u1_ref[x]
    inner, outer = (east_t, north_t, south_t, upper_t, lower_t), (edge_east, edge_west, edge_north, edge_south)
    apply(padded, halo_north, halo_south, storage, inner, outer, image)
    total = u1_v1 = u0_v1 = jnp.zeros((8, LANES), jnp.float32)
    for x in range(cx):
        v1 = image[x]
        s = scale[x] * v1
        first[x] = s
        work[0, x + 1] = s
        total = total + fold(v1)
        u1_v1 = u1_v1 + fold(u1_ref[x] * v1)
        u0_v1 = u0_v1 + fold(u0_ref[x] * v1)
    clear_ends(work)
    smooth(first, work, (w_east, w_west, w_north, w_south, w_upper, w_lower))
    for x in range(cx):
        result[x] = work[1, x + 1]
    out[...] = dots[...] + placed(((0, total_of(total)), (5, total_of(u1_v1)), (6, total_of(u0_v1))))


def last_kernel(steps, table, solver, u0_ref, u1_ref, result, pressure, precond):
    t = table[...]
    me = lax.axis_index("sub")
    lane = lax.broadcasted_iota(jnp.int32, t.shape, 1)
    factors = [(solver[2 * step], solver[2 * step + 1]) for step in range(steps)]
    c2 = solve_rows(factors, solver[2 * steps], t)
    c2 = total_of(jnp.where((rows_of(t.shape) == me) & (lane == 0), c2, 0.0))
    sums = jnp.sum(t, axis=0, keepdims=True)
    r_u0, u0_v0, v0_u1, r_u1, u1_v1, u0_v1 = (sums[:, at : at + 1] for at in range(1, 7))
    a0 = r_u0 / u0_v0
    rz = r_u0 - a0 * r_u1 - a0 * u0_v0 + a0 * a0 * v0_u1
    keep = 1.0 + rz / r_u0
    a1 = rz / (keep * keep * u0_v0 - keep * a0 * (u0_v1 + v0_u1) + a0 * a0 * u1_v1)
    p0 = a0 + a1 * keep
    p1 = a1 * a0
    z1 = a0 + a1 * keep
    z2 = a1 * a0
    for x in range(u0_ref.shape[0]):
        u0, u1 = u0_ref[x], u1_ref[x]
        pressure[x] = p0 * u0 - p1 * u1
        precond[x] = u0 - z1 * u1 + z2 * (result[x] + c2)


def call(body, outs, scratch, *operands, cost=0):
    space = pl.BlockSpec(memory_space=pltpu.VMEM)
    estimate = pl.CostEstimate(flops=cost, bytes_accessed=4 * cost, transcendentals=0) if cost else None
    return pl.pallas_call(
        body,
        out_shape=[jax.ShapeDtypeStruct(s, jnp.float32) for s in outs],
        in_specs=[space] * len(operands),
        out_specs=[space] * len(outs),
        scratch_shapes=[pltpu.VMEM(s, jnp.float32) for s in scratch],
        compiler_params=pltpu.CompilerParams(vmem_limit_bytes=VMEM),
        cost_estimate=estimate,
    )(*operands)


def exchange(to_a, to_b, to_north, to_south):
    groups, peers = lax.axis_size("group"), lax.axis_size("sub")
    a = lax.ppermute(to_a, "group", [(i, i ^ 1) for i in range(groups)])
    b = lax.ppermute(to_b, "group", [(i, (((i + 1) ^ 1) - 1) % groups) for i in range(groups)])
    up = [(i, (i + 1) % peers) for i in range(peers)]
    south = lax.ppermute(to_north, "sub", up)
    north = lax.ppermute(to_south, "sub", [(j, i) for i, j in up])
    return a, b, north, south


def gather(row, axis):
    peers = lax.axis_size(axis)
    return lax.all_to_all(jnp.broadcast_to(row[None], (peers, 1, LANES)), axis, 0, 0).reshape(peers, LANES)


def shards(source, perm, storage):
    cx, cy, cz = source.shape
    members = lax.axis_size("sub")
    steps = members.bit_length() - 1
    full, wide, tall, layer, edge = (cx, cy, cz), (cx + 2, cy, cz), (cy + 8, cz), (cy, cz), (cx, cz)
    row, rounds = (1, LANES), [full, (2,) + wide]
    odd = lax.axis_index("group") % 2
    to_a = lax.dynamic_index_in_dim(perm, (1 - odd) * (cx - 1), 0, keepdims=False)
    to_b = lax.dynamic_index_in_dim(perm, odd * (cx - 1), 0, keepdims=False)
    halos = exchange(to_a, to_b, perm[:, -1], perm[:, 0])
    *inner, diagonal = call(inner_kernel, [(cx + 1, cy, cz)] + [full] * 5, [], perm, storage, cost=2**21)
    (sums,) = call(sums_kernel, [row], [], source, storage, cost=2**19)
    *made, result, to_a, to_b, to_north, to_south, own = call(
        assemble_kernel,
        [layer, layer, edge, edge] + [full] * 8 + [tall, tall, edge, edge, row],
        rounds,
        *halos, source, perm, storage, sums, *inner, diagonal,
    )
    shared = [storage, *inner, *made]
    halos = exchange(to_a, to_b, to_north, to_south)
    mixed = own + halos[0][cy : cy + 1, :LANES] + halos[1][cy : cy + 1, :LANES]
    mixed = jnp.where(jnp.arange(LANES)[None] < 64, mixed, halos[2][:1, :LANES] + halos[3][:1, :LANES])
    u0, image, u1, to_a, to_b, to_north, to_south, solver = call(
        functools.partial(first_kernel, steps),
        [full, full, full, layer, layer, edge, edge, (2 * steps + 1, members, LANES)],
        [wide] + rounds + [(2,) + edge],
        gather(mixed, "sub"), *halos, *shared, result,
    )
    halos = exchange(to_a, to_b, to_north, to_south)
    (dots,) = call(dots_kernel, [row], [], source, u0, image, u1, cost=2**20)
    result, mixed = call(second_kernel, [full, row], [wide, full] + rounds, *halos, u0, u1, dots, *shared)
    by_group = gather(mixed, "group")
    over_groups = sum(by_group[i : i + 1] for i in range(by_group.shape[0]))
    mixed = jnp.where(jnp.arange(LANES)[None] == 0, mixed, over_groups)
    table = gather(mixed, "sub")
    return tuple(call(functools.partial(last_kernel, steps), [full, full], [], table, solver, u0, u1, result))


def solution(mesh):
    spec = P("group", "sub", None)
    return jax.shard_map(shards, mesh=mesh, in_specs=(spec,) * 3, out_specs=(spec,) * 2, check_vma=False)
```

time: 119 us -> 107 us (0.90)
  blocking collectives: 29.2 us -> 51.6 us
  waiting for transfers between devices: 22.8 us -> 7.99 us
  starting transfers between devices: 42.1 us -> 30.6 us
  local copies, waits for them, and re-layouts: 12.8 us -> 4.48 us
    all_to_all x2 -> x3, blocking collectives: 29.2 us -> 51.6 us  [gather(): lax.all_to_all(jnp.broadcast_to(row[None], (peers, 1, LANES)), axis, 0, 0)]
    all_to_all x1 -> x0, starting transfers between devices: 12 us -> none  [gather(): lax.all_to_all(jnp.broadcast_to(row[None], (peers, 1, LANES)), axis, 0, 0)]
    ppermute x9, waiting for transfers between devices: 11.6 us -> 2.24 us  [the longest x3 2.22 us: exchange(): north = lax.ppermute(to_south, 'sub', [(j, i) for i, j in up])]
    all_to_all x1 -> x0, waiting for transfers between devices: 7.75 us -> none  [gather(): lax.all_to_all(jnp.broadcast_to(row[None], (peers, 1, LANES)), axis, 0, 0)]
    unnamed x34 -> x10, local copies, waits for them, and re-layouts: 10.5 us -> 2.78 us
    ppermute x3, waiting for transfers between devices: 3.36 us -> 5.75 us  [exchange(): south = lax.ppermute(to_north, 'sub', up)]
    pallas_call x4 -> x7, Pallas kernels: 10.9 us -> 10.9 us  [call(): pl.pallas_call(body, out_shape=[jax.ShapeDtypeStruct(s, jnp.float32) for...]
  transfers between devices with their start and end apart: 13 -> 12, of which waited for: 8 -> 4; matrix products, arithmetic and copies ran while one was open for 1% -> 1% of each run, Pallas kernels for 0% -> 1%
where the time goes in v2:
time: 107 us; the launch traced here: 106 us
  blocking collectives  51.6 us (48%)
  starting transfers between devices  30.6 us (29%)
  Pallas kernels  10.9 us (10%)
  waiting for transfers between devices  7.99 us (7%)
  local copies, waits for them, and re-layouts  4.48 us (4%)
    all_to_all x3, blocking collectives, gather(): lax.all_to_all(jnp.broadcast_to(row[None], (peers, 1, LANES)), axis, 0, 0)  51.6 us
    ppermute x3, starting transfers between devices, exchange(): lax.ppermute(to_b, 'group', [(i, ((i + 1 ^ 1) - 1) % groups) for i in ran...  15 us
    pallas_call x7, Pallas kernels, call(): pl.pallas_call(body, out_shape=[jax.ShapeDtypeStruct(s, jnp.float32) for...  10.9 us
    ppermute x3, starting transfers between devices, exchange(): a = lax.ppermute(to_a, 'group', [(i, i ^ 1) for i in range(groups)])  7.19 us
    ppermute x3, starting transfers between devices, exchange(): north = lax.ppermute(to_south, 'sub', [(j, i) for i, j in up])  6.54 us
    ppermute x3, waiting for transfers between devices, exchange(): south = lax.ppermute(to_north, 'sub', up)  5.75 us
    unnamed x10, local copies, waits for them, and re-layouts  2.78 us
    ppermute x3, waiting for transfers between devices, exchange(): north = lax.ppermute(to_south, 'sub', [(j, i) for i, j in up])  2.22 us
  transfers between devices with their start and end apart: 12, of which 4 were waited for; matrix products, arithmetic and copies ran while one was open for 1% of the time, Pallas kernels for 1%

profile of v2, /device:TPU:1, one launch (start us, length us, event | category | flops | bytes accessed | tf_op | source)
XLA Modules:
  0.0 106.4 jit_solution(12216637599543126264)
XLA Ops:
  0.7 0.8 dynamic-slice_bitcast_fusion
  1.4 7.7 %collective-permute-start.1 = (f32[32,256]{1,0:T(8,128)S(1)}, f32[32,256]{1,0:T(8,128)S(1)}, u32[]{:S(2)}, u32[]{:S(2)}) collective-permute-start(f32[32,256]{1,0:T(8,128)S(1)} %get-tuple-element.70), channel_id=1, source_target_pairs={{0,480},{32,64},{64,32},{96,128},{128,96},{160,192},{192,160},{224... | collective-permute-start | bytes 98312 | tf_op jit(solution)/shard_map/ppermute | solution.py:370
  9.1 1.9 %collective-permute-start = (f32[32,256]{1,0:T(8,128)S(1)}, f32[32,256]{1,0:T(8,128)S(1)}, u32[]{:S(2)}, u32[]{:S(2)}) collective-permute-start(f32[32,256]{1,0:T(8,128)S(1)} %get-tuple-element.71), channel_id=1, source_target_pairs={{0,32},{32,0},{64,96},{96,64},{128,160},{160,128},{192,224},{224,1... | collective-permute-start | bytes 98312 | tf_op jit(solution)/shard_map/ppermute | solution.py:369
  11.0 0.9 fusion.3
  11.9 1.1 %collective-permute-start.2 = (f32[8,256]{1,0:T(8,128)S(1)}, f32[8,256]{1,0:T(8,128)S(1)}, u32[]{:S(2)}, u32[]{:S(2)}) collective-permute-start(f32[8,256]{1,0:T(8,128)S(1)} %bitcast.24), channel_id=1, source_target_pairs={{1,0},{2,1},{3,2},{4,3},{5,4},{6,5},{7,6},{8,7},{9,8},{10,9},{11,1... | collective-permute-start | bytes 24584 | tf_op jit(solution)/shard_map/ppermute | solution.py:373
  13.1 1.4 %collective-permute-start.3 = (f32[8,256]{1,0:T(8,128)S(1)}, f32[8,256]{1,0:T(8,128)S(1)}, u32[]{:S(2)}, u32[]{:S(2)}) collective-permute-start(f32[8,256]{1,0:T(8,128)S(1)} %bitcast.25), channel_id=1, source_target_pairs={{0,1},{1,2},{2,3},{3,4},{4,5},{5,6},{6,7},{7,8},{8,9},{9,10},{10,1... | collective-permute-start | bytes 24584 | tf_op jit(solution)/shard_map/ppermute | solution.py:372
  14.5 0.9 copy-done
  15.4 0.9 copy-done.2
  16.4 0.1 shard_map.50.sums
  16.5 0.8 copy-done.1
  17.3 0.1 copy-done.3
  17.4 0.3 shard_map.51
  17.7 0.0 collective-permute-done.2.perm_north
  17.7 4.5 %collective-permute-done.3.perm_south = f32[8,256]{1,0:T(8,128)S(1)} collective-permute-done((f32[8,256]{1,0:T(8,128)S(1)}, f32[8,256]{1,0:T(8,128)S(1)}, u32[]{:S(2)}, u32[]{:S(2)}) %collective-permute-start.3) | collective-permute-done | bytes 8224 | tf_op jit(solution)/shard_map/ppermute | solution.py:372
  22.2 2.7 %shard_map.52 = (f32[32,256]{1,0:T(8,128)S(1)}, f32[32,256]{1,0:T(8,128)S(1)}, f32[8,256]{1,0:T(8,128)S(1)}, f32[8,256]{1,0:T(8,128)S(1)}, f32[8,32,256]{2,1,0:T...) custom-call(f32[32,256]{1,0:T(8,128)S(1)} %collective-permute-done.p, ...), custom_call_target="tpu_custom_call" | custom-call | tf_op jit(solution)/shard_map/pallas_call | solution.py:356
  24.9 3.4 %collective-permute-start.4 = (f32[40,256]{1,0:T(8,128)S(1)}, f32[40,256]{1,0:T(8,128)S(1)}, u32[]{:S(2)}, u32[]{:S(2)}) collective-permute-start(f32[40,256]{1,0:T(8,128)S(1)} %get-tuple-element.42), channel_id=1, source_target_pairs={{0,32},{32,0},{64,96},{96,64},{128,160},{160,128},{192,224},{224,1... | collective-permute-start | bytes 122888 | tf_op jit(solution)/shard_map/ppermute | solution.py:369
  28.2 1.9 %collective-permute-start.5 = (f32[40,256]{1,0:T(8,128)S(1)}, f32[40,256]{1,0:T(8,128)S(1)}, u32[]{:S(2)}, u32[]{:S(2)}) collective-permute-start(f32[40,256]{1,0:T(8,128)S(1)} %get-tuple-element.43), channel_id=1, source_target_pairs={{0,480},{32,64},{64,32},{96,128},{128,96},{160,192},{192,160},{224... | collective-permute-start | bytes 122888 | tf_op jit(solution)/shard_map/ppermute | solution.py:370
  30.2 4.2 %collective-permute-start.6 = (f32[8,256]{1,0:T(8,128)S(1)}, f32[8,256]{1,0:T(8,128)S(1)}, u32[]{:S(2)}, u32[]{:S(2)}) collective-permute-start(f32[8,256]{1,0:T(8,128)S(1)} %get-tuple-element.44), channel_id=1, source_target_pairs={{1,0},{2,1},{3,2},{4,3},{5,4},{6,5},{7,6},{8,7},{9,8},{10,9},{11,1... | collective-permute-start | bytes 24584 | tf_op jit(solution)/shard_map/ppermute | solution.py:373
  34.4 0.8 collective-permute-done.6.halo_north
  35.2 1.2 %collective-permute-done.7.halo_south = f32[8,256]{1,0:T(8,128)S(1)} collective-permute-done((f32[8,256]{1,0:T(8,128)S(1)}, f32[8,256]{1,0:T(8,128)S(1)}, u32[]{:S(2)}, u32[]{:S(2)}) %collective-permute-start.7) | collective-permute-done | bytes 8224 | tf_op jit(solution)/shard_map/ppermute | solution.py:372
  36.5 23.4 %all_to_all.15 = f32[32,1,128]{2,1,0:T(1,128)S(1)} all-to-all(f32[32,1,128]{2,1,0:T(1,128)S(1)} %broadcast_in_dim.13), channel_id=1, replica_groups=mesh['group'=16,'sub'=32] {'sub'}, dimensions={0} | all-to-all | bytes 32768 | tf_op jit(solution)/shard_map/all_to_all | solution.py:379
  59.9 3.4 %shard_map.53 = (f32[8,32,256]{2,1,0:T(8,128)S(1)}, f32[8,32,256]{2,1,0:T(8,128)S(1)}, f32[8,32,256]{2,1,0:T(8,128)S(1)}, f32[32,256]{1,0:T(8,128)S(1)}, f32[32,...) custom-call(f32[32,128]{1,0:T(8,128)S(1)} %bitcast.21, ...), custom_call_target="tpu_custom_call" | custom-call | tf_op jit(solution)/shard_map/pallas_call | solution.py:356
  63.2 1.9 %collective-permute-start.8 = (f32[32,256]{1,0:T(8,128)S(1)}, f32[32,256]{1,0:T(8,128)S(1)}, u32[]{:S(2)}, u32[]{:S(2)}) collective-permute-start(f32[32,256]{1,0:T(8,128)S(1)} %get-tuple-element.58), channel_id=1, source_target_pairs={{0,32},{32,0},{64,96},{96,64},{128,160},{160,128},{192,224},{224,1... | collective-permute-start | bytes 98312 | tf_op jit(solution)/shard_map/ppermute | solution.py:369
  65.2 5.4 %collective-permute-start.9 = (f32[32,256]{1,0:T(8,128)S(1)}, f32[32,256]{1,0:T(8,128)S(1)}, u32[]{:S(2)}, u32[]{:S(2)}) collective-permute-start(f32[32,256]{1,0:T(8,128)S(1)} %get-tuple-element.59), channel_id=1, source_target_pairs={{0,480},{32,64},{64,32},{96,128},{128,96},{160,192},{192,160},{224... | collective-permute-start | bytes 98312 | tf_op jit(solution)/shard_map/ppermute | solution.py:370
  70.6 1.2 %collective-permute-start.10 = (f32[8,256]{1,0:T(8,128)S(1)}, f32[8,256]{1,0:T(8,128)S(1)}, u32[]{:S(2)}, u32[]{:S(2)}) collective-permute-start(f32[8,256]{1,0:T(8,128)S(1)} %get-tuple-element.60), channel_id=1, source_target_pairs={{1,0},{2,1},{3,2},{4,3},{5,4},{6,5},{7,6},{8,7},{9,8},{10,9},{11,1... | collective-permute-start | bytes 24584 | tf_op jit(solution)/shard_map/ppermute | solution.py:373
  71.8 0.6 collective-permute-start.11
  72.3 0.2 shard_map.54.dots
  72.6 1.4 %collective-permute-done.10.halo_north = f32[8,256]{1,0:T(8,128)S(1)} collective-permute-done((f32[8,256]{1,0:T(8,128)S(1)}, f32[8,256]{1,0:T(8,128)S(1)}, u32[]{:S(2)}, u32[]{:S(2)}) %collective-permute-start.10) | collective-permute-done | bytes 8224 | tf_op jit(solution)/shard_map/ppermute | solution.py:373
  74.0 3.1 %shard_map.55 = (f32[8,32,256]{2,1,0:T(8,128)S(1)}, f32[1,128]{1,0:T(1,128)S(1)}) custom-call(f32[32,256]{1,0:T(8,128)S(1)} %collective-permute-done.8.halo_a, f32[32,256]{1,0:T(8,128)S(1)} %collective-permute-done.9.halo_b, f32[8,256]{1,0:T(8,128)S(1)} %collective-permute-done.10.halo_north, f32[8,256]{1,0:T(8,128)S(1)} %collective-permute-done.11.halo_south, ...), custom_call_target="tpu_custom_call" | custom-call | tf_op jit(solution)/shard_map/pallas_call | solution.py:356
  77.0 10.3 %all_to_all.16 = f32[16,1,128]{2,1,0:T(1,128)S(1)} all-to-all(f32[16,1,128]{2,1,0:T(1,128)S(1)} %broadcast_in_dim.29), channel_id=1, replica_groups=mesh['group'=16,'sub'=32] {'group'}, dimensions={0} | all-to-all | bytes 16384 | tf_op jit(solution)/shard_map/all_to_all | solution.py:379
  87.3 18.0 %all_to_all.17 = f32[32,1,128]{2,1,0:T(1,128)S(1)} all-to-all(f32[32,1,128]{2,1,0:T(1,128)S(1)} %broadcast_in_dim.31), channel_id=1, replica_groups=mesh['group'=16,'sub'=32] {'sub'}, dimensions={0} | all-to-all | bytes 32768 | tf_op jit(solution)/shard_map/all_to_all | solution.py:379
  105.3 1.1 %shard_map.56 = (f32[8,32,256]{2,1,0:T(8,128)}, f32[8,32,256]{2,1,0:T(8,128)}) custom-call(f32[32,128]{1,0:T(8,128)S(1)} %bitcast.22, f32[11,32,128]{2,1,0:T(8,128)S(1)} %get-tuple-element.66.solver, f32[8,32,256]{2,1,0:T(8,128)S(1)} %get-tuple-element.62.u0_ref, f32[8,32,256]{2,1,0:T(8,128)S(1)} %get-tuple-element.63.u1_ref, ...), custom_call_target="tpu_custom_call" | custom-call | tf_op jit(solution)/shard_map/pallas_call | solution.py:356
  (19 shorter events, 0.1 us)
Async XLA Ops:
  1.4 20.8 %collective-permute-start.1 = (f32[32,256]{1,0:T(8,128)S(1)}, f32[32,256]{1,0:T(8,128)S(1)}, u32[]{:S(2)}, u32[]{:S(2)}) collective-permute-start(f32[32,256]{1,0:T(8,128)S(1)} %get-tuple-element.70), channel_id=1, source_target_pairs={{0,480},{32,64},{64,32},{96,128},{128,96},{160,192},{192,160},{224... | collective-permute-start | bytes 98312 | tf_op jit(solution)/shard_map/ppermute | solution.py:370
  9.1 13.1 %collective-permute-start = (f32[32,256]{1,0:T(8,128)S(1)}, f32[32,256]{1,0:T(8,128)S(1)}, u32[]{:S(2)}, u32[]{:S(2)}) collective-permute-start(f32[32,256]{1,0:T(8,128)S(1)} %get-tuple-element.71), channel_id=1, source_target_pairs={{0,32},{32,0},{64,96},{96,64},{128,160},{160,128},{192,224},{224,1... | collective-permute-start | bytes 98312 | tf_op jit(solution)/shard_map/ppermute | solution.py:369
  11.9 5.8 %collective-permute-start.2 = (f32[8,256]{1,0:T(8,128)S(1)}, f32[8,256]{1,0:T(8,128)S(1)}, u32[]{:S(2)}, u32[]{:S(2)}) collective-permute-start(f32[8,256]{1,0:T(8,128)S(1)} %bitcast.24), channel_id=1, source_target_pairs={{1,0},{2,1},{3,2},{4,3},{5,4},{6,5},{7,6},{8,7},{9,8},{10,9},{11,1... | collective-permute-start | bytes 24584 | tf_op jit(solution)/shard_map/ppermute | solution.py:373
  13.1 9.1 %collective-permute-start.3 = (f32[8,256]{1,0:T(8,128)S(1)}, f32[8,256]{1,0:T(8,128)S(1)}, u32[]{:S(2)}, u32[]{:S(2)}) collective-permute-start(f32[8,256]{1,0:T(8,128)S(1)} %bitcast.25), channel_id=1, source_target_pairs={{0,1},{1,2},{2,3},{3,4},{4,5},{5,6},{6,7},{7,8},{8,9},{9,10},{10,1... | collective-permute-start | bytes 24584 | tf_op jit(solution)/shard_map/ppermute | solution.py:372
  14.5 0.9 copy-start
  15.4 0.9 copy-start.2
  16.4 0.9 copy-start.1
  16.4 1.0 copy-start.3
  24.9 11.6 %collective-permute-start.4 = (f32[40,256]{1,0:T(8,128)S(1)}, f32[40,256]{1,0:T(8,128)S(1)}, u32[]{:S(2)}, u32[]{:S(2)}) collective-permute-start(f32[40,256]{1,0:T(8,128)S(1)} %get-tuple-element.42), channel_id=1, source_target_pairs={{0,32},{32,0},{64,96},{96,64},{128,160},{160,128},{192,224},{224,1... | collective-permute-start | bytes 122888 | tf_op jit(solution)/shard_map/ppermute | solution.py:369
  28.2 8.2 %collective-permute-start.5 = (f32[40,256]{1,0:T(8,128)S(1)}, f32[40,256]{1,0:T(8,128)S(1)}, u32[]{:S(2)}, u32[]{:S(2)}) collective-permute-start(f32[40,256]{1,0:T(8,128)S(1)} %get-tuple-element.43), channel_id=1, source_target_pairs={{0,480},{32,64},{64,32},{96,128},{128,96},{160,192},{192,160},{224... | collective-permute-start | bytes 122888 | tf_op jit(solution)/shard_map/ppermute | solution.py:370
  30.2 5.0 %collective-permute-start.6 = (f32[8,256]{1,0:T(8,128)S(1)}, f32[8,256]{1,0:T(8,128)S(1)}, u32[]{:S(2)}, u32[]{:S(2)}) collective-permute-start(f32[8,256]{1,0:T(8,128)S(1)} %get-tuple-element.44), channel_id=1, source_target_pairs={{1,0},{2,1},{3,2},{4,3},{5,4},{6,5},{7,6},{8,7},{9,8},{10,9},{11,1... | collective-permute-start | bytes 24584 | tf_op jit(solution)/shard_map/ppermute | solution.py:373
  34.4 2.1 %collective-permute-start.7 = (f32[8,256]{1,0:T(8,128)S(1)}, f32[8,256]{1,0:T(8,128)S(1)}, u32[]{:S(2)}, u32[]{:S(2)}) collective-permute-start(f32[8,256]{1,0:T(8,128)S(1)} %get-tuple-element.45), channel_id=1, source_target_pairs={{0,1},{1,2},{2,3},{3,4},{4,5},{5,6},{6,7},{7,8},{8,9},{9,10},{10,1... | collective-permute-start | bytes 24584 | tf_op jit(solution)/shard_map/ppermute | solution.py:372
  63.2 10.7 %collective-permute-start.8 = (f32[32,256]{1,0:T(8,128)S(1)}, f32[32,256]{1,0:T(8,128)S(1)}, u32[]{:S(2)}, u32[]{:S(2)}) collective-permute-start(f32[32,256]{1,0:T(8,128)S(1)} %get-tuple-element.58), channel_id=1, source_target_pairs={{0,32},{32,0},{64,96},{96,64},{128,160},{160,128},{192,224},{224,1... | collective-permute-start | bytes 98312 | tf_op jit(solution)/shard_map/ppermute | solution.py:369
  65.2 8.8 %collective-permute-start.9 = (f32[32,256]{1,0:T(8,128)S(1)}, f32[32,256]{1,0:T(8,128)S(1)}, u32[]{:S(2)}, u32[]{:S(2)}) collective-permute-start(f32[32,256]{1,0:T(8,128)S(1)} %get-tuple-element.59), channel_id=1, source_target_pairs={{0,480},{32,64},{64,32},{96,128},{128,96},{160,192},{192,160},{224... | collective-permute-start | bytes 98312 | tf_op jit(solution)/shard_map/ppermute | solution.py:370
  70.6 3.4 %collective-permute-start.10 = (f32[8,256]{1,0:T(8,128)S(1)}, f32[8,256]{1,0:T(8,128)S(1)}, u32[]{:S(2)}, u32[]{:S(2)}) collective-permute-start(f32[8,256]{1,0:T(8,128)S(1)} %get-tuple-element.60), channel_id=1, source_target_pairs={{1,0},{2,1},{3,2},{4,3},{5,4},{6,5},{7,6},{8,7},{9,8},{10,9},{11,1... | collective-permute-start | bytes 24584 | tf_op jit(solution)/shard_map/ppermute | solution.py:373
  71.8 2.2 %collective-permute-start.11 = (f32[8,256]{1,0:T(8,128)S(1)}, f32[8,256]{1,0:T(8,128)S(1)}, u32[]{:S(2)}, u32[]{:S(2)}) collective-permute-start(f32[8,256]{1,0:T(8,128)S(1)} %get-tuple-element.61), channel_id=1, source_target_pairs={{0,1},{1,2},{2,3},{3,4},{4,5},{5,6},{6,7},{7,8},{8,9},{9,10},{10,1... | collective-permute-start | bytes 24584 | tf_op jit(solution)/shard_map/ppermute | solution.py:372

commit v3 on v2

--- a/solution.py
+++ b/solution.py
@@ -10,7 +10,7 @@
 OMEGA = 0.8
 LANES = 128
 VMEM = 16 * 2**20
-UNROLL = 1
+UNROLL = True
 STORED, COUPLING, SOURCE, PARTIAL, NORTH, SOUTH, EAST, WEST, EAST_T, WEST_T = range(10)
 FROM_EAST, FROM_WEST = 16, 32
 
@@ -128,10 +128,10 @@
 
 
 def assemble_kernel(
-    perm_a, perm_b, perm_north, perm_south, source, perm, storage, sums,
+    perm_a, perm_b, perm_north, perm_south, source, perm,
     east_in, north_in, south_in, upper_t, lower_t, diagonal,
     edge_east, edge_west, edge_north, edge_south,
-    scale, w_east, w_west, w_north, w_south, w_upper, w_lower, result, to_a, to_b, to_north, to_south, own, first, work,
+    scale, w_east, w_west, w_north, w_south, w_upper, w_lower, result, to_north, to_south, first, work,
 ):
     cx, cy, cz = source.shape
     odd = lax.axis_index("group") % 2 == 1
@@ -163,15 +163,23 @@
         work[0, x + 1] = s
     clear_ends(work)
     smooth(first, work, (w_east, w_west, w_north, w_south, w_upper, w_lower))
-    inside = jnp.zeros((8, LANES), jnp.float32)
     for x in range(cx):
         s = work[1, x + 1]
         result[x] = s
-        inside = inside + fold(storage[x] * s)
         to_north[x : x + 1] = s[cy - 1 : cy]
         to_south[x : x + 1] = s[0:1]
-    flux_east = total_of(fold(edge_east[...] * work[1, cx]))
-    flux_west = total_of(fold(edge_west[...] * work[1, 1]))
+
+
+def pack_kernel(
+    storage, sums, result, to_north, to_south, edge_east, edge_west, edge_north, edge_south, to_a, to_b, own
+):
+    cx, cy, cz = storage.shape
+    odd = lax.axis_index("group") % 2 == 1
+    inside = jnp.zeros((8, LANES), jnp.float32)
+    for x in range(cx):
+        inside = inside + fold(storage[x] * result[x])
+    flux_east = total_of(fold(edge_east[...] * result[cx - 1]))
+    flux_west = total_of(fold(edge_west[...] * result[0]))
     flux_north = total_of(edge_north[...] * to_north[...])
     flux_south = total_of(edge_south[...] * to_south[...])
     totals = (
@@ -193,7 +201,7 @@
         moved = jnp.concatenate([moved] + [jnp.zeros_like(moved)] * (cz // LANES - 1), axis=1)
         return layer, jnp.where(tail, moved, 0.0)
 
-    east, west = message(work[1, cx], FROM_WEST), message(work[1, 1], FROM_EAST)
+    east, west = message(result[cx - 1], FROM_WEST), message(result[0], FROM_EAST)
     for part, place in ((0, slice(0, cy)), (1, slice(cy, cy + 8))):
         to_a[place] = jnp.where(odd, west[part], east[part])
         to_b[place] = jnp.where(odd, east[part], west[part])
@@ -224,7 +232,7 @@
     steps, table, halo_a, halo_b, halo_north, halo_south, storage,
     east_t, north_t, south_t, upper_t, lower_t, edge_east, edge_west, edge_north, edge_south,
     scale, w_east, w_west, w_north, w_south, w_upper, w_lower, result,
-    u0_ref, image, u1_ref, to_a, to_b, to_north, to_south, solver, padded, first, work, edges,
+    u0_ref, image, u1_ref, to_north, to_south, solver, padded, first, work, edges,
 ):
     cx, cy, cz = storage.shape
     members = table.shape[0]
@@ -280,7 +288,11 @@
         u1_ref[x] = u1
         to_north[x : x + 1] = u1[cy - 1 : cy]
         to_south[x : x + 1] = u1[0:1]
-    east, west = u1_ref[cx - 1], u1_ref[0]
+
+
+def layers_kernel(field, to_a, to_b):
+    odd = lax.axis_index("group") % 2 == 1
+    west, east = field[0], field[field.shape[0] - 1]
     to_a[...] = jnp.where(odd, west, east)
     to_b[...] = jnp.where(odd, east, west)
 
@@ -391,22 +403,26 @@
     halos = exchange(to_a, to_b, perm[:, -1], perm[:, 0])
     *inner, diagonal = call(inner_kernel, [(cx + 1, cy, cz)] + [full] * 5, [], perm, storage, cost=2**21)
     (sums,) = call(sums_kernel, [row], [], source, storage, cost=2**19)
-    *made, result, to_a, to_b, to_north, to_south, own = call(
+    *made, result, to_north, to_south = call(
         assemble_kernel,
-        [layer, layer, edge, edge] + [full] * 8 + [tall, tall, edge, edge, row],
+        [layer, layer, edge, edge] + [full] * 8 + [edge, edge],
         rounds,
-        *halos, source, perm, storage, sums, *inner, diagonal,
+        *halos, source, perm, *inner, diagonal,
+    )
+    to_a, to_b, own = call(
+        pack_kernel, [tall, tall, row], [], storage, sums, result, to_north, to_south, *made[:4]
     )
     shared = [storage, *inner, *made]
     halos = exchange(to_a, to_b, to_north, to_south)
     mixed = own + halos[0][cy : cy + 1, :LANES] + halos[1][cy : cy + 1, :LANES]
     mixed = jnp.where(jnp.arange(LANES)[None] < 64, mixed, halos[2][:1, :LANES] + halos[3][:1, :LANES])
-    u0, image, u1, to_a, to_b, to_north, to_south, solver = call(
+    u0, image, u1, to_north, to_south, solver = call(
         functools.partial(first_kernel, steps),
-        [full, full, full, layer, layer, edge, edge, (2 * steps + 1, members, LANES)],
+        [full, full, full, edge, edge, (2 * steps + 1, members, LANES)],
         [wide] + rounds + [(2,) + edge],
         gather(mixed, "sub"), *halos, *shared, result,
     )
+    to_a, to_b = call(layers_kernel, [layer, layer], [], u1)
     halos = exchange(to_a, to_b, to_north, to_south)
     (dots,) = call(dots_kernel, [row], [], source, u0, image, u1, cost=2**20)
     result, mixed = call(second_kernel, [full, row], [wide, full] + rounds, *halos, u0, u1, dots, *shared)

time: 107 us -> 101 us (0.944)
  Pallas kernels: 10.9 us -> 4.83 us
    pallas_call x7 -> x9, Pallas kernels: 10.9 us -> 4.83 us  [call(): pl.pallas_call(body, out_shape=[jax.ShapeDtypeStruct(s, jnp.float32) for...]
    ppermute x3, waiting for transfers between devices: 0.01 us -> 1.5 us  [exchange(): lax.ppermute(to_b, 'group', [(i, ((i + 1 ^ 1) - 1) % groups) for i in ran...]
    unnamed x10 -> x12, local copies, waits for them, and re-layouts: 2.78 us -> 2.78 us
  transfers between devices with their start and end apart: 12 -> 12, of which waited for: 4 -> 6; matrix products, arithmetic and copies ran while one was open for 1% -> 1% of each run, Pallas kernels for 1% -> 1%
where the time goes in v3:
time: 101 us; the launch traced here: 100 us
  blocking collectives  52.2 us (52%)
  starting transfers between devices  29.9 us (30%)
  waiting for transfers between devices  7.97 us (8%)
  Pallas kernels  4.83 us (5%)
  local copies, waits for them, and re-layouts  4.49 us (4%)
    all_to_all x3, blocking collectives, gather(): lax.all_to_all(jnp.broadcast_to(row[None], (peers, 1, LANES)), axis, 0, 0)  52.2 us
    ppermute x3, starting transfers between devices, exchange(): lax.ppermute(to_b, 'group', [(i, ((i + 1 ^ 1) - 1) % groups) for i in ran...  14 us
    ppermute x3, starting transfers between devices, exchange(): a = lax.ppermute(to_a, 'group', [(i, i ^ 1) for i in range(groups)])  7.32 us
    ppermute x3, starting transfers between devices, exchange(): north = lax.ppermute(to_south, 'sub', [(j, i) for i, j in up])  6.54 us
    ppermute x3, waiting for transfers between devices, exchange(): south = lax.ppermute(to_north, 'sub', up)  5.17 us
    pallas_call x9, Pallas kernels, call(): pl.pallas_call(body, out_shape=[jax.ShapeDtypeStruct(s, jnp.float32) for...  4.83 us
    unnamed x12, local copies, waits for them, and re-layouts  2.78 us
  transfers between devices with their start and end apart: 12, of which 6 were waited for; matrix products, arithmetic and copies ran while one was open for 1% of the time, Pallas kernels for 1%

profile of v3, /device:TPU:1, one launch (start us, length us, event | category | flops | bytes accessed | tf_op | source)
XLA Modules:
  0.0 100.2 jit_solution(13258304866396053730)
XLA Ops:
  0.7 0.8 dynamic-slice_bitcast_fusion
  1.4 7.7 %collective-permute-start.1 = (f32[32,256]{1,0:T(8,128)S(1)}, f32[32,256]{1,0:T(8,128)S(1)}, u32[]{:S(2)}, u32[]{:S(2)}) collective-permute-start(f32[32,256]{1,0:T(8,128)S(1)} %get-tuple-element.70), channel_id=1, source_target_pairs={{0,480},{32,64},{64,32},{96,128},{128,96},{160,192},{192,160},{224... | collective-permute-start | bytes 98312 | tf_op jit(solution)/shard_map/ppermute | solution.py:382
  9.1 1.9 %collective-permute-start = (f32[32,256]{1,0:T(8,128)S(1)}, f32[32,256]{1,0:T(8,128)S(1)}, u32[]{:S(2)}, u32[]{:S(2)}) collective-permute-start(f32[32,256]{1,0:T(8,128)S(1)} %get-tuple-element.71), channel_id=1, source_target_pairs={{0,32},{32,0},{64,96},{96,64},{128,160},{160,128},{192,224},{224,1... | collective-permute-start | bytes 98312 | tf_op jit(solution)/shard_map/ppermute | solution.py:381
  11.0 0.9 fusion.3
  11.9 1.1 %collective-permute-start.2 = (f32[8,256]{1,0:T(8,128)S(1)}, f32[8,256]{1,0:T(8,128)S(1)}, u32[]{:S(2)}, u32[]{:S(2)}) collective-permute-start(f32[8,256]{1,0:T(8,128)S(1)} %bitcast.24), channel_id=1, source_target_pairs={{1,0},{2,1},{3,2},{4,3},{5,4},{6,5},{7,6},{8,7},{9,8},{10,9},{11,1... | collective-permute-start | bytes 24584 | tf_op jit(solution)/shard_map/ppermute | solution.py:385
  13.1 1.4 %collective-permute-start.3 = (f32[8,256]{1,0:T(8,128)S(1)}, f32[8,256]{1,0:T(8,128)S(1)}, u32[]{:S(2)}, u32[]{:S(2)}) collective-permute-start(f32[8,256]{1,0:T(8,128)S(1)} %bitcast.25), channel_id=1, source_target_pairs={{0,1},{1,2},{2,3},{3,4},{4,5},{5,6},{6,7},{7,8},{8,9},{9,10},{10,1... | collective-permute-start | bytes 24584 | tf_op jit(solution)/shard_map/ppermute | solution.py:384
  14.5 0.9 copy-done
  15.4 0.9 copy-done.2
  16.5 0.8 copy-done.1
  17.4 0.3 shard_map.51
  17.7 4.5 %collective-permute-done.3.perm_south = f32[8,256]{1,0:T(8,128)S(1)} collective-permute-done((f32[8,256]{1,0:T(8,128)S(1)}, f32[8,256]{1,0:T(8,128)S(1)}, u32[]{:S(2)}, u32[]{:S(2)}) %collective-permute-start.3) | collective-permute-done | bytes 8224 | tf_op jit(solution)/shard_map/ppermute | solution.py:384
  22.2 0.7 shard_map.52
  23.0 0.2 shard_map.53
  23.2 3.4 %collective-permute-start.4 = (f32[40,256]{1,0:T(8,128)S(1)}, f32[40,256]{1,0:T(8,128)S(1)}, u32[]{:S(2)}, u32[]{:S(2)}) collective-permute-start(f32[40,256]{1,0:T(8,128)S(1)} %get-tuple-element.49), channel_id=1, source_target_pairs={{0,32},{32,0},{64,96},{96,64},{128,160},{160,128},{192,224},{224,1... | collective-permute-start | bytes 122888 | tf_op jit(solution)/shard_map/ppermute | solution.py:381
  26.6 1.9 %collective-permute-start.5 = (f32[40,256]{1,0:T(8,128)S(1)}, f32[40,256]{1,0:T(8,128)S(1)}, u32[]{:S(2)}, u32[]{:S(2)}) collective-permute-start(f32[40,256]{1,0:T(8,128)S(1)} %get-tuple-element.50), channel_id=1, source_target_pairs={{0,480},{32,64},{64,32},{96,128},{128,96},{160,192},{192,160},{224... | collective-permute-start | bytes 122888 | tf_op jit(solution)/shard_map/ppermute | solution.py:382
  28.5 4.2 %collective-permute-start.6 = (f32[8,256]{1,0:T(8,128)S(1)}, f32[8,256]{1,0:T(8,128)S(1)}, u32[]{:S(2)}, u32[]{:S(2)}) collective-permute-start(f32[8,256]{1,0:T(8,128)S(1)} %get-tuple-element.43.to_south), channel_id=1, source_target_pairs={{1,0},{2,1},{3,2},{4,3},{5,4},{6,5},{7,6},{8,7},{9,8},{10,9},{11,1... | collective-permute-start | bytes 24584 | tf_op jit(solution)/shard_map/ppermute | solution.py:385
  32.7 0.6 collective-permute-done.7.halo_south
  33.3 0.2 collective-permute-done.6.halo_north
  33.5 1.1 %collective-permute-done.5.halo_b = f32[40,256]{1,0:T(8,128)S(1)} collective-permute-done((f32[40,256]{1,0:T(8,128)S(1)}, f32[40,256]{1,0:T(8,128)S(1)}, u32[]{:S(2)}, u32[]{:S(2)}) %collective-permute-start.5) | collective-permute-done | bytes 40992 | tf_op jit(solution)/shard_map/ppermute | solution.py:382
  34.6 23.5 %all_to_all.15 = f32[32,1,128]{2,1,0:T(1,128)S(1)} all-to-all(f32[32,1,128]{2,1,0:T(1,128)S(1)} %broadcast_in_dim.13), channel_id=1, replica_groups=mesh['group'=16,'sub'=32] {'sub'}, dimensions={0} | all-to-all | bytes 32768 | tf_op jit(solution)/shard_map/all_to_all | solution.py:391
  58.2 1.2 %shard_map.54 = (f32[8,32,256]{2,1,0:T(8,128)S(1)}, f32[8,32,256]{2,1,0:T(8,128)S(1)}, f32[8,32,256]{2,1,0:T(8,128)S(1)}, f32[8,256]{1,0:T(8,128)S(1)}, f32[8,25...) custom-call(f32[32,128]{1,0:T(8,128)S(1)} %bitcast.21, f32[40,256]{1,0:T(8,128)S(1)} %collective-permute-done.4.halo_a, ...), custom_call_target="tpu_custom_call" | custom-call | tf_op jit(solution)/shard_map/pallas_call | solution.py:368
  59.4 2.1 %collective-permute-start.8 = (f32[32,256]{1,0:T(8,128)S(1)}, f32[32,256]{1,0:T(8,128)S(1)}, u32[]{:S(2)}, u32[]{:S(2)}) collective-permute-start(f32[32,256]{1,0:T(8,128)S(1)} %get-tuple-element.59), channel_id=1, source_target_pairs={{0,32},{32,0},{64,96},{96,64},{128,160},{160,128},{192,224},{224,1... | collective-permute-start | bytes 98312 | tf_op jit(solution)/shard_map/ppermute | solution.py:381
  61.5 4.5 %collective-permute-start.9 = (f32[32,256]{1,0:T(8,128)S(1)}, f32[32,256]{1,0:T(8,128)S(1)}, u32[]{:S(2)}, u32[]{:S(2)}) collective-permute-start(f32[32,256]{1,0:T(8,128)S(1)} %get-tuple-element.60), channel_id=1, source_target_pairs={{0,480},{32,64},{64,32},{96,128},{128,96},{160,192},{192,160},{224... | collective-permute-start | bytes 98312 | tf_op jit(solution)/shard_map/ppermute | solution.py:382
  66.0 1.2 %collective-permute-start.10 = (f32[8,256]{1,0:T(8,128)S(1)}, f32[8,256]{1,0:T(8,128)S(1)}, u32[]{:S(2)}, u32[]{:S(2)}) collective-permute-start(f32[8,256]{1,0:T(8,128)S(1)} %get-tuple-element.61), channel_id=1, source_target_pairs={{1,0},{2,1},{3,2},{4,3},{5,4},{6,5},{7,6},{8,7},{9,8},{10,9},{11,1... | collective-permute-start | bytes 24584 | tf_op jit(solution)/shard_map/ppermute | solution.py:385
  67.2 0.6 collective-permute-start.11
  67.7 0.2 shard_map.56.dots
  67.9 1.1 %collective-permute-done.10.halo_north = f32[8,256]{1,0:T(8,128)S(1)} collective-permute-done((f32[8,256]{1,0:T(8,128)S(1)}, f32[8,256]{1,0:T(8,128)S(1)}, u32[]{:S(2)}, u32[]{:S(2)}) %collective-permute-start.10) | collective-permute-done | bytes 8224 | tf_op jit(solution)/shard_map/ppermute | solution.py:385
  69.0 0.4 collective-permute-done.9.halo_b
  69.5 0.9 shard_map.57
  70.4 10.1 %all_to_all.16 = f32[16,1,128]{2,1,0:T(1,128)S(1)} all-to-all(f32[16,1,128]{2,1,0:T(1,128)S(1)} %broadcast_in_dim.29), channel_id=1, replica_groups=mesh['group'=16,'sub'=32] {'group'}, dimensions={0} | all-to-all | bytes 16384 | tf_op jit(solution)/shard_map/all_to_all | solution.py:391
  80.6 18.5 %all_to_all.17 = f32[32,1,128]{2,1,0:T(1,128)S(1)} all-to-all(f32[32,1,128]{2,1,0:T(1,128)S(1)} %broadcast_in_dim.31), channel_id=1, replica_groups=mesh['group'=16,'sub'=32] {'sub'}, dimensions={0} | all-to-all | bytes 32768 | tf_op jit(solution)/shard_map/all_to_all | solution.py:391
  99.1 1.1 %shard_map.58 = (f32[8,32,256]{2,1,0:T(8,128)}, f32[8,32,256]{2,1,0:T(8,128)}) custom-call(f32[32,128]{1,0:T(8,128)S(1)} %bitcast.22, f32[11,32,128]{2,1,0:T(8,128)S(1)} %get-tuple-element.66.solver, f32[8,32,256]{2,1,0:T(8,128)S(1)} %get-tuple-element.63.u0_ref, f32[8,32,256]{2,1,0:T(8,128)S(1)} %get-tuple-element.58.field.u1_ref, ...), custom_call_target="tpu_custom_call" | custom-call | tf_op jit(solution)/shard_map/pallas_call | solution.py:368
  (23 shorter events, 0.4 us)
Async XLA Ops:
  1.4 20.8 %collective-permute-start.1 = (f32[32,256]{1,0:T(8,128)S(1)}, f32[32,256]{1,0:T(8,128)S(1)}, u32[]{:S(2)}, u32[]{:S(2)}) collective-permute-start(f32[32,256]{1,0:T(8,128)S(1)} %get-tuple-element.70), channel_id=1, source_target_pairs={{0,480},{32,64},{64,32},{96,128},{128,96},{160,192},{192,160},{224... | collective-permute-start | bytes 98312 | tf_op jit(solution)/shard_map/ppermute | solution.py:382
  9.1 13.1 %collective-permute-start = (f32[32,256]{1,0:T(8,128)S(1)}, f32[32,256]{1,0:T(8,128)S(1)}, u32[]{:S(2)}, u32[]{:S(2)}) collective-permute-start(f32[32,256]{1,0:T(8,128)S(1)} %get-tuple-element.71), channel_id=1, source_target_pairs={{0,32},{32,0},{64,96},{96,64},{128,160},{160,128},{192,224},{224,1... | collective-permute-start | bytes 98312 | tf_op jit(solution)/shard_map/ppermute | solution.py:381
  11.9 5.8 %collective-permute-start.2 = (f32[8,256]{1,0:T(8,128)S(1)}, f32[8,256]{1,0:T(8,128)S(1)}, u32[]{:S(2)}, u32[]{:S(2)}) collective-permute-start(f32[8,256]{1,0:T(8,128)S(1)} %bitcast.24), channel_id=1, source_target_pairs={{1,0},{2,1},{3,2},{4,3},{5,4},{6,5},{7,6},{8,7},{9,8},{10,9},{11,1... | collective-permute-start | bytes 24584 | tf_op jit(solution)/shard_map/ppermute | solution.py:385
  13.1 9.1 %collective-permute-start.3 = (f32[8,256]{1,0:T(8,128)S(1)}, f32[8,256]{1,0:T(8,128)S(1)}, u32[]{:S(2)}, u32[]{:S(2)}) collective-permute-start(f32[8,256]{1,0:T(8,128)S(1)} %bitcast.25), channel_id=1, source_target_pairs={{0,1},{1,2},{2,3},{3,4},{4,5},{5,6},{6,7},{7,8},{8,9},{9,10},{10,1... | collective-permute-start | bytes 24584 | tf_op jit(solution)/shard_map/ppermute | solution.py:384
  14.5 0.9 copy-start
  15.4 0.9 copy-start.2
  16.4 0.9 copy-start.1
  16.4 1.0 %copy-start.4 = (f32[8,32,256]{2,1,0:T(8,128)S(1)}, f32[8,32,256]{2,1,0:T(8,128)}, u32[]{:S(2)}) copy-start(f32[8,32,256]{2,1,0:T(8,128)} %perm.3) | copy-start | bytes 786436
  23.2 10.3 %collective-permute-start.4 = (f32[40,256]{1,0:T(8,128)S(1)}, f32[40,256]{1,0:T(8,128)S(1)}, u32[]{:S(2)}, u32[]{:S(2)}) collective-permute-start(f32[40,256]{1,0:T(8,128)S(1)} %get-tuple-element.49), channel_id=1, source_target_pairs={{0,32},{32,0},{64,96},{96,64},{128,160},{160,128},{192,224},{224,1... | collective-permute-start | bytes 122888 | tf_op jit(solution)/shard_map/ppermute | solution.py:381
  26.6 8.1 %collective-permute-start.5 = (f32[40,256]{1,0:T(8,128)S(1)}, f32[40,256]{1,0:T(8,128)S(1)}, u32[]{:S(2)}, u32[]{:S(2)}) collective-permute-start(f32[40,256]{1,0:T(8,128)S(1)} %get-tuple-element.50), channel_id=1, source_target_pairs={{0,480},{32,64},{64,32},{96,128},{128,96},{160,192},{192,160},{224... | collective-permute-start | bytes 122888 | tf_op jit(solution)/shard_map/ppermute | solution.py:382
  28.5 4.9 %collective-permute-start.7 = (f32[8,256]{1,0:T(8,128)S(1)}, f32[8,256]{1,0:T(8,128)S(1)}, u32[]{:S(2)}, u32[]{:S(2)}) collective-permute-start(f32[8,256]{1,0:T(8,128)S(1)} %get-tuple-element.42.to_north), channel_id=1, source_target_pairs={{0,1},{1,2},{2,3},{3,4},{4,5},{5,6},{6,7},{7,8},{8,9},{9,10},{10,1... | collective-permute-start | bytes 24584 | tf_op jit(solution)/shard_map/ppermute | solution.py:384
  28.5 5.0 %collective-permute-start.6 = (f32[8,256]{1,0:T(8,128)S(1)}, f32[8,256]{1,0:T(8,128)S(1)}, u32[]{:S(2)}, u32[]{:S(2)}) collective-permute-start(f32[8,256]{1,0:T(8,128)S(1)} %get-tuple-element.43.to_south), channel_id=1, source_target_pairs={{1,0},{2,1},{3,2},{4,3},{5,4},{6,5},{7,6},{8,7},{9,8},{10,9},{11,1... | collective-permute-start | bytes 24584 | tf_op jit(solution)/shard_map/ppermute | solution.py:385
  59.4 8.3 %copy-start.3 = (f32[8,32,256]{2,1,0:T(8,128)S(1)}, f32[8,32,256]{2,1,0:T(8,128)}, u32[]{:S(2)}) copy-start(f32[8,32,256]{2,1,0:T(8,128)} %source.5) | copy-start | bytes 786436
  59.4 9.6 %collective-permute-start.8 = (f32[32,256]{1,0:T(8,128)S(1)}, f32[32,256]{1,0:T(8,128)S(1)}, u32[]{:S(2)}, u32[]{:S(2)}) collective-permute-start(f32[32,256]{1,0:T(8,128)S(1)} %get-tuple-element.59), channel_id=1, source_target_pairs={{0,32},{32,0},{64,96},{96,64},{128,160},{160,128},{192,224},{224,1... | collective-permute-start | bytes 98312 | tf_op jit(solution)/shard_map/ppermute | solution.py:381
  61.5 8.0 %collective-permute-start.9 = (f32[32,256]{1,0:T(8,128)S(1)}, f32[32,256]{1,0:T(8,128)S(1)}, u32[]{:S(2)}, u32[]{:S(2)}) collective-permute-start(f32[32,256]{1,0:T(8,128)S(1)} %get-tuple-element.60), channel_id=1, source_target_pairs={{0,480},{32,64},{64,32},{96,128},{128,96},{160,192},{192,160},{224... | collective-permute-start | bytes 98312 | tf_op jit(solution)/shard_map/ppermute | solution.py:382
  66.0 3.1 %collective-permute-start.10 = (f32[8,256]{1,0:T(8,128)S(1)}, f32[8,256]{1,0:T(8,128)S(1)}, u32[]{:S(2)}, u32[]{:S(2)}) collective-permute-start(f32[8,256]{1,0:T(8,128)S(1)} %get-tuple-element.61), channel_id=1, source_target_pairs={{1,0},{2,1},{3,2},{4,3},{5,4},{6,5},{7,6},{8,7},{9,8},{10,9},{11,1... | collective-permute-start | bytes 24584 | tf_op jit(solution)/shard_map/ppermute | solution.py:385
  67.2 1.9 %collective-permute-start.11 = (f32[8,256]{1,0:T(8,128)S(1)}, f32[8,256]{1,0:T(8,128)S(1)}, u32[]{:S(2)}, u32[]{:S(2)}) collective-permute-start(f32[8,256]{1,0:T(8,128)S(1)} %get-tuple-element.62), channel_id=1, source_target_pairs={{0,1},{1,2},{2,3},{3,4},{4,5},{5,6},{6,7},{7,8},{8,9},{9,10},{10,1... | collective-permute-start | bytes 24584 | tf_op jit(solution)/shard_map/ppermute | solution.py:384

commit v4 on v2

v4 whole, which is shorter than its diff:
```python
import functools

import jax
import jax.numpy as jnp
from jax import lax
from jax.experimental import pallas as pl
from jax.experimental.pallas import tpu as pltpu
from jax.sharding import PartitionSpec as P

OMEGA = 0.8
LANES = 128
VMEM = 16 * 2**20
UNROLL = True
AGAINST, IMAGE, STORED, COUPLING, EAST = range(5)
DOTS = 120


def harmonic(left, right):
    return 2.0 * left * right / (left + right)


def shift(value, by, axis):
    return pltpu.roll(value, by % value.shape[axis], axis)


def rows_of(shape):
    return lax.broadcasted_iota(jnp.int32, shape, 0)


def fold(value):
    total = None
    for y in range(0, value.shape[0], 8):
        for z in range(0, value.shape[1], LANES):
            tile = value[y : y + 8, z : z + LANES]
            total = tile if total is None else total + tile
    return total


def total_of(value):
    return jnp.sum(value, axis=(0, 1), keepdims=True)


def placed(totals):
    lane = lax.broadcasted_iota(jnp.int32, (1, LANES), 1)
    row = jnp.zeros((1, LANES), jnp.float32)
    for at, total in totals:
        row = jnp.where(lane == at, total, row)
    return row


def smooth(first, work, weights):
    cx = first.shape[0]
    east, west, north, south, upper, lower = weights

    def sweep(src, dst):
        def slab(x, carry):
            s = src[x + 1]
            total = (1.0 - OMEGA) * s + first[x]
            total = total + east[x] * src[x + 2] + west[x] * src[x]
            total = total + north[x] * shift(s, -1, 0) + south[x] * shift(s, 1, 0)
            total = total + upper[x] * shift(s, -1, 1) + lower[x] * shift(s, 1, 1)
            dst[x + 1] = total
            return carry

        lax.fori_loop(0, cx, slab, 0, unroll=UNROLL)

    sweep(work.at[0], work.at[1])
    sweep(work.at[1], work.at[0])
    sweep(work.at[0], work.at[1])


def clear_ends(work):
    for at in range(2):
        for end in (0, work.shape[1] - 1):
            work[at, end] = jnp.zeros(work.shape[2:], jnp.float32)


def apply(padded, north_halo, south_halo, storage, inner, edges, out):
    cx, cy = storage.shape[:2]
    east_t, north_t, south_t, upper_t, lower_t = inner
    edge_east, edge_west, edge_north, edge_south = edges

    def slab(x, carry):
        u = padded[x + 1]
        row = rows_of(u.shape)
        total = storage[x] * u
        total = total + east_t[x + 1] * (u - padded[x + 2]) + east_t[x] * (u - padded[x])
        total = total + north_t[x] * (u - shift(u, -1, 0)) + south_t[x] * (u - shift(u, 1, 0))
        total = total + upper_t[x] * (u - shift(u, -1, 1)) + lower_t[x] * (u - shift(u, 1, 1))
        one = pl.ds(x, 1)
        north = jnp.where(row == cy - 1, edge_north[one] * (u - north_halo[one]), 0.0)
        total = total + jnp.where(row == 0, edge_south[one] * (u - south_halo[one]), north)
        out[x] = total
        return carry

    lax.fori_loop(0, cx, slab, 0, unroll=UNROLL)
    out[0] = out[0] + edge_west[...] * (padded[1] - padded[0])
    out[cx - 1] = out[cx - 1] + edge_east[...] * (padded[cx] - padded[cx + 1])


def load_kernel(
    source_in, perm_in, storage_in,
    source, perm, storage, east_t, north_t, south_t, upper_t, lower_t, diagonal, sums, sems,
):
    cx, cy, cz = source.shape
    pairs = ((perm_in, perm), (storage_in, storage), (source_in, source))
    copies = [pltpu.make_async_copy(src, dst, sems.at[at]) for at, (src, dst) in enumerate(pairs)]
    for copy in copies:
        copy.start()
    row = rows_of((cy, cz))
    west = jnp.zeros((cy, cz), jnp.float32)
    east_t[0] = west
    copies[0].wait()
    copies[1].wait()
    stored = total_r = jnp.zeros((8, LANES), jnp.float32)
    for x in range(cx):
        k = perm[x]
        east = harmonic(k, perm[x + 1]) if x + 1 < cx else jnp.zeros((cy, cz), jnp.float32)
        north = jnp.where(row == cy - 1, 0.0, harmonic(k, shift(k, -1, 0)))
        south = shift(north, 1, 0)
        upper = harmonic(k, shift(k, -1, 1))
        lower = shift(upper, 1, 1)
        east_t[x + 1] = east
        north_t[x] = north
        south_t[x] = south
        upper_t[x] = upper
        lower_t[x] = lower
        diagonal[x] = storage[x] + east + west + north + south + upper + lower
        stored = stored + fold(storage[x])
        west = east
    copies[2].wait()
    for x in range(cx):
        total_r = total_r + fold(source[x])
    sums[...] = placed(((0, total_of(stored)), (2, total_of(total_r))))


def edge_kernel(perm_north, perm_south, perm, sums, edge_north, edge_south, to_a, to_b, out):
    cx, cy = perm.shape[:2]
    top = jnp.concatenate([perm[x, cy - 1 : cy] for x in range(cx)], axis=0)
    bottom = jnp.concatenate([perm[x, 0:1] for x in range(cx)], axis=0)
    north = harmonic(top, perm_north[...])
    edge_north[...] = north
    edge_south[...] = harmonic(perm_south[...], bottom)
    out[...] = sums[...] + placed(((1, total_of(north)),))
    layers_kernel(perm, to_a, to_b)


def layers_kernel(field, to_a, to_b):
    odd = lax.axis_index("group") % 2 == 1
    west, east = field[0], field[field.shape[0] - 1]
    to_a[...] = jnp.where(odd, west, east)
    to_b[...] = jnp.where(odd, east, west)


def assemble_kernel(
    perm_a, perm_b, source, perm, east_in, north_in, south_in, upper_t, lower_t, diagonal, edge_north, edge_south,
    edge_east, edge_west, scale, w_east, w_west, w_north, w_south, w_upper, w_lower, result, first, work,
):
    cx, cy, cz = source.shape
    odd = lax.axis_index("group") % 2 == 1
    row = rows_of((cy, cz))
    a, b = perm_a[...], perm_b[...]
    edge_east[...] = harmonic(perm[cx - 1], jnp.where(odd, b, a))
    edge_west[...] = harmonic(jnp.where(odd, a, b), perm[0])
    for x in range(cx):
        d = diagonal[x]
        d = d + jnp.where(row == cy - 1, edge_north[x : x + 1], jnp.where(row == 0, edge_south[x : x + 1], 0.0))
        if x == 0:
            d = d + edge_west[...]
        if x == cx - 1:
            d = d + edge_east[...]
        q = OMEGA / d
        scale[x] = q
        w_east[x] = q * east_in[x + 1]
        w_west[x] = q * east_in[x]
        w_north[x] = q * north_in[x]
        w_south[x] = q * south_in[x]
        w_upper[x] = q * upper_t[x]
        w_lower[x] = q * lower_t[x]
        s = q * source[x]
        first[x] = s
        work[0, x + 1] = s
    clear_ends(work)
    smooth(first, work, (w_east, w_west, w_north, w_south, w_upper, w_lower))
    for x in range(cx):
        result[x] = work[1, x + 1]


def reduce_rows(margin, coupling, steps):
    before, after = shift(coupling, 1, 0), coupling
    factors = []
    for step in range(steps):
        h = 2**step
        inverse = 1.0 / (margin + before + after)
        from_before = before * shift(inverse, h, 0)
        from_after = after * shift(inverse, -h, 0)
        margin = margin + from_before * shift(margin, h, 0) + from_after * shift(margin, -h, 0)
        before, after = from_before * shift(before, h, 0), from_after * shift(after, -h, 0)
        factors.append((from_before, from_after))
    return factors, 1.0 / margin


def solve_rows(factors, last, right):
    for step, (from_before, from_after) in enumerate(factors):
        h = 2**step
        right = right + from_before * shift(right, h, 0) + from_after * shift(right, -h, 0)
    return right * last


def coarse_kernel(steps, table, result, u0_ref, to_a, to_b, to_north, to_south):
    cx, cy = result.shape[:2]
    members = table.shape[0]
    t = table[...]
    factors, last = reduce_rows(t / members, shift(t, -1, 1) * members, steps)
    c0 = solve_rows(factors, last, shift(t, -2, 1))
    lane = lax.broadcasted_iota(jnp.int32, t.shape, 1)
    c0 = total_of(jnp.where((rows_of(t.shape) == lax.axis_index("sub")) & (lane == 0), c0, 0.0))
    for x in range(cx):
        u = result[x] + c0
        u0_ref[x] = u
        to_north[x : x + 1] = u[cy - 1 : cy]
        to_south[x : x + 1] = u[0:1]
    layers_kernel(u0_ref, to_a, to_b)


def fill(padded, field, halo_a, halo_b):
    odd = lax.axis_index("group") % 2 == 1
    cx = field.shape[0]
    a, b = halo_a[...], halo_b[...]
    padded[0] = jnp.where(odd, a, b)
    padded[cx + 1] = jnp.where(odd, b, a)
    for x in range(cx):
        padded[x + 1] = field[x]


def first_kernel(
    halo_a, halo_b, halo_north, halo_south, u0_ref, storage,
    east_t, north_t, south_t, upper_t, lower_t, edge_east, edge_west, edge_north, edge_south,
    scale, w_east, w_west, w_north, w_south, w_upper, w_lower,
    image, result, to_north, to_south, padded, first, work,
):
    cx, cy, cz = storage.shape
    fill(padded, u0_ref, halo_a, halo_b)
    inner, outer = (east_t, north_t, south_t, upper_t, lower_t), (edge_east, edge_west, edge_north, edge_south)
    apply(padded, halo_north, halo_south, storage, inner, outer, image)
    for x in range(cx):
        s = scale[x] * image[x]
        first[x] = s
        work[0, x + 1] = s
    clear_ends(work)
    smooth(first, work, (w_east, w_west, w_north, w_south, w_upper, w_lower))
    for x in range(cx):
        f1 = work[1, x + 1]
        result[x] = f1
        to_north[x : x + 1] = f1[cy - 1 : cy]
        to_south[x : x + 1] = f1[0:1]


def dots_kernel(groups, source, u0_ref, image, f1_ref, edge_east, edge_north, sums, out):
    r_u0 = u0_v0 = v0_f1 = total = jnp.zeros((8, LANES), jnp.float32)
    for x in range(source.shape[0]):
        r, u0, v0, f1 = source[x], u0_ref[x], image[x], f1_ref[x]
        r_u0 = r_u0 + fold(r * u0)
        u0_v0 = u0_v0 + fold(u0 * v0)
        v0_f1 = v0_f1 + fold(v0 * f1)
        total = total + fold(v0)
    me = lax.axis_index("group")
    totals = (
        (AGAINST * groups + me, total_of(total)),
        (STORED * groups + me, sums[0:1, 0:1]),
        (COUPLING * groups + me, total_of(edge_north[...])),
        (EAST * groups + me, total_of(fold(edge_east[...]))),
        (DOTS, total_of(r_u0)),
        (DOTS + 1, total_of(u0_v0)),
        (DOTS + 2, total_of(v0_f1)),
    )
    out[...] = placed(totals)


def second_kernel(
    groups, halo_a, halo_b, halo_north, halo_south, f1_ref, dots, storage,
    east_t, north_t, south_t, upper_t, lower_t, edge_east, edge_west, edge_north, edge_south,
    image, out, padded,
):
    fill(padded, f1_ref, halo_a, halo_b)
    inner, outer = (east_t, north_t, south_t, upper_t, lower_t), (edge_east, edge_west, edge_north, edge_south)
    apply(padded, halo_north, halo_south, storage, inner, outer, image)
    total = f1_g1 = jnp.zeros((8, LANES), jnp.float32)
    for x in range(storage.shape[0]):
        g1 = image[x]
        total = total + fold(g1)
        f1_g1 = f1_g1 + fold(f1_ref[x] * g1)
    me = lax.axis_index("group")
    out[...] = dots[...] + placed(((IMAGE * groups + me, total_of(total)), (DOTS + 3, total_of(f1_g1))))


def last_kernel(
    steps, groups, table, u0_ref, f1_ref, image, storage, edge_east, edge_west, edge_north, edge_south,
    scale, w_east, w_west, w_north, w_south, w_upper, w_lower, pressure, precond, first, work,
):
    cx, cy, cz = storage.shape
    t = table[...]
    members = t.shape[0]
    lane = lax.broadcasted_iota(jnp.int32, t.shape, 1)
    mine = (rows_of(t.shape) == lax.axis_index("sub")) & (lane == lax.axis_index("group"))

    def column(at):
        return shift(t, -at * groups, 1)

    def pick(value):
        return total_of(jnp.where(mine, value, 0.0))

    def to_the_east(value):
        return jnp.where(lane == groups - 1, shift(value, groups - 1, 1), shift(value, -1, 1))

    def to_the_west(value):
        return jnp.where(lane == 0, shift(value, 1 - groups, 1), shift(value, 1, 1))

    against, image_sum, stored, after, right = (column(at) for at in (AGAINST, IMAGE, STORED, COUPLING, EAST))
    factors, last = reduce_rows(stored / members, after * members, steps)
    c1 = solve_rows(factors, last, against)
    c_east, c_west, c_north, c_south = to_the_east(c1), to_the_west(c1), shift(c1, -1, 0), shift(c1, 1, 0)
    coupled = (
        stored * c1 + after * (c1 - c_north) + shift(after, 1, 0) * (c1 - c_south)
        + right * (c1 - c_east) + to_the_west(right) * (c1 - c_west)
    )
    c2 = solve_rows(factors, last, image_sum + coupled)
    valid = lane < groups
    sums = jnp.sum(t, axis=0, keepdims=True)
    r_u0, u0_v0, v0_u1, u1_v1 = (sums[:, DOTS + at : DOTS + at + 1] for at in range(4))
    v0_u1 = v0_u1 + total_of(jnp.where(valid, c1 * against, 0.0))
    u1_v1 = u1_v1 + total_of(jnp.where(valid, c1 * (2.0 * image_sum + coupled), 0.0))
    c1, c_east, c_west, c_north, c_south, c2 = (pick(c) for c in (c1, c_east, c_west, c_north, c_south, c2))

    row = rows_of((cy, cz))
    for x in range(cx):
        one = slice(x, x + 1)
        edge = jnp.where(row == 0, edge_south[one] * (c1 - c_south), 0.0)
        edge = jnp.where(row == cy - 1, edge_north[one] * (c1 - c_north), edge)
        v1 = image[x] + storage[x] * c1 + edge
        if x == 0:
            v1 = v1 + edge_west[...] * (c1 - c_west)
        if x == cx - 1:
            v1 = v1 + edge_east[...] * (c1 - c_east)
        s = scale[x] * v1
        first[x] = s
        work[0, x + 1] = s
    clear_ends(work)
    smooth(first, work, (w_east, w_west, w_north, w_south, w_upper, w_lower))

    a0 = r_u0 / u0_v0
    rz = a0 * a0 * v0_u1 - r_u0
    keep = 1.0 + rz / r_u0
    a1 = rz / (keep * keep * u0_v0 - 2.0 * keep * a0 * v0_u1 + a0 * a0 * u1_v1)
    p0, p1, z2 = a0 + a1 * keep, a1 * a0, a1 * a0
    for x in range(cx):
        u0, u1 = u0_ref[x], f1_ref[x] + c1
        pressure[x] = p0 * u0 - p1 * u1
        precond[x] = u0 - p0 * u1 + z2 * (work[1, x + 1] + c2)


def call(body, outs, scratch, *operands, cost=0, hbm=False):
    space = pl.BlockSpec(memory_space=pltpu.VMEM)
    return pl.pallas_call(
        body,
        out_shape=[jax.ShapeDtypeStruct(s, jnp.float32) for s in outs],
        in_specs=[pl.BlockSpec(memory_space=pl.ANY) if hbm else space] * len(operands),
        out_specs=[space] * len(outs),
        scratch_shapes=[pltpu.VMEM(s, jnp.float32) if isinstance(s, tuple) else s for s in scratch],
        compiler_params=pltpu.CompilerParams(vmem_limit_bytes=VMEM),
        cost_estimate=pl.CostEstimate(flops=cost, bytes_accessed=4 * cost, transcendentals=0) if cost else None,
    )(*operands)


def over_group(to_a, to_b):
    groups = lax.axis_size("group")
    a = lax.ppermute(to_a, "group", [(i, i ^ 1) for i in range(groups)])
    b = lax.ppermute(to_b, "group", [(i, (((i + 1) ^ 1) - 1) % groups) for i in range(groups)])
    return a, b


def over_sub(to_north, to_south):
    peers = lax.axis_size("sub")
    up = [(i, (i + 1) % peers) for i in range(peers)]
    south = lax.ppermute(to_north, "sub", up)
    north = lax.ppermute(to_south, "sub", [(j, i) for i, j in up])
    return north, south


def gather(row, axis):
    peers = lax.axis_size(axis)
    return lax.all_to_all(jnp.broadcast_to(row[None], (peers, 1, LANES)), axis, 0, 0).reshape(peers, LANES)


def shards(source, perm, storage):
    cx, cy, cz = source.shape
    groups, members = lax.axis_size("group"), lax.axis_size("sub")
    steps = members.bit_length() - 1
    full, wide, layer, edge, row = (cx, cy, cz), (cx + 2, cy, cz), (cy, cz), (cx, cz), (1, LANES)
    rounds = [full, (2,) + wide]
    halos = over_sub(perm[:, -1], perm[:, 0])
    source, perm, storage, *inner, diagonal, sums = call(
        load_kernel,
        [full] * 3 + [(cx + 1, cy, cz)] + [full] * 5 + [row],
        [pltpu.SemaphoreType.DMA((3,))],
        source, perm, storage, cost=2**21, hbm=True,
    )
    edge_north, edge_south, to_a, to_b, scalars = call(
        edge_kernel, [edge, edge, layer, layer, row], [], *halos, perm, sums
    )
    table = gather(scalars, "sub")
    edge_east, edge_west, *weights, result = call(
        assemble_kernel,
        [layer, layer] + [full] * 8,
        rounds,
        *over_group(to_a, to_b), source, perm, *inner, diagonal, edge_north, edge_south, cost=2**21,
    )
    outer = [edge_east, edge_west, edge_north, edge_south]
    u0, to_a, to_b, to_north, to_south = call(
        functools.partial(coarse_kernel, steps), [full, layer, layer, edge, edge], [], table, result
    )
    halos = over_group(to_a, to_b) + over_sub(to_north, to_south)
    v0, f1, to_north, to_south = call(
        first_kernel, [full, full, edge, edge], [wide] + rounds, *halos, u0, storage, *inner, *outer, *weights
    )
    to_a, to_b = call(layers_kernel, [layer, layer], [], f1)
    halos = over_group(to_a, to_b) + over_sub(to_north, to_south)
    (dots,) = call(
        functools.partial(dots_kernel, groups), [row], [],
        source, u0, v0, f1, edge_east, edge_north, sums, cost=2**20,
    )
    g1, scalars = call(
        functools.partial(second_kernel, groups), [full, row], [wide], *halos, f1, dots, storage, *inner, *outer
    )
    by_group = gather(scalars, "group")
    table = gather(sum(by_group[i : i + 1] for i in range(groups)), "sub")
    return tuple(
        call(
            functools.partial(last_kernel, steps, groups),
            [full, full],
            rounds,
            table, u0, f1, g1, storage, *outer, *weights,
        )
    )


def solution(mesh):
    spec = P("group", "sub", None)
    return jax.shard_map(shards, mesh=mesh, in_specs=(spec,) * 3, out_specs=(spec,) * 2, check_vma=False)
```

time: 107 us -> 106 us (level)
  starting transfers between devices: 30.6 us -> 47.8 us
  blocking collectives: 51.6 us -> 36.7 us
  Pallas kernels: 10.9 us -> 5.02 us
  local copies, waits for them, and re-layouts: 4.48 us -> 10 us
  waiting for transfers between devices: 7.99 us -> 4.8 us
    all_to_all x3 -> x2, blocking collectives: 51.6 us -> 36.7 us  [gather(): lax.all_to_all(jnp.broadcast_to(row[None], (peers, 1, LANES)), axis, 0, 0)]
    all_to_all x0 -> x1, starting transfers between devices: none -> 10.9 us  [gather(): lax.all_to_all(jnp.broadcast_to(row[None], (peers, 1, LANES)), axis, 0, 0)]
    ppermute x12, starting transfers between devices: 30.6 us -> 36.8 us  [the longest x3 15.6 us: over_group(): lax.ppermute(to_b, 'group', [(i, ((i + 1 ^ 1) - 1) % groups) for i in ran...]
    pallas_call x7 -> x9, Pallas kernels: 10.9 us -> 5.02 us  [call(): pl.pallas_call(body, out_shape=[jax.ShapeDtypeStruct(s, jnp.float32) for...]
    unnamed x10 -> x24, local copies, waits for them, and re-layouts: 2.78 us -> 8.53 us
    ppermute x12, waiting for transfers between devices: 7.99 us -> 4.79 us  [the longest x3 2.4 us: over_sub(): north = lax.ppermute(to_south, 'sub', [(j, i) for i, j in up])]
  transfers between devices with their start and end apart: 12 -> 13, of which waited for: 4 -> 4; matrix products, arithmetic and copies ran while one was open for 1% -> 0% of each run, Pallas kernels for 1% -> 1%
where the time goes in v4:
time: 106 us; the launch traced here: 105 us
  starting transfers between devices  47.8 us (45%)
  blocking collectives  36.7 us (35%)
  local copies, waits for them, and re-layouts  10 us (9%)
  Pallas kernels  5.02 us (5%)
  waiting for transfers between devices  4.8 us (5%)
    all_to_all x2, blocking collectives, gather(): lax.all_to_all(jnp.broadcast_to(row[None], (peers, 1, LANES)), axis, 0, 0)  36.7 us
    ppermute x3, starting transfers between devices, over_group(): lax.ppermute(to_b, 'group', [(i, ((i + 1 ^ 1) - 1) % groups) for i in ran...  15.6 us
    ppermute x3, starting transfers between devices, over_sub(): north = lax.ppermute(to_south, 'sub', [(j, i) for i, j in up])  11.6 us
    all_to_all x1, starting transfers between devices, gather(): lax.all_to_all(jnp.broadcast_to(row[None], (peers, 1, LANES)), axis, 0, 0)  10.9 us
    unnamed x24, local copies, waits for them, and re-layouts  8.53 us
    ppermute x3, starting transfers between devices, over_group(): a = lax.ppermute(to_a, 'group', [(i, i ^ 1) for i in range(groups)])  7.05 us
    pallas_call x9, Pallas kernels, call(): pl.pallas_call(body, out_shape=[jax.ShapeDtypeStruct(s, jnp.float32) for...  5.02 us
    ppermute x3, starting transfers between devices, over_sub(): south = lax.ppermute(to_north, 'sub', up)  2.6 us
  transfers between devices with their start and end apart: 13, of which 4 were waited for; matrix products, arithmetic and copies ran while one was open for 0% of the time, Pallas kernels for 1%

profile of v4, /device:TPU:1, one launch (start us, length us, event | category | flops | bytes accessed | tf_op | source)
XLA Modules:
  0.0 105.2 jit_solution(6338998300923450133)
XLA Ops:
  0.6 0.9 fusion.1
  1.5 6.9 %collective-permute-start = (f32[8,256]{1,0:T(8,128)S(1)}, f32[8,256]{1,0:T(8,128)S(1)}, u32[]{:S(2)}, u32[]{:S(2)}) collective-permute-start(f32[8,256]{1,0:T(8,128)S(1)} %bitcast.16), channel_id=1, source_target_pairs={{1,0},{2,1},{3,2},{4,3},{5,4},{6,5},{7,6},{8,7},{9,8},{10,9},{11,1... | collective-permute-start | bytes 24584 | tf_op jit(solution)/shard_map/ppermute | solution.py:386
  8.4 0.9 copy-done.4
  9.4 0.9 copy-done.5
  10.3 0.9 copy-done.6
  11.8 0.7 copy-done.7
  12.8 0.6 broadcast_in_dim.25
  13.4 10.9 %all-to-all-start = ((f32[32,1,128]{2,1,0:T(1,128)}), f32[32,1,128]{2,1,0:T(1,128)S(1)}, u32[]{:S(2)}, u32[]{:S(2)}) async-start(f32[32,1,128]{2,1,0:T(1,128)} %broadcast_in_dim.25), calls=%async_computation | async-start | bytes 32768 | tf_op jit(solution)/shard_map/all_to_all | solution.py:392
  24.3 3.2 %collective-permute-start.2 = (f32[32,256]{1,0:T(8,128)S(1)}, f32[32,256]{1,0:T(8,128)S(1)}, u32[]{:S(2)}, u32[]{:S(2)}) collective-permute-start(f32[32,256]{1,0:T(8,128)S(1)} %get-tuple-element.43), channel_id=1, source_target_pairs={{0,32},{32,0},{64,96},{96,64},{128,160},{160,128},{192,224},{224,1... | collective-permute-start | bytes 98312 | tf_op jit(solution)/shard_map/ppermute | solution.py:377
  27.6 6.0 %collective-permute-start.3 = (f32[32,256]{1,0:T(8,128)S(1)}, f32[32,256]{1,0:T(8,128)S(1)}, u32[]{:S(2)}, u32[]{:S(2)}) collective-permute-start(f32[32,256]{1,0:T(8,128)S(1)} %get-tuple-element.44), channel_id=1, source_target_pairs={{0,480},{32,64},{64,32},{96,128},{128,96},{160,192},{192,160},{224... | collective-permute-start | bytes 98312 | tf_op jit(solution)/shard_map/ppermute | solution.py:378
  33.6 2.3 %collective-permute-done.3.perm_b = f32[32,256]{1,0:T(8,128)S(1)} collective-permute-done((f32[32,256]{1,0:T(8,128)S(1)}, f32[32,256]{1,0:T(8,128)S(1)}, u32[]{:S(2)}, u32[]{:S(2)}) %collective-permute-start.3) | collective-permute-done | bytes 32800 | tf_op jit(solution)/shard_map/ppermute | solution.py:378
  35.8 0.9 copy-done.8
  36.8 0.7 shard_map.52
  37.5 0.7 copy-done
  38.2 0.7 copy-done.2
  38.9 0.7 copy-done.9
  39.6 1.0 copy-done.10
  40.9 1.9 %collective-permute-start.4 = (f32[32,256]{1,0:T(8,128)S(1)}, f32[32,256]{1,0:T(8,128)S(1)}, u32[]{:S(2)}, u32[]{:S(2)}) collective-permute-start(f32[32,256]{1,0:T(8,128)S(1)} %get-tuple-element.55), channel_id=1, source_target_pairs={{0,32},{32,0},{64,96},{96,64},{128,160},{160,128},{192,224},{224,1... | collective-permute-start | bytes 98312 | tf_op jit(solution)/shard_map/ppermute | solution.py:377
  42.8 6.0 %collective-permute-start.5 = (f32[32,256]{1,0:T(8,128)S(1)}, f32[32,256]{1,0:T(8,128)S(1)}, u32[]{:S(2)}, u32[]{:S(2)}) collective-permute-start(f32[32,256]{1,0:T(8,128)S(1)} %get-tuple-element.56), channel_id=1, source_target_pairs={{0,480},{32,64},{64,32},{96,128},{128,96},{160,192},{192,160},{224... | collective-permute-start | bytes 98312 | tf_op jit(solution)/shard_map/ppermute | solution.py:378
  48.8 1.7 %collective-permute-start.6 = (f32[8,256]{1,0:T(8,128)S(1)}, f32[8,256]{1,0:T(8,128)S(1)}, u32[]{:S(2)}, u32[]{:S(2)}) collective-permute-start(f32[8,256]{1,0:T(8,128)S(1)} %get-tuple-element.57), channel_id=1, source_target_pairs={{1,0},{2,1},{3,2},{4,3},{5,4},{6,5},{7,6},{8,7},{9,8},{10,9},{11,1... | collective-permute-start | bytes 24584 | tf_op jit(solution)/shard_map/ppermute | solution.py:386
  50.5 1.4 %collective-permute-start.7 = (f32[8,256]{1,0:T(8,128)S(1)}, f32[8,256]{1,0:T(8,128)S(1)}, u32[]{:S(2)}, u32[]{:S(2)}) collective-permute-start(f32[8,256]{1,0:T(8,128)S(1)} %get-tuple-element.58), channel_id=1, source_target_pairs={{0,1},{1,2},{2,3},{3,4},{4,5},{5,6},{6,7},{7,8},{8,9},{9,10},{10,1... | collective-permute-start | bytes 24584 | tf_op jit(solution)/shard_map/ppermute | solution.py:385
  51.9 1.3 %collective-permute-done.6.halo_north = f32[8,256]{1,0:T(8,128)S(1)} collective-permute-done((f32[8,256]{1,0:T(8,128)S(1)}, f32[8,256]{1,0:T(8,128)S(1)}, u32[]{:S(2)}, u32[]{:S(2)}) %collective-permute-start.6) | collective-permute-done | bytes 8224 | tf_op jit(solution)/shard_map/ppermute | solution.py:386
  53.3 0.9 copy-done.3
  54.2 0.8 shard_map.54
  55.1 1.9 %collective-permute-start.8 = (f32[32,256]{1,0:T(8,128)S(1)}, f32[32,256]{1,0:T(8,128)S(1)}, u32[]{:S(2)}, u32[]{:S(2)}) collective-permute-start(f32[32,256]{1,0:T(8,128)S(1)} %get-tuple-element.71), channel_id=1, source_target_pairs={{0,32},{32,0},{64,96},{96,64},{128,160},{160,128},{192,224},{224,1... | collective-permute-start | bytes 98312 | tf_op jit(solution)/shard_map/ppermute | solution.py:377
  57.0 3.6 %collective-permute-start.9 = (f32[32,256]{1,0:T(8,128)S(1)}, f32[32,256]{1,0:T(8,128)S(1)}, u32[]{:S(2)}, u32[]{:S(2)}) collective-permute-start(f32[32,256]{1,0:T(8,128)S(1)} %get-tuple-element.72), channel_id=1, source_target_pairs={{0,480},{32,64},{64,32},{96,128},{128,96},{160,192},{192,160},{224... | collective-permute-start | bytes 98312 | tf_op jit(solution)/shard_map/ppermute | solution.py:378
  60.6 3.1 %collective-permute-start.10 = (f32[8,256]{1,0:T(8,128)S(1)}, f32[8,256]{1,0:T(8,128)S(1)}, u32[]{:S(2)}, u32[]{:S(2)}) collective-permute-start(f32[8,256]{1,0:T(8,128)S(1)} %get-tuple-element.73), channel_id=1, source_target_pairs={{1,0},{2,1},{3,2},{4,3},{5,4},{6,5},{7,6},{8,7},{9,8},{10,9},{11,1... | collective-permute-start | bytes 24584 | tf_op jit(solution)/shard_map/ppermute | solution.py:386
  63.6 1.2 %collective-permute-start.11 = (f32[8,256]{1,0:T(8,128)S(1)}, f32[8,256]{1,0:T(8,128)S(1)}, u32[]{:S(2)}, u32[]{:S(2)}) collective-permute-start(f32[8,256]{1,0:T(8,128)S(1)} %get-tuple-element.74), channel_id=1, source_target_pairs={{0,1},{1,2},{2,3},{3,4},{4,5},{5,6},{6,7},{7,8},{8,9},{9,10},{10,1... | collective-permute-start | bytes 24584 | tf_op jit(solution)/shard_map/ppermute | solution.py:385
  65.0 1.1 %collective-permute-done.10.halo_north = f32[8,256]{1,0:T(8,128)S(1)} collective-permute-done((f32[8,256]{1,0:T(8,128)S(1)}, f32[8,256]{1,0:T(8,128)S(1)}, u32[]{:S(2)}, u32[]{:S(2)}) %collective-permute-start.10) | collective-permute-done | bytes 8224 | tf_op jit(solution)/shard_map/ppermute | solution.py:386
  66.6 9.3 %all_to_all.15 = f32[16,1,128]{2,1,0:T(1,128)S(1)} all-to-all(f32[16,1,128]{2,1,0:T(1,128)S(1)} %broadcast_in_dim.27), channel_id=1, replica_groups=mesh['group'=16,'sub'=32] {'group'}, dimensions={0} | all-to-all | bytes 16384 | tf_op jit(solution)/shard_map/all_to_all | solution.py:392
  75.9 27.4 %all_to_all.16 = f32[32,1,128]{2,1,0:T(1,128)S(1)} all-to-all(f32[32,1,128]{2,1,0:T(1,128)S(1)} %broadcast_in_dim.29), channel_id=1, replica_groups=mesh['group'=16,'sub'=32] {'sub'}, dimensions={0} | all-to-all | bytes 32768 | tf_op jit(solution)/shard_map/all_to_all | solution.py:392
  103.3 1.9 %shard_map.58 = (f32[8,32,256]{2,1,0:T(8,128)}, f32[8,32,256]{2,1,0:T(8,128)}) custom-call(f32[32,128]{1,0:T(8,128)S(1)} %bitcast.12, f32[8,32,256]{2,1,0:T(8,128)S(1)} %get-tuple-element.59.u0_ref, f32[8,32,256]{2,1,0:T(8,128)S(1)} %get-tuple-element.70.field.f1_ref, f32[8,32,256]{2,1,0:T(8,128)S(1)} %get-tuple-element.77.image, ...), custom_call_target="tpu_custom_call" | custom-call | tf_op jit(solution)/shard_map/pallas_call | solution.py:364
  (34 shorter events, 1.8 us)
Async XLA Ops:
  1.5 11.0 %collective-permute-start = (f32[8,256]{1,0:T(8,128)S(1)}, f32[8,256]{1,0:T(8,128)S(1)}, u32[]{:S(2)}, u32[]{:S(2)}) collective-permute-start(f32[8,256]{1,0:T(8,128)S(1)} %bitcast.16), channel_id=1, source_target_pairs={{1,0},{2,1},{3,2},{4,3},{5,4},{6,5},{7,6},{8,7},{9,8},{10,9},{11,1... | collective-permute-start | bytes 24584 | tf_op jit(solution)/shard_map/ppermute | solution.py:386
  8.4 4.2 %collective-permute-start.1 = (f32[8,256]{1,0:T(8,128)S(1)}, f32[8,256]{1,0:T(8,128)S(1)}, u32[]{:S(2)}, u32[]{:S(2)}) collective-permute-start(f32[8,256]{1,0:T(8,128)S(1)} %bitcast.17), channel_id=1, source_target_pairs={{0,1},{1,2},{2,3},{3,4},{4,5},{5,6},{6,7},{7,8},{8,9},{9,10},{10,1... | collective-permute-start | bytes 24584 | tf_op jit(solution)/shard_map/ppermute | solution.py:385
  8.4 1.0 copy-start.4
  9.4 0.9 copy-start.5
  10.3 0.9 copy-start.6
  11.8 0.7 copy-start.7
  13.4 26.2 %all-to-all-start = ((f32[32,1,128]{2,1,0:T(1,128)}), f32[32,1,128]{2,1,0:T(1,128)S(1)}, u32[]{:S(2)}, u32[]{:S(2)}) async-start(f32[32,1,128]{2,1,0:T(1,128)} %broadcast_in_dim.25), calls=%async_computation | async-start | bytes 32768 | tf_op jit(solution)/shard_map/all_to_all | solution.py:392
  24.3 9.2 %collective-permute-start.2 = (f32[32,256]{1,0:T(8,128)S(1)}, f32[32,256]{1,0:T(8,128)S(1)}, u32[]{:S(2)}, u32[]{:S(2)}) collective-permute-start(f32[32,256]{1,0:T(8,128)S(1)} %get-tuple-element.43), channel_id=1, source_target_pairs={{0,32},{32,0},{64,96},{96,64},{128,160},{160,128},{192,224},{224,1... | collective-permute-start | bytes 98312 | tf_op jit(solution)/shard_map/ppermute | solution.py:377
  27.6 8.3 %collective-permute-start.3 = (f32[32,256]{1,0:T(8,128)S(1)}, f32[32,256]{1,0:T(8,128)S(1)}, u32[]{:S(2)}, u32[]{:S(2)}) collective-permute-start(f32[32,256]{1,0:T(8,128)S(1)} %get-tuple-element.44), channel_id=1, source_target_pairs={{0,480},{32,64},{64,32},{96,128},{128,96},{160,192},{192,160},{224... | collective-permute-start | bytes 98312 | tf_op jit(solution)/shard_map/ppermute | solution.py:378
  35.8 1.0 copy-start.8
  37.5 0.7 copy-start
  38.2 0.7 copy-start.2
  38.9 0.7 copy-start.9
  39.6 13.7 %copy-start.1 = (f32[8,32,256]{2,1,0:T(8,128)S(1)}, f32[8,32,256]{2,1,0:T(8,128)}, u32[]{:S(2)}) copy-start(f32[8,32,256]{2,1,0:T(8,128)} %copy-done) | copy-start | bytes 786436
  39.6 1.0 copy-start.10
  40.9 12.3 %collective-permute-start.4 = (f32[32,256]{1,0:T(8,128)S(1)}, f32[32,256]{1,0:T(8,128)S(1)}, u32[]{:S(2)}, u32[]{:S(2)}) collective-permute-start(f32[32,256]{1,0:T(8,128)S(1)} %get-tuple-element.55), channel_id=1, source_target_pairs={{0,32},{32,0},{64,96},{96,64},{128,160},{160,128},{192,224},{224,1... | collective-permute-start | bytes 98312 | tf_op jit(solution)/shard_map/ppermute | solution.py:377
  42.8 10.4 %collective-permute-start.5 = (f32[32,256]{1,0:T(8,128)S(1)}, f32[32,256]{1,0:T(8,128)S(1)}, u32[]{:S(2)}, u32[]{:S(2)}) collective-permute-start(f32[32,256]{1,0:T(8,128)S(1)} %get-tuple-element.56), channel_id=1, source_target_pairs={{0,480},{32,64},{64,32},{96,128},{128,96},{160,192},{192,160},{224... | collective-permute-start | bytes 98312 | tf_op jit(solution)/shard_map/ppermute | solution.py:378
  48.8 4.4 %collective-permute-start.6 = (f32[8,256]{1,0:T(8,128)S(1)}, f32[8,256]{1,0:T(8,128)S(1)}, u32[]{:S(2)}, u32[]{:S(2)}) collective-permute-start(f32[8,256]{1,0:T(8,128)S(1)} %get-tuple-element.57), channel_id=1, source_target_pairs={{1,0},{2,1},{3,2},{4,3},{5,4},{6,5},{7,6},{8,7},{9,8},{10,9},{11,1... | collective-permute-start | bytes 24584 | tf_op jit(solution)/shard_map/ppermute | solution.py:386
  50.5 2.7 %collective-permute-start.7 = (f32[8,256]{1,0:T(8,128)S(1)}, f32[8,256]{1,0:T(8,128)S(1)}, u32[]{:S(2)}, u32[]{:S(2)}) collective-permute-start(f32[8,256]{1,0:T(8,128)S(1)} %get-tuple-element.58), channel_id=1, source_target_pairs={{0,1},{1,2},{2,3},{3,4},{4,5},{5,6},{6,7},{7,8},{8,9},{9,10},{10,1... | collective-permute-start | bytes 24584 | tf_op jit(solution)/shard_map/ppermute | solution.py:385
  53.2 1.0 copy-start.3
  55.1 11.0 %collective-permute-start.8 = (f32[32,256]{1,0:T(8,128)S(1)}, f32[32,256]{1,0:T(8,128)S(1)}, u32[]{:S(2)}, u32[]{:S(2)}) collective-permute-start(f32[32,256]{1,0:T(8,128)S(1)} %get-tuple-element.71), channel_id=1, source_target_pairs={{0,32},{32,0},{64,96},{96,64},{128,160},{160,128},{192,224},{224,1... | collective-permute-start | bytes 98312 | tf_op jit(solution)/shard_map/ppermute | solution.py:377
  57.0 9.1 %collective-permute-start.9 = (f32[32,256]{1,0:T(8,128)S(1)}, f32[32,256]{1,0:T(8,128)S(1)}, u32[]{:S(2)}, u32[]{:S(2)}) collective-permute-start(f32[32,256]{1,0:T(8,128)S(1)} %get-tuple-element.72), channel_id=1, source_target_pairs={{0,480},{32,64},{64,32},{96,128},{128,96},{160,192},{192,160},{224... | collective-permute-start | bytes 98312 | tf_op jit(solution)/shard_map/ppermute | solution.py:378
  60.6 5.5 %collective-permute-start.10 = (f32[8,256]{1,0:T(8,128)S(1)}, f32[8,256]{1,0:T(8,128)S(1)}, u32[]{:S(2)}, u32[]{:S(2)}) collective-permute-start(f32[8,256]{1,0:T(8,128)S(1)} %get-tuple-element.73), channel_id=1, source_target_pairs={{1,0},{2,1},{3,2},{4,3},{5,4},{6,5},{7,6},{8,7},{9,8},{10,9},{11,1... | collective-permute-start | bytes 24584 | tf_op jit(solution)/shard_map/ppermute | solution.py:386
  63.6 2.5 %collective-permute-start.11 = (f32[8,256]{1,0:T(8,128)S(1)}, f32[8,256]{1,0:T(8,128)S(1)}, u32[]{:S(2)}, u32[]{:S(2)}) collective-permute-start(f32[8,256]{1,0:T(8,128)S(1)} %get-tuple-element.74), channel_id=1, source_target_pairs={{0,1},{1,2},{2,3},{3,4},{4,5},{5,6},{6,7},{7,8},{8,9},{9,10},{10,1... | collective-permute-start | bytes 24584 | tf_op jit(solution)/shard_map/ppermute | solution.py:385

commit v5 on v4

--- a/solution.py
+++ b/solution.py
@@ -98,20 +98,16 @@
     out[cx - 1] = out[cx - 1] + edge_east[...] * (padded[cx] - padded[cx + 1])
 
 
-def load_kernel(
-    source_in, perm_in, storage_in,
-    source, perm, storage, east_t, north_t, south_t, upper_t, lower_t, diagonal, sums, sems,
+def inner_kernel(
+    source, perm, storage,
+    source_out, storage_out, west_out, east_out, east_t, north_t, south_t, upper_t, lower_t, diagonal, sums,
 ):
     cx, cy, cz = source.shape
-    pairs = ((perm_in, perm), (storage_in, storage), (source_in, source))
-    copies = [pltpu.make_async_copy(src, dst, sems.at[at]) for at, (src, dst) in enumerate(pairs)]
-    for copy in copies:
-        copy.start()
+    west_out[...] = perm[0]
+    east_out[...] = perm[cx - 1]
     row = rows_of((cy, cz))
     west = jnp.zeros((cy, cz), jnp.float32)
     east_t[0] = west
-    copies[0].wait()
-    copies[1].wait()
     stored = total_r = jnp.zeros((8, LANES), jnp.float32)
     for x in range(cx):
         k = perm[x]
@@ -125,43 +121,69 @@
         south_t[x] = south
         upper_t[x] = upper
         lower_t[x] = lower
-        diagonal[x] = storage[x] + east + west + north + south + upper + lower
-        stored = stored + fold(storage[x])
+        w, r = storage[x], source[x]
+        diagonal[x] = w + east + west + north + south + upper + lower
+        storage_out[x] = w
+        source_out[x] = r
+        stored = stored + fold(w)
+        total_r = total_r + fold(r)
         west = east
-    copies[2].wait()
-    for x in range(cx):
-        total_r = total_r + fold(source[x])
     sums[...] = placed(((0, total_of(stored)), (2, total_of(total_r))))
 
 
-def edge_kernel(perm_north, perm_south, perm, sums, edge_north, edge_south, to_a, to_b, out):
-    cx, cy = perm.shape[:2]
-    top = jnp.concatenate([perm[x, cy - 1 : cy] for x in range(cx)], axis=0)
-    bottom = jnp.concatenate([perm[x, 0:1] for x in range(cx)], axis=0)
-    north = harmonic(top, perm_north[...])
+def edge_kernel(
+    perm_north, perm_south, strip_north, strip_south, west, east, sums, edge_north, edge_south, to_a, to_b, out
+):
+    north = harmonic(strip_north[...], perm_north[...])
     edge_north[...] = north
-    edge_south[...] = harmonic(perm_south[...], bottom)
-    out[...] = sums[...] + placed(((1, total_of(north)),))
-    layers_kernel(perm, to_a, to_b)
-
-
-def layers_kernel(field, to_a, to_b):
+    edge_south[...] = harmonic(perm_south[...], strip_south[...])
+    out[...] = jnp.broadcast_to(sums[...] + placed(((1, total_of(north)),)), out.shape)
+    by_side(west[...], east[...], to_a, to_b)
+
+
+def by_side(west, east, to_a, to_b):
     odd = lax.axis_index("group") % 2 == 1
-    west, east = field[0], field[field.shape[0] - 1]
     to_a[...] = jnp.where(odd, west, east)
     to_b[...] = jnp.where(odd, east, west)
 
 
+def layers_kernel(field, to_a, to_b):
+    by_side(field[0], field[field.shape[0] - 1], to_a, to_b)
+
+
+def reduce_rows(margin, coupling, steps):
+    before, after = shift(coupling, 1, 0), coupling
+    factors = []
+    for step in range(steps):
+        h = 2**step
+        inverse = 1.0 / (margin + before + after)
+        from_before = before * shift(inverse, h, 0)
+        from_after = after * shift(inverse, -h, 0)
+        margin = margin + from_before * shift(margin, h, 0) + from_after * shift(margin, -h, 0)
+        before, after = from_before * shift(before, h, 0), from_after * shift(after, -h, 0)
+        factors.append((from_before, from_after))
+    return factors, 1.0 / margin
+
+
+def solve_rows(factors, last, right):
+    for step, (from_before, from_after) in enumerate(factors):
+        h = 2**step
+        right = right + from_before * shift(right, h, 0) + from_after * shift(right, -h, 0)
+    return right * last
+
+
 def assemble_kernel(
-    perm_a, perm_b, source, perm, east_in, north_in, south_in, upper_t, lower_t, diagonal, edge_north, edge_south,
-    edge_east, edge_west, scale, w_east, w_west, w_north, w_south, w_upper, w_lower, result, first, work,
+    steps, perm_a, perm_b, table, source, perm_west, perm_east,
+    east_in, north_in, south_in, upper_t, lower_t, diagonal, edge_north, edge_south,
+    edge_east, edge_west, scale, w_east, w_west, w_north, w_south, w_upper, w_lower,
+    u0_ref, to_a, to_b, to_north, to_south, first, work,
 ):
     cx, cy, cz = source.shape
     odd = lax.axis_index("group") % 2 == 1
     row = rows_of((cy, cz))
     a, b = perm_a[...], perm_b[...]
-    edge_east[...] = harmonic(perm[cx - 1], jnp.where(odd, b, a))
-    edge_west[...] = harmonic(jnp.where(odd, a, b), perm[0])
+    edge_east[...] = harmonic(perm_east[...], jnp.where(odd, b, a))
+    edge_west[...] = harmonic(jnp.where(odd, a, b), perm_west[...])
     for x in range(cx):
         d = diagonal[x]
         d = d + jnp.where(row == cy - 1, edge_north[x : x + 1], jnp.where(row == 0, edge_south[x : x + 1], 0.0))
@@ -182,41 +204,15 @@
         work[0, x + 1] = s
     clear_ends(work)
     smooth(first, work, (w_east, w_west, w_north, w_south, w_upper, w_lower))
-    for x in range(cx):
-        result[x] = work[1, x + 1]
-
-
-def reduce_rows(margin, coupling, steps):
-    before, after = shift(coupling, 1, 0), coupling
-    factors = []
-    for step in range(steps):
-        h = 2**step
-        inverse = 1.0 / (margin + before + after)
-        from_before = before * shift(inverse, h, 0)
-        from_after = after * shift(inverse, -h, 0)
-        margin = margin + from_before * shift(margin, h, 0) + from_after * shift(margin, -h, 0)
-        before, after = from_before * shift(before, h, 0), from_after * shift(after, -h, 0)
-        factors.append((from_before, from_after))
-    return factors, 1.0 / margin
-
-
-def solve_rows(factors, last, right):
-    for step, (from_before, from_after) in enumerate(factors):
-        h = 2**step
-        right = right + from_before * shift(right, h, 0) + from_after * shift(right, -h, 0)
-    return right * last
-
-
-def coarse_kernel(steps, table, result, u0_ref, to_a, to_b, to_north, to_south):
-    cx, cy = result.shape[:2]
-    members = table.shape[0]
+
     t = table[...]
+    members = t.shape[0]
     factors, last = reduce_rows(t / members, shift(t, -1, 1) * members, steps)
     c0 = solve_rows(factors, last, shift(t, -2, 1))
     lane = lax.broadcasted_iota(jnp.int32, t.shape, 1)
     c0 = total_of(jnp.where((rows_of(t.shape) == lax.axis_index("sub")) & (lane == 0), c0, 0.0))
     for x in range(cx):
-        u = result[x] + c0
+        u = work[1, x + 1] + c0
         u0_ref[x] = u
         to_north[x : x + 1] = u[cy - 1 : cy]
         to_south[x : x + 1] = u[0:1]
@@ -359,14 +355,14 @@
         precond[x] = u0 - p0 * u1 + z2 * (work[1, x + 1] + c2)
 
 
-def call(body, outs, scratch, *operands, cost=0, hbm=False):
+def call(body, outs, scratch, *operands, cost=0):
     space = pl.BlockSpec(memory_space=pltpu.VMEM)
     return pl.pallas_call(
         body,
         out_shape=[jax.ShapeDtypeStruct(s, jnp.float32) for s in outs],
-        in_specs=[pl.BlockSpec(memory_space=pl.ANY) if hbm else space] * len(operands),
+        in_specs=[space] * len(operands),
         out_specs=[space] * len(outs),
-        scratch_shapes=[pltpu.VMEM(s, jnp.float32) if isinstance(s, tuple) else s for s in scratch],
+        scratch_shapes=[pltpu.VMEM(s, jnp.float32) for s in scratch],
         compiler_params=pltpu.CompilerParams(vmem_limit_bytes=VMEM),
         cost_estimate=pl.CostEstimate(flops=cost, bytes_accessed=4 * cost, transcendentals=0) if cost else None,
     )(*operands)
@@ -389,7 +385,8 @@
 
 def gather(row, axis):
     peers = lax.axis_size(axis)
-    return lax.all_to_all(jnp.broadcast_to(row[None], (peers, 1, LANES)), axis, 0, 0).reshape(peers, LANES)
+    rows = jnp.broadcast_to(row, (peers, LANES)).reshape(peers, 1, LANES)
+    return lax.all_to_all(rows, axis, 0, 0).reshape(peers, LANES)
 
 
 def shards(source, perm, storage):
@@ -398,27 +395,28 @@
     steps = members.bit_length() - 1
     full, wide, layer, edge, row = (cx, cy, cz), (cx + 2, cy, cz), (cy, cz), (cx, cz), (1, LANES)
     rounds = [full, (2,) + wide]
-    halos = over_sub(perm[:, -1], perm[:, 0])
-    source, perm, storage, *inner, diagonal, sums = call(
-        load_kernel,
-        [full] * 3 + [(cx + 1, cy, cz)] + [full] * 5 + [row],
-        [pltpu.SemaphoreType.DMA((3,))],
-        source, perm, storage, cost=2**21, hbm=True,
+    strip_north, strip_south = perm[:, -1], perm[:, 0]
+    halos = over_sub(strip_north, strip_south)
+    source, storage, west, east, *inner, diagonal, sums = call(
+        inner_kernel,
+        [full, full, layer, layer, (cx + 1, cy, cz)] + [full] * 5 + [row],
+        [],
+        source, perm, storage, cost=2**21,
     )
     edge_north, edge_south, to_a, to_b, scalars = call(
-        edge_kernel, [edge, edge, layer, layer, row], [], *halos, perm, sums
+        edge_kernel,
+        [edge, edge, layer, layer, (members, LANES)],
+        [],
+        *halos, strip_north, strip_south, west, east, sums,
     )
     table = gather(scalars, "sub")
-    edge_east, edge_west, *weights, result = call(
-        assemble_kernel,
-        [layer, layer] + [full] * 8,
+    edge_east, edge_west, *weights, u0, to_a, to_b, to_north, to_south = call(
+        functools.partial(assemble_kernel, steps),
+        [layer, layer] + [full] * 8 + [layer, layer, edge, edge],
         rounds,
-        *over_group(to_a, to_b), source, perm, *inner, diagonal, edge_north, edge_south, cost=2**21,
+        *over_group(to_a, to_b), table, source, west, east, *inner, diagonal, edge_north, edge_south,
     )
     outer = [edge_east, edge_west, edge_north, edge_south]
-    u0, to_a, to_b, to_north, to_south = call(
-        functools.partial(coarse_kernel, steps), [full, layer, layer, edge, edge], [], table, result
-    )
     halos = over_group(to_a, to_b) + over_sub(to_north, to_south)
     v0, f1, to_north, to_south = call(
         first_kernel, [full, full, edge, edge], [wide] + rounds, *halos, u0, storage, *inner, *outer, *weights

time: 106 us -> 99.8 us (0.942)
  local copies, waits for them, and re-layouts: 10 us -> 3.76 us
  waiting for transfers between devices: 4.8 us -> 6.2 us
  starting transfers between devices: 47.8 us -> 46.5 us
    unnamed x24 -> x8, local copies, waits for them, and re-layouts: 8.53 us -> 2.85 us
    ppermute x3, starting transfers between devices: 2.6 us -> 0.48 us  [over_sub(): south = lax.ppermute(to_north, 'sub', up)]
    ppermute x3, starting transfers between devices: 7.05 us -> 8.33 us  [over_group(): a = lax.ppermute(to_a, 'group', [(i, i ^ 1) for i in range(groups)])]
    pallas_call x9 -> x8, Pallas kernels: 5.02 us -> 5.4 us  [call(): pl.pallas_call(body, out_shape=[jax.ShapeDtypeStruct(s, jnp.float32) for...]
  transfers between devices with their start and end apart: 13 -> 13, of which waited for: 4 -> 5; matrix products, arithmetic and copies ran while one was open for 0% -> 0% of each run, Pallas kernels for 1% -> 1%
where the time goes in v5:
time: 99.8 us; the launch traced here: 99.2 us
  starting transfers between devices  46.5 us (47%)
  blocking collectives  36.6 us (37%)
  waiting for transfers between devices  6.2 us (6%)
  Pallas kernels  5.4 us (5%)
  local copies, waits for them, and re-layouts  3.76 us (4%)
    all_to_all x2, blocking collectives, gather(): return lax.all_to_all(rows, axis, 0, 0).reshape(peers, LANES)  36.6 us
    ppermute x3, starting transfers between devices, over_group(): lax.ppermute(to_b, 'group', [(i, ((i + 1 ^ 1) - 1) % groups) for i in ran...  16.6 us
    ppermute x3, starting transfers between devices, over_sub(): north = lax.ppermute(to_south, 'sub', [(j, i) for i, j in up])  11 us
    all_to_all x1, starting transfers between devices, gather(): return lax.all_to_all(rows, axis, 0, 0).reshape(peers, LANES)  10.1 us
    ppermute x3, starting transfers between devices, over_group(): a = lax.ppermute(to_a, 'group', [(i, i ^ 1) for i in range(groups)])  8.33 us
    pallas_call x8, Pallas kernels, call(): pl.pallas_call(body, out_shape=[jax.ShapeDtypeStruct(s, jnp.float32) for...  5.4 us
    unnamed x8, local copies, waits for them, and re-layouts  2.85 us
    ppermute x3, waiting for transfers between devices, over_sub(): north = lax.ppermute(to_south, 'sub', [(j, i) for i, j in up])  2.71 us
  transfers between devices with their start and end apart: 13, of which 5 were waited for; matrix products, arithmetic and copies ran while one was open for 0% of the time, Pallas kernels for 1%

profile of v5, /device:TPU:1, one launch (start us, length us, event | category | flops | bytes accessed | tf_op | source)
XLA Modules:
  0.0 99.2 jit_solution(4239983026896738501)
XLA Ops:
  0.6 0.9 fusion.1
  1.5 6.9 %collective-permute-start = (f32[8,256]{1,0:T(8,128)S(1)}, f32[8,256]{1,0:T(8,128)S(1)}, u32[]{:S(2)}, u32[]{:S(2)}) collective-permute-start(f32[8,256]{1,0:T(8,128)S(1)} %bitcast.16), channel_id=1, source_target_pairs={{1,0},{2,1},{3,2},{4,3},{5,4},{6,5},{7,6},{8,7},{9,8},{10,9},{11,1... | collective-permute-start | bytes 24584 | tf_op jit(solution)/shard_map/ppermute | solution.py:382
  8.4 0.9 copy-done
  9.4 0.9 copy-done.1
  10.3 0.9 copy-done.2
  11.3 0.4 shard_map.50
  11.6 0.0 collective-permute-done.perm_north
  11.7 1.0 collective-permute-done.1.perm_south
  12.7 0.7 shard_map.51
  13.4 10.1 %all-to-all-start = ((f32[32,1,128]{2,1,0:T(1,128)}), f32[32,1,128]{2,1,0:T(1,128)S(1)}, u32[]{:S(2)}, u32[]{:S(2)}) async-start(f32[32,1,128]{2,1,0:T(1,128)} %bitcast.3), calls=%async_computation | async-start | bytes 32768 | tf_op jit(solution)/shard_map/all_to_all | solution.py:389
  23.5 3.2 %collective-permute-start.2 = (f32[32,256]{1,0:T(8,128)S(1)}, f32[32,256]{1,0:T(8,128)S(1)}, u32[]{:S(2)}, u32[]{:S(2)}) collective-permute-start(f32[32,256]{1,0:T(8,128)S(1)} %get-tuple-element.43), channel_id=1, source_target_pairs={{0,32},{32,0},{64,96},{96,64},{128,160},{160,128},{192,224},{224,1... | collective-permute-start | bytes 98312 | tf_op jit(solution)/shard_map/ppermute | solution.py:373
  26.7 6.0 %collective-permute-start.3 = (f32[32,256]{1,0:T(8,128)S(1)}, f32[32,256]{1,0:T(8,128)S(1)}, u32[]{:S(2)}, u32[]{:S(2)}) collective-permute-start(f32[32,256]{1,0:T(8,128)S(1)} %get-tuple-element.44), channel_id=1, source_target_pairs={{0,480},{32,64},{64,32},{96,128},{128,96},{160,192},{192,160},{224... | collective-permute-start | bytes 98312 | tf_op jit(solution)/shard_map/ppermute | solution.py:374
  32.7 0.0 collective-permute-done.2.perm_a
  32.7 2.3 %collective-permute-done.3.perm_b = f32[32,256]{1,0:T(8,128)S(1)} collective-permute-done((f32[32,256]{1,0:T(8,128)S(1)}, f32[32,256]{1,0:T(8,128)S(1)}, u32[]{:S(2)}, u32[]{:S(2)}) %collective-permute-start.3) | collective-permute-done | bytes 32800 | tf_op jit(solution)/shard_map/ppermute | solution.py:374
  35.0 0.2 all-to-all-done
  35.2 0.8 shard_map.52
  36.0 3.2 %collective-permute-start.4 = (f32[32,256]{1,0:T(8,128)S(1)}, f32[32,256]{1,0:T(8,128)S(1)}, u32[]{:S(2)}, u32[]{:S(2)}) collective-permute-start(f32[32,256]{1,0:T(8,128)S(1)} %get-tuple-element.55), channel_id=1, source_target_pairs={{0,32},{32,0},{64,96},{96,64},{128,160},{160,128},{192,224},{224,1... | collective-permute-start | bytes 98312 | tf_op jit(solution)/shard_map/ppermute | solution.py:373
  39.2 6.0 %collective-permute-start.5 = (f32[32,256]{1,0:T(8,128)S(1)}, f32[32,256]{1,0:T(8,128)S(1)}, u32[]{:S(2)}, u32[]{:S(2)}) collective-permute-start(f32[32,256]{1,0:T(8,128)S(1)} %get-tuple-element.56), channel_id=1, source_target_pairs={{0,480},{32,64},{64,32},{96,128},{128,96},{160,192},{192,160},{224... | collective-permute-start | bytes 98312 | tf_op jit(solution)/shard_map/ppermute | solution.py:374
  45.3 1.5 %collective-permute-start.6 = (f32[8,256]{1,0:T(8,128)S(1)}, f32[8,256]{1,0:T(8,128)S(1)}, u32[]{:S(2)}, u32[]{:S(2)}) collective-permute-start(f32[8,256]{1,0:T(8,128)S(1)} %get-tuple-element.57), channel_id=1, source_target_pairs={{1,0},{2,1},{3,2},{4,3},{5,4},{6,5},{7,6},{8,7},{9,8},{10,9},{11,1... | collective-permute-start | bytes 24584 | tf_op jit(solution)/shard_map/ppermute | solution.py:382
  46.7 0.3 collective-permute-start.7
  47.0 1.6 %collective-permute-done.6.halo_north = f32[8,256]{1,0:T(8,128)S(1)} collective-permute-done((f32[8,256]{1,0:T(8,128)S(1)}, f32[8,256]{1,0:T(8,128)S(1)}, u32[]{:S(2)}, u32[]{:S(2)}) %collective-permute-start.6) | collective-permute-done | bytes 8224 | tf_op jit(solution)/shard_map/ppermute | solution.py:382
  48.6 0.9 shard_map.53
  49.6 1.9 %collective-permute-start.8 = (f32[32,256]{1,0:T(8,128)S(1)}, f32[32,256]{1,0:T(8,128)S(1)}, u32[]{:S(2)}, u32[]{:S(2)}) collective-permute-start(f32[32,256]{1,0:T(8,128)S(1)} %get-tuple-element.71), channel_id=1, source_target_pairs={{0,32},{32,0},{64,96},{96,64},{128,160},{160,128},{192,224},{224,1... | collective-permute-start | bytes 98312 | tf_op jit(solution)/shard_map/ppermute | solution.py:373
  51.5 4.6 %collective-permute-start.9 = (f32[32,256]{1,0:T(8,128)S(1)}, f32[32,256]{1,0:T(8,128)S(1)}, u32[]{:S(2)}, u32[]{:S(2)}) collective-permute-start(f32[32,256]{1,0:T(8,128)S(1)} %get-tuple-element.72), channel_id=1, source_target_pairs={{0,480},{32,64},{64,32},{96,128},{128,96},{160,192},{192,160},{224... | collective-permute-start | bytes 98312 | tf_op jit(solution)/shard_map/ppermute | solution.py:374
  56.1 2.6 %collective-permute-start.10 = (f32[8,256]{1,0:T(8,128)S(1)}, f32[8,256]{1,0:T(8,128)S(1)}, u32[]{:S(2)}, u32[]{:S(2)}) collective-permute-start(f32[8,256]{1,0:T(8,128)S(1)} %get-tuple-element.73), channel_id=1, source_target_pairs={{1,0},{2,1},{3,2},{4,3},{5,4},{6,5},{7,6},{8,7},{9,8},{10,9},{11,1... | collective-permute-start | bytes 24584 | tf_op jit(solution)/shard_map/ppermute | solution.py:382
  58.7 0.2 collective-permute-start.11
  58.9 0.2 shard_map.55.dots
  59.1 1.1 %collective-permute-done.10.halo_north = f32[8,256]{1,0:T(8,128)S(1)} collective-permute-done((f32[8,256]{1,0:T(8,128)S(1)}, f32[8,256]{1,0:T(8,128)S(1)}, u32[]{:S(2)}, u32[]{:S(2)}) %collective-permute-start.10) | collective-permute-done | bytes 8224 | tf_op jit(solution)/shard_map/ppermute | solution.py:382
  60.2 0.4 shard_map.56
  60.7 9.5 %all_to_all.15 = f32[16,1,128]{2,1,0:T(1,128)S(1)} all-to-all(f32[16,1,128]{2,1,0:T(1,128)S(1)} %reshape.152), channel_id=1, replica_groups=mesh['group'=16,'sub'=32] {'group'}, dimensions={0} | all-to-all | bytes 16384 | tf_op jit(solution)/shard_map/all_to_all | solution.py:389
  70.2 27.1 %all_to_all.16 = f32[32,1,128]{2,1,0:T(1,128)S(1)} all-to-all(f32[32,1,128]{2,1,0:T(1,128)S(1)} %reshape.153), channel_id=1, replica_groups=mesh['group'=16,'sub'=32] {'sub'}, dimensions={0} | all-to-all | bytes 32768 | tf_op jit(solution)/shard_map/all_to_all | solution.py:389
  97.3 1.9 %shard_map.57 = (f32[8,32,256]{2,1,0:T(8,128)}, f32[8,32,256]{2,1,0:T(8,128)}) custom-call(f32[32,128]{1,0:T(8,128)S(1)} %bitcast.15, f32[8,32,256]{2,1,0:T(8,128)S(1)} %get-tuple-element.59.u0_ref, f32[8,32,256]{2,1,0:T(8,128)S(1)} %get-tuple-element.70.field.f1_ref, f32[8,32,256]{2,1,0:T(8,128)S(1)} %get-tuple-element.77.image, ...), custom_call_target="tpu_custom_call" | custom-call | tf_op jit(solution)/shard_map/pallas_call | solution.py:360
  (16 shorter events, 0.1 us)
Async XLA Ops:
  1.5 10.1 %collective-permute-start = (f32[8,256]{1,0:T(8,128)S(1)}, f32[8,256]{1,0:T(8,128)S(1)}, u32[]{:S(2)}, u32[]{:S(2)}) collective-permute-start(f32[8,256]{1,0:T(8,128)S(1)} %bitcast.16), channel_id=1, source_target_pairs={{1,0},{2,1},{3,2},{4,3},{5,4},{6,5},{7,6},{8,7},{9,8},{10,9},{11,1... | collective-permute-start | bytes 24584 | tf_op jit(solution)/shard_map/ppermute | solution.py:382
  8.4 4.2 %collective-permute-start.1 = (f32[8,256]{1,0:T(8,128)S(1)}, f32[8,256]{1,0:T(8,128)S(1)}, u32[]{:S(2)}, u32[]{:S(2)}) collective-permute-start(f32[8,256]{1,0:T(8,128)S(1)} %bitcast.18), channel_id=1, source_target_pairs={{0,1},{1,2},{2,3},{3,4},{4,5},{5,6},{6,7},{7,8},{8,9},{9,10},{10,1... | collective-permute-start | bytes 24584 | tf_op jit(solution)/shard_map/ppermute | solution.py:381
  8.4 1.0 copy-start
  9.4 0.9 copy-start.1
  10.3 0.9 copy-start.2
  13.4 21.8 %all-to-all-start = ((f32[32,1,128]{2,1,0:T(1,128)}), f32[32,1,128]{2,1,0:T(1,128)S(1)}, u32[]{:S(2)}, u32[]{:S(2)}) async-start(f32[32,1,128]{2,1,0:T(1,128)} %bitcast.3), calls=%async_computation | async-start | bytes 32768 | tf_op jit(solution)/shard_map/all_to_all | solution.py:389
  23.5 9.2 %collective-permute-start.2 = (f32[32,256]{1,0:T(8,128)S(1)}, f32[32,256]{1,0:T(8,128)S(1)}, u32[]{:S(2)}, u32[]{:S(2)}) collective-permute-start(f32[32,256]{1,0:T(8,128)S(1)} %get-tuple-element.43), channel_id=1, source_target_pairs={{0,32},{32,0},{64,96},{96,64},{128,160},{160,128},{192,224},{224,1... | collective-permute-start | bytes 98312 | tf_op jit(solution)/shard_map/ppermute | solution.py:373
  26.7 8.3 %collective-permute-start.3 = (f32[32,256]{1,0:T(8,128)S(1)}, f32[32,256]{1,0:T(8,128)S(1)}, u32[]{:S(2)}, u32[]{:S(2)}) collective-permute-start(f32[32,256]{1,0:T(8,128)S(1)} %get-tuple-element.44), channel_id=1, source_target_pairs={{0,480},{32,64},{64,32},{96,128},{128,96},{160,192},{192,160},{224... | collective-permute-start | bytes 98312 | tf_op jit(solution)/shard_map/ppermute | solution.py:374
  36.0 12.6 %collective-permute-start.4 = (f32[32,256]{1,0:T(8,128)S(1)}, f32[32,256]{1,0:T(8,128)S(1)}, u32[]{:S(2)}, u32[]{:S(2)}) collective-permute-start(f32[32,256]{1,0:T(8,128)S(1)} %get-tuple-element.55), channel_id=1, source_target_pairs={{0,32},{32,0},{64,96},{96,64},{128,160},{160,128},{192,224},{224,1... | collective-permute-start | bytes 98312 | tf_op jit(solution)/shard_map/ppermute | solution.py:373
  39.2 9.4 %collective-permute-start.5 = (f32[32,256]{1,0:T(8,128)S(1)}, f32[32,256]{1,0:T(8,128)S(1)}, u32[]{:S(2)}, u32[]{:S(2)}) collective-permute-start(f32[32,256]{1,0:T(8,128)S(1)} %get-tuple-element.56), channel_id=1, source_target_pairs={{0,480},{32,64},{64,32},{96,128},{128,96},{160,192},{192,160},{224... | collective-permute-start | bytes 98312 | tf_op jit(solution)/shard_map/ppermute | solution.py:374
  45.3 3.4 %collective-permute-start.6 = (f32[8,256]{1,0:T(8,128)S(1)}, f32[8,256]{1,0:T(8,128)S(1)}, u32[]{:S(2)}, u32[]{:S(2)}) collective-permute-start(f32[8,256]{1,0:T(8,128)S(1)} %get-tuple-element.57), channel_id=1, source_target_pairs={{1,0},{2,1},{3,2},{4,3},{5,4},{6,5},{7,6},{8,7},{9,8},{10,9},{11,1... | collective-permute-start | bytes 24584 | tf_op jit(solution)/shard_map/ppermute | solution.py:382
  46.7 1.9 %collective-permute-start.7 = (f32[8,256]{1,0:T(8,128)S(1)}, f32[8,256]{1,0:T(8,128)S(1)}, u32[]{:S(2)}, u32[]{:S(2)}) collective-permute-start(f32[8,256]{1,0:T(8,128)S(1)} %get-tuple-element.58), channel_id=1, source_target_pairs={{0,1},{1,2},{2,3},{3,4},{4,5},{5,6},{6,7},{7,8},{8,9},{9,10},{10,1... | collective-permute-start | bytes 24584 | tf_op jit(solution)/shard_map/ppermute | solution.py:381
  49.6 10.6 %collective-permute-start.8 = (f32[32,256]{1,0:T(8,128)S(1)}, f32[32,256]{1,0:T(8,128)S(1)}, u32[]{:S(2)}, u32[]{:S(2)}) collective-permute-start(f32[32,256]{1,0:T(8,128)S(1)} %get-tuple-element.71), channel_id=1, source_target_pairs={{0,32},{32,0},{64,96},{96,64},{128,160},{160,128},{192,224},{224,1... | collective-permute-start | bytes 98312 | tf_op jit(solution)/shard_map/ppermute | solution.py:373
  51.5 8.7 %collective-permute-start.9 = (f32[32,256]{1,0:T(8,128)S(1)}, f32[32,256]{1,0:T(8,128)S(1)}, u32[]{:S(2)}, u32[]{:S(2)}) collective-permute-start(f32[32,256]{1,0:T(8,128)S(1)} %get-tuple-element.72), channel_id=1, source_target_pairs={{0,480},{32,64},{64,32},{96,128},{128,96},{160,192},{192,160},{224... | collective-permute-start | bytes 98312 | tf_op jit(solution)/shard_map/ppermute | solution.py:374
  56.1 4.1 %collective-permute-start.10 = (f32[8,256]{1,0:T(8,128)S(1)}, f32[8,256]{1,0:T(8,128)S(1)}, u32[]{:S(2)}, u32[]{:S(2)}) collective-permute-start(f32[8,256]{1,0:T(8,128)S(1)} %get-tuple-element.73), channel_id=1, source_target_pairs={{1,0},{2,1},{3,2},{4,3},{5,4},{6,5},{7,6},{8,7},{9,8},{10,9},{11,1... | collective-permute-start | bytes 24584 | tf_op jit(solution)/shard_map/ppermute | solution.py:382
  58.7 1.5 %collective-permute-start.11 = (f32[8,256]{1,0:T(8,128)S(1)}, f32[8,256]{1,0:T(8,128)S(1)}, u32[]{:S(2)}, u32[]{:S(2)}) collective-permute-start(f32[8,256]{1,0:T(8,128)S(1)} %get-tuple-element.74), channel_id=1, source_target_pairs={{0,1},{1,2},{2,3},{3,4},{4,5},{5,6},{6,7},{7,8},{8,9},{9,10},{10,1... | collective-permute-start | bytes 24584 | tf_op jit(solution)/shard_map/ppermute | solution.py:381

commit v6 on v5

--- a/solution.py
+++ b/solution.py
@@ -11,6 +11,7 @@
 LANES = 128
 VMEM = 16 * 2**20
 UNROLL = True
+SUB = ("z", "core")
 AGAINST, IMAGE, STORED, COUPLING, EAST = range(5)
 DOTS = 120
 
@@ -21,6 +22,10 @@
 
 def shift(value, by, axis):
     return pltpu.roll(value, by % value.shape[axis], axis)
+
+
+def my_sub():
+    return lax.axis_index("z") * lax.axis_size("core") + lax.axis_index("core")
 
 
 def rows_of(shape):
@@ -143,8 +148,8 @@
 
 def by_side(west, east, to_a, to_b):
     odd = lax.axis_index("group") % 2 == 1
-    to_a[...] = jnp.where(odd, west, east)
-    to_b[...] = jnp.where(odd, east, west)
+    to_a[...] = jnp.where(odd, east, west)
+    to_b[...] = jnp.where(odd, west, east)
 
 
 def layers_kernel(field, to_a, to_b):
@@ -182,8 +187,8 @@
     odd = lax.axis_index("group") % 2 == 1
     row = rows_of((cy, cz))
     a, b = perm_a[...], perm_b[...]
-    edge_east[...] = harmonic(perm_east[...], jnp.where(odd, b, a))
-    edge_west[...] = harmonic(jnp.where(odd, a, b), perm_west[...])
+    edge_east[...] = harmonic(perm_east[...], jnp.where(odd, a, b))
+    edge_west[...] = harmonic(jnp.where(odd, b, a), perm_west[...])
     for x in range(cx):
         d = diagonal[x]
         d = d + jnp.where(row == cy - 1, edge_north[x : x + 1], jnp.where(row == 0, edge_south[x : x + 1], 0.0))
@@ -210,7 +215,7 @@
     factors, last = reduce_rows(t / members, shift(t, -1, 1) * members, steps)
     c0 = solve_rows(factors, last, shift(t, -2, 1))
     lane = lax.broadcasted_iota(jnp.int32, t.shape, 1)
-    c0 = total_of(jnp.where((rows_of(t.shape) == lax.axis_index("sub")) & (lane == 0), c0, 0.0))
+    c0 = total_of(jnp.where((rows_of(t.shape) == my_sub()) & (lane == 0), c0, 0.0))
     for x in range(cx):
         u = work[1, x + 1] + c0
         u0_ref[x] = u
@@ -223,8 +228,8 @@
     odd = lax.axis_index("group") % 2 == 1
     cx = field.shape[0]
     a, b = halo_a[...], halo_b[...]
-    padded[0] = jnp.where(odd, a, b)
-    padded[cx + 1] = jnp.where(odd, b, a)
+    padded[0] = jnp.where(odd, b, a)
+    padded[cx + 1] = jnp.where(odd, a, b)
     for x in range(cx):
         padded[x + 1] = field[x]
 
@@ -287,18 +292,22 @@
         total = total + fold(g1)
         f1_g1 = f1_g1 + fold(f1_ref[x] * g1)
     me = lax.axis_index("group")
-    out[...] = dots[...] + placed(((IMAGE * groups + me, total_of(total)), (DOTS + 3, total_of(f1_g1))))
+    scalars = dots[...] + placed(((IMAGE * groups + me, total_of(total)), (DOTS + 3, total_of(f1_g1))))
+    core = lax.axis_index("core")
+    cores = out.shape[1] // LANES
+    out[...] = jnp.concatenate([jnp.where(core == at, scalars, 0.0) for at in range(cores)], axis=1)
 
 
 def last_kernel(
     steps, groups, table, u0_ref, f1_ref, image, storage, edge_east, edge_west, edge_north, edge_south,
-    scale, w_east, w_west, w_north, w_south, w_upper, w_lower, pressure, precond, first, work,
+    scale, w_east, w_west, w_north, w_south, w_upper, w_lower, pressure_out, precond_out,
+    first, work, pressure, precond, sems,
 ):
     cx, cy, cz = storage.shape
     t = table[...]
     members = t.shape[0]
     lane = lax.broadcasted_iota(jnp.int32, t.shape, 1)
-    mine = (rows_of(t.shape) == lax.axis_index("sub")) & (lane == lax.axis_index("group"))
+    mine = (rows_of(t.shape) == my_sub()) & (lane == lax.axis_index("group"))
 
     def column(at):
         return shift(t, -at * groups, 1)
@@ -328,8 +337,23 @@
     u1_v1 = u1_v1 + total_of(jnp.where(valid, c1 * (2.0 * image_sum + coupled), 0.0))
     c1, c_east, c_west, c_north, c_south, c2 = (pick(c) for c in (c1, c_east, c_west, c_north, c_south, c2))
 
+    a0 = r_u0 / u0_v0
+    rz = a0 * a0 * v0_u1 - r_u0
+    keep = 1.0 + rz / r_u0
+    a1 = rz / (keep * keep * u0_v0 - 2.0 * keep * a0 * v0_u1 + a0 * a0 * u1_v1)
+    p0, p1 = a0 + a1 * keep, a1 * a0
+
+    def send(at, x):
+        src, dst = ((pressure, pressure_out), (precond, precond_out))[at]
+        copy = pltpu.make_async_copy(src.at[x], dst.at[x], sems.at[at, x])
+        copy.start()
+        return copy
+
+    copies = []
     row = rows_of((cy, cz))
     for x in range(cx):
+        pressure[x] = p0 * u0_ref[x] - p1 * (f1_ref[x] + c1)
+        copies.append(send(0, x))
         one = slice(x, x + 1)
         edge = jnp.where(row == 0, edge_south[one] * (c1 - c_south), 0.0)
         edge = jnp.where(row == cy - 1, edge_north[one] * (c1 - c_north), edge)
@@ -343,26 +367,21 @@
         work[0, x + 1] = s
     clear_ends(work)
     smooth(first, work, (w_east, w_west, w_north, w_south, w_upper, w_lower))
-
-    a0 = r_u0 / u0_v0
-    rz = a0 * a0 * v0_u1 - r_u0
-    keep = 1.0 + rz / r_u0
-    a1 = rz / (keep * keep * u0_v0 - 2.0 * keep * a0 * v0_u1 + a0 * a0 * u1_v1)
-    p0, p1, z2 = a0 + a1 * keep, a1 * a0, a1 * a0
-    for x in range(cx):
-        u0, u1 = u0_ref[x], f1_ref[x] + c1
-        pressure[x] = p0 * u0 - p1 * u1
-        precond[x] = u0 - p0 * u1 + z2 * (work[1, x + 1] + c2)
-
-
-def call(body, outs, scratch, *operands, cost=0):
+    for x in range(cx):
+        precond[x] = u0_ref[x] - p0 * (f1_ref[x] + c1) + p1 * (work[1, x + 1] + c2)
+        copies.append(send(1, x))
+    for copy in copies:
+        copy.wait()
+
+
+def call(body, outs, scratch, *operands, cost=0, hbm=False):
     space = pl.BlockSpec(memory_space=pltpu.VMEM)
     return pl.pallas_call(
         body,
         out_shape=[jax.ShapeDtypeStruct(s, jnp.float32) for s in outs],
         in_specs=[space] * len(operands),
-        out_specs=[space] * len(outs),
-        scratch_shapes=[pltpu.VMEM(s, jnp.float32) for s in scratch],
+        out_specs=[pl.BlockSpec(memory_space=pl.ANY) if hbm else space] * len(outs),
+        scratch_shapes=[pltpu.VMEM(s, jnp.float32) if isinstance(s, tuple) else s for s in scratch],
         compiler_params=pltpu.CompilerParams(vmem_limit_bytes=VMEM),
         cost_estimate=pl.CostEstimate(flops=cost, bytes_accessed=4 * cost, transcendentals=0) if cost else None,
     )(*operands)
@@ -370,28 +389,28 @@
 
 def over_group(to_a, to_b):
     groups = lax.axis_size("group")
-    a = lax.ppermute(to_a, "group", [(i, i ^ 1) for i in range(groups)])
-    b = lax.ppermute(to_b, "group", [(i, (((i + 1) ^ 1) - 1) % groups) for i in range(groups)])
+    a = lax.ppermute(to_a, "group", [(i, (((i + 1) ^ 1) - 1) % groups) for i in range(groups)])
+    b = lax.ppermute(to_b, "group", [(i, i ^ 1) for i in range(groups)])
     return a, b
 
 
 def over_sub(to_north, to_south):
-    peers = lax.axis_size("sub")
+    peers = lax.axis_size(SUB)
     up = [(i, (i + 1) % peers) for i in range(peers)]
-    south = lax.ppermute(to_north, "sub", up)
-    north = lax.ppermute(to_south, "sub", [(j, i) for i, j in up])
+    south = lax.ppermute(to_north, SUB, up)
+    north = lax.ppermute(to_south, SUB, [(j, i) for i, j in up])
     return north, south
 
 
 def gather(row, axis):
     peers = lax.axis_size(axis)
-    rows = jnp.broadcast_to(row, (peers, LANES)).reshape(peers, 1, LANES)
-    return lax.all_to_all(rows, axis, 0, 0).reshape(peers, LANES)
+    rows = jnp.broadcast_to(row, (peers, row.shape[1]))[:, None]
+    return lax.all_to_all(rows, axis, 0, 0).reshape(peers, row.shape[1])
 
 
 def shards(source, perm, storage):
     cx, cy, cz = source.shape
-    groups, members = lax.axis_size("group"), lax.axis_size("sub")
+    groups, members = lax.axis_size("group"), lax.axis_size(SUB)
     steps = members.bit_length() - 1
     full, wide, layer, edge, row = (cx, cy, cz), (cx + 2, cy, cz), (cy, cz), (cx, cz), (1, LANES)
     rounds = [full, (2,) + wide]
@@ -409,7 +428,7 @@
         [],
         *halos, strip_north, strip_south, west, east, sums,
     )
-    table = gather(scalars, "sub")
+    table = gather(scalars, SUB)
     edge_east, edge_west, *weights, u0, to_a, to_b, to_north, to_south = call(
         functools.partial(assemble_kernel, steps),
         [layer, layer] + [full] * 8 + [layer, layer, edge, edge],
@@ -427,21 +446,29 @@
         functools.partial(dots_kernel, groups), [row], [],
         source, u0, v0, f1, edge_east, edge_north, sums, cost=2**20,
     )
+    cores = lax.axis_size("core")
     g1, scalars = call(
-        functools.partial(second_kernel, groups), [full, row], [wide], *halos, f1, dots, storage, *inner, *outer
-    )
-    by_group = gather(scalars, "group")
-    table = gather(sum(by_group[i : i + 1] for i in range(groups)), "sub")
+        functools.partial(second_kernel, groups),
+        [full, (1, cores * LANES)],
+        [wide],
+        *halos, f1, dots, storage, *inner, *outer,
+    )
+    scalars = gather(scalars, ("group", "core"))
+    scalars = sum(scalars[i : i + 1] for i in range(groups * cores))
+    table = gather(scalars, "z").reshape(members, LANES)
     return tuple(
         call(
             functools.partial(last_kernel, steps, groups),
             [full, full],
-            rounds,
-            table, u0, f1, g1, storage, *outer, *weights,
+            rounds + [full, full, pltpu.SemaphoreType.DMA((2, cx))],
+            table, u0, f1, g1, storage, *outer, *weights, hbm=True,
         )
     )
 
 
 def solution(mesh):
-    spec = P("group", "sub", None)
+    groups, members = (mesh.shape[axis] for axis in ("group", "sub"))
+    cores = 2
+    mesh = jax.sharding.Mesh(mesh.devices.reshape(groups, members // cores, cores), ("group", "z", "core"))
+    spec = P("group", SUB, None)
     return jax.shard_map(shards, mesh=mesh, in_specs=(spec,) * 3, out_specs=(spec,) * 2, check_vma=False)

time: 99.8 us -> 97.3 us (0.975)
  starting transfers between devices: 46.5 us -> 44.4 us
    ppermute x12, starting transfers between devices: 36.4 us -> 34.4 us  [the longest x3 17 us: over_group(): lax.ppermute(to_a, 'group', [(i, ((i + 1 ^ 1) - 1) % groups) for i in ran...]
  transfers between devices with their start and end apart: 13 -> 13, of which waited for: 5 -> 4; matrix products, arithmetic and copies ran while one was open for 0% -> 0% of each run, Pallas kernels for 1% -> 1%
where the time goes in v6:
time: 97.3 us; the launch traced here: 96.7 us
  starting transfers between devices  44.4 us (46%)
  blocking collectives  35.9 us (37%)
  waiting for transfers between devices  6.38 us (7%)
  Pallas kernels  5.44 us (6%)
  local copies, waits for them, and re-layouts  3.78 us (4%)
    all_to_all x2, blocking collectives, gather(): return lax.all_to_all(rows, axis, 0, 0).reshape(peers, row.shape[1])  35.9 us
    ppermute x3, starting transfers between devices, over_group(): lax.ppermute(to_a, 'group', [(i, ((i + 1 ^ 1) - 1) % groups) for i in ran...  17 us
    ppermute x3, starting transfers between devices, over_sub(): north = lax.ppermute(to_south, SUB, [(j, i) for i, j in up])  11 us
    all_to_all x1, starting transfers between devices, gather(): return lax.all_to_all(rows, axis, 0, 0).reshape(peers, row.shape[1])  10.1 us
    ppermute x3, starting transfers between devices, over_group(): b = lax.ppermute(to_b, 'group', [(i, i ^ 1) for i in range(groups)])  5.76 us
    pallas_call x8, Pallas kernels, call(): pl.pallas_call(body, out_shape=[jax.ShapeDtypeStruct(s, jnp.float32) for...  5.44 us
    ppermute x3, waiting for transfers between devices, over_group(): b = lax.ppermute(to_b, 'group', [(i, i ^ 1) for i in range(groups)])  3.02 us
    unnamed x8, local copies, waits for them, and re-layouts  2.85 us
  transfers between devices with their start and end apart: 13, of which 4 were waited for; matrix products, arithmetic and copies ran while one was open for 0% of the time, Pallas kernels for 1%

profile of v6, /device:TPU:1, one launch (start us, length us, event | category | flops | bytes accessed | tf_op | source)
XLA Modules:
  0.0 96.7 jit_solution(14696899698804526301)
XLA Ops:
  0.6 0.9 fusion
  1.5 6.9 %collective-permute-start = (f32[8,256]{1,0:T(8,128)S(1)}, f32[8,256]{1,0:T(8,128)S(1)}, u32[]{:S(2)}, u32[]{:S(2)}) collective-permute-start(f32[8,256]{1,0:T(8,128)S(1)} %bitcast.30), channel_id=1, source_target_pairs={{1,0},{2,1},{3,2},{4,3},{5,4},{6,5},{7,6},{8,7},{9,8},{10,9},{11,1... | collective-permute-start | bytes 24584 | tf_op jit(solution)/shard_map/ppermute | solution.py:401
  8.4 0.9 copy-done
  9.4 0.9 copy-done.1
  10.3 0.9 copy-done.2
  11.3 0.4 shard_map.50
  11.6 0.0 collective-permute-done.perm_north
  11.7 1.0 %collective-permute-done.1.perm_south = f32[8,256]{1,0:T(8,128)S(1)} collective-permute-done((f32[8,256]{1,0:T(8,128)S(1)}, f32[8,256]{1,0:T(8,128)S(1)}, u32[]{:S(2)}, u32[]{:S(2)}) %collective-permute-start.1) | collective-permute-done | bytes 8224 | tf_op jit(solution)/shard_map/ppermute | solution.py:400
  12.7 0.7 shard_map.51
  13.4 10.1 %all-to-all-start = ((f32[32,1,128]{2,1,0:T(1,128)}), f32[32,1,128]{2,1,0:T(1,128)S(1)}, u32[]{:S(2)}, u32[]{:S(2)}) async-start(f32[32,1,128]{2,1,0:T(1,128)} %bitcast.3), calls=%async_computation | async-start | bytes 32768 | tf_op jit(solution)/shard_map/all_to_all | solution.py:408
  23.5 6.8 %collective-permute-start.2 = (f32[32,256]{1,0:T(8,128)S(1)}, f32[32,256]{1,0:T(8,128)S(1)}, u32[]{:S(2)}, u32[]{:S(2)}) collective-permute-start(f32[32,256]{1,0:T(8,128)S(1)} %get-tuple-element.43), channel_id=1, source_target_pairs={{0,480},{32,64},{64,32},{96,128},{128,96},{160,192},{192,160},{224... | collective-permute-start | bytes 98312 | tf_op jit(solution)/shard_map/ppermute | solution.py:392
  30.3 1.9 %collective-permute-start.3 = (f32[32,256]{1,0:T(8,128)S(1)}, f32[32,256]{1,0:T(8,128)S(1)}, u32[]{:S(2)}, u32[]{:S(2)}) collective-permute-start(f32[32,256]{1,0:T(8,128)S(1)} %get-tuple-element.44), channel_id=1, source_target_pairs={{0,32},{32,0},{64,96},{96,64},{128,160},{160,128},{192,224},{224,1... | collective-permute-start | bytes 98312 | tf_op jit(solution)/shard_map/ppermute | solution.py:393
  32.3 3.0 %collective-permute-done.3.perm_b = f32[32,256]{1,0:T(8,128)S(1)} collective-permute-done((f32[32,256]{1,0:T(8,128)S(1)}, f32[32,256]{1,0:T(8,128)S(1)}, u32[]{:S(2)}, u32[]{:S(2)}) %collective-permute-start.3) | collective-permute-done | bytes 32800 | tf_op jit(solution)/shard_map/ppermute | solution.py:393
  35.3 0.0 all-to-all-done
  35.3 0.8 shard_map.52
  36.1 6.8 %collective-permute-start.4 = (f32[32,256]{1,0:T(8,128)S(1)}, f32[32,256]{1,0:T(8,128)S(1)}, u32[]{:S(2)}, u32[]{:S(2)}) collective-permute-start(f32[32,256]{1,0:T(8,128)S(1)} %get-tuple-element.55), channel_id=1, source_target_pairs={{0,480},{32,64},{64,32},{96,128},{128,96},{160,192},{192,160},{224... | collective-permute-start | bytes 98312 | tf_op jit(solution)/shard_map/ppermute | solution.py:392
  42.9 1.9 %collective-permute-start.5 = (f32[32,256]{1,0:T(8,128)S(1)}, f32[32,256]{1,0:T(8,128)S(1)}, u32[]{:S(2)}, u32[]{:S(2)}) collective-permute-start(f32[32,256]{1,0:T(8,128)S(1)} %get-tuple-element.56), channel_id=1, source_target_pairs={{0,32},{32,0},{64,96},{96,64},{128,160},{160,128},{192,224},{224,1... | collective-permute-start | bytes 98312 | tf_op jit(solution)/shard_map/ppermute | solution.py:393
  44.8 1.2 %collective-permute-start.6 = (f32[8,256]{1,0:T(8,128)S(1)}, f32[8,256]{1,0:T(8,128)S(1)}, u32[]{:S(2)}, u32[]{:S(2)}) collective-permute-start(f32[8,256]{1,0:T(8,128)S(1)} %get-tuple-element.57), channel_id=1, source_target_pairs={{1,0},{2,1},{3,2},{4,3},{5,4},{6,5},{7,6},{8,7},{9,8},{10,9},{11,1... | collective-permute-start | bytes 24584 | tf_op jit(solution)/shard_map/ppermute | solution.py:401
  46.0 0.6 collective-permute-start.7
  46.6 1.3 %collective-permute-done.6.halo_north = f32[8,256]{1,0:T(8,128)S(1)} collective-permute-done((f32[8,256]{1,0:T(8,128)S(1)}, f32[8,256]{1,0:T(8,128)S(1)}, u32[]{:S(2)}, u32[]{:S(2)}) %collective-permute-start.6) | collective-permute-done | bytes 8224 | tf_op jit(solution)/shard_map/ppermute | solution.py:401
  47.9 0.0 collective-permute-done.7.halo_south
  47.9 0.9 shard_map.53
  48.8 3.5 %collective-permute-start.8 = (f32[32,256]{1,0:T(8,128)S(1)}, f32[32,256]{1,0:T(8,128)S(1)}, u32[]{:S(2)}, u32[]{:S(2)}) collective-permute-start(f32[32,256]{1,0:T(8,128)S(1)} %get-tuple-element.71), channel_id=1, source_target_pairs={{0,480},{32,64},{64,32},{96,128},{128,96},{160,192},{192,160},{224... | collective-permute-start | bytes 98312 | tf_op jit(solution)/shard_map/ppermute | solution.py:392
  52.3 1.9 %collective-permute-start.9 = (f32[32,256]{1,0:T(8,128)S(1)}, f32[32,256]{1,0:T(8,128)S(1)}, u32[]{:S(2)}, u32[]{:S(2)}) collective-permute-start(f32[32,256]{1,0:T(8,128)S(1)} %get-tuple-element.72), channel_id=1, source_target_pairs={{0,32},{32,0},{64,96},{96,64},{128,160},{160,128},{192,224},{224,1... | collective-permute-start | bytes 98312 | tf_op jit(solution)/shard_map/ppermute | solution.py:393
  54.2 2.9 %collective-permute-start.10 = (f32[8,256]{1,0:T(8,128)S(1)}, f32[8,256]{1,0:T(8,128)S(1)}, u32[]{:S(2)}, u32[]{:S(2)}) collective-permute-start(f32[8,256]{1,0:T(8,128)S(1)} %get-tuple-element.73), channel_id=1, source_target_pairs={{1,0},{2,1},{3,2},{4,3},{5,4},{6,5},{7,6},{8,7},{9,8},{10,9},{11,1... | collective-permute-start | bytes 24584 | tf_op jit(solution)/shard_map/ppermute | solution.py:401
  57.1 0.0 collective-permute-start.11
  57.1 0.2 shard_map.55.dots
  57.3 1.0 %collective-permute-done.10.halo_north = f32[8,256]{1,0:T(8,128)S(1)} collective-permute-done((f32[8,256]{1,0:T(8,128)S(1)}, f32[8,256]{1,0:T(8,128)S(1)}, u32[]{:S(2)}, u32[]{:S(2)}) %collective-permute-start.10) | collective-permute-done | bytes 8224 | tf_op jit(solution)/shard_map/ppermute | solution.py:401
  58.4 0.4 shard_map.56
  58.8 16.3 %all_to_all.15 = f32[32,1,256]{2,1,0:T(1,128)S(1)} all-to-all(f32[32,1,256]{2,1,0:T(1,128)S(1)} %broadcast_in_dim_broadcast_in_dim.4), channel_id=1, replica_groups=mesh['group'=16,'z'=16,'core'=2] {'group','core'}, dimensions={0} | all-to-all | bytes 65536 | tf_op jit(solution)/shard_map/all_to_all | solution.py:408
  75.3 19.6 %all_to_all.16 = f32[16,1,256]{2,1,0:T(1,128)S(1)} all-to-all(f32[16,1,256]{2,1,0:T(1,128)S(1)} %broadcast_in_dim_broadcast_in_dim.5), channel_id=1, replica_groups=mesh['group'=16,'z'=16,'core'=2] {'z'}, dimensions={0} | all-to-all | bytes 32768 | tf_op jit(solution)/shard_map/all_to_all | solution.py:408
  94.8 1.9 %shard_map.57 = (f32[8,32,256]{2,1,0:T(8,128)}, f32[8,32,256]{2,1,0:T(8,128)}) custom-call(f32[32,128]{1,0:T(8,128)S(1)} %bitcast.29, f32[8,32,256]{2,1,0:T(8,128)S(1)} %get-tuple-element.59.u0_ref, f32[8,32,256]{2,1,0:T(8,128)S(1)} %get-tuple-element.70.field.f1_ref, f32[8,32,256]{2,1,0:T(8,128)S(1)} %get-tuple-element.77.image, ...), custom_call_target="tpu_custom_call" | custom-call | tf_op jit(solution)/shard_map/pallas_call | solution.py:379
  (18 shorter events, 0.1 us)
Async XLA Ops:
  1.5 10.1 %collective-permute-start = (f32[8,256]{1,0:T(8,128)S(1)}, f32[8,256]{1,0:T(8,128)S(1)}, u32[]{:S(2)}, u32[]{:S(2)}) collective-permute-start(f32[8,256]{1,0:T(8,128)S(1)} %bitcast.30), channel_id=1, source_target_pairs={{1,0},{2,1},{3,2},{4,3},{5,4},{6,5},{7,6},{8,7},{9,8},{10,9},{11,1... | collective-permute-start | bytes 24584 | tf_op jit(solution)/shard_map/ppermute | solution.py:401
  8.4 4.2 %collective-permute-start.1 = (f32[8,256]{1,0:T(8,128)S(1)}, f32[8,256]{1,0:T(8,128)S(1)}, u32[]{:S(2)}, u32[]{:S(2)}) collective-permute-start(f32[8,256]{1,0:T(8,128)S(1)} %bitcast.32), channel_id=1, source_target_pairs={{0,1},{1,2},{2,3},{3,4},{4,5},{5,6},{6,7},{7,8},{8,9},{9,10},{10,1... | collective-permute-start | bytes 24584 | tf_op jit(solution)/shard_map/ppermute | solution.py:400
  8.4 1.0 copy-start
  9.4 0.9 copy-start.1
  10.3 0.9 copy-start.2
  13.4 21.9 %all-to-all-start = ((f32[32,1,128]{2,1,0:T(1,128)}), f32[32,1,128]{2,1,0:T(1,128)S(1)}, u32[]{:S(2)}, u32[]{:S(2)}) async-start(f32[32,1,128]{2,1,0:T(1,128)} %bitcast.3), calls=%async_computation | async-start | bytes 32768 | tf_op jit(solution)/shard_map/all_to_all | solution.py:408
  23.5 8.8 %collective-permute-start.2 = (f32[32,256]{1,0:T(8,128)S(1)}, f32[32,256]{1,0:T(8,128)S(1)}, u32[]{:S(2)}, u32[]{:S(2)}) collective-permute-start(f32[32,256]{1,0:T(8,128)S(1)} %get-tuple-element.43), channel_id=1, source_target_pairs={{0,480},{32,64},{64,32},{96,128},{128,96},{160,192},{192,160},{224... | collective-permute-start | bytes 98312 | tf_op jit(solution)/shard_map/ppermute | solution.py:392
  30.3 5.0 %collective-permute-start.3 = (f32[32,256]{1,0:T(8,128)S(1)}, f32[32,256]{1,0:T(8,128)S(1)}, u32[]{:S(2)}, u32[]{:S(2)}) collective-permute-start(f32[32,256]{1,0:T(8,128)S(1)} %get-tuple-element.44), channel_id=1, source_target_pairs={{0,32},{32,0},{64,96},{96,64},{128,160},{160,128},{192,224},{224,1... | collective-permute-start | bytes 98312 | tf_op jit(solution)/shard_map/ppermute | solution.py:393
  36.1 11.8 %collective-permute-start.4 = (f32[32,256]{1,0:T(8,128)S(1)}, f32[32,256]{1,0:T(8,128)S(1)}, u32[]{:S(2)}, u32[]{:S(2)}) collective-permute-start(f32[32,256]{1,0:T(8,128)S(1)} %get-tuple-element.55), channel_id=1, source_target_pairs={{0,480},{32,64},{64,32},{96,128},{128,96},{160,192},{192,160},{224... | collective-permute-start | bytes 98312 | tf_op jit(solution)/shard_map/ppermute | solution.py:392
  42.9 5.0 %collective-permute-start.5 = (f32[32,256]{1,0:T(8,128)S(1)}, f32[32,256]{1,0:T(8,128)S(1)}, u32[]{:S(2)}, u32[]{:S(2)}) collective-permute-start(f32[32,256]{1,0:T(8,128)S(1)} %get-tuple-element.56), channel_id=1, source_target_pairs={{0,32},{32,0},{64,96},{96,64},{128,160},{160,128},{192,224},{224,1... | collective-permute-start | bytes 98312 | tf_op jit(solution)/shard_map/ppermute | solution.py:393
  44.8 3.1 %collective-permute-start.6 = (f32[8,256]{1,0:T(8,128)S(1)}, f32[8,256]{1,0:T(8,128)S(1)}, u32[]{:S(2)}, u32[]{:S(2)}) collective-permute-start(f32[8,256]{1,0:T(8,128)S(1)} %get-tuple-element.57), channel_id=1, source_target_pairs={{1,0},{2,1},{3,2},{4,3},{5,4},{6,5},{7,6},{8,7},{9,8},{10,9},{11,1... | collective-permute-start | bytes 24584 | tf_op jit(solution)/shard_map/ppermute | solution.py:401
  46.0 1.9 %collective-permute-start.7 = (f32[8,256]{1,0:T(8,128)S(1)}, f32[8,256]{1,0:T(8,128)S(1)}, u32[]{:S(2)}, u32[]{:S(2)}) collective-permute-start(f32[8,256]{1,0:T(8,128)S(1)} %get-tuple-element.58), channel_id=1, source_target_pairs={{0,1},{1,2},{2,3},{3,4},{4,5},{5,6},{6,7},{7,8},{8,9},{9,10},{10,1... | collective-permute-start | bytes 24584 | tf_op jit(solution)/shard_map/ppermute | solution.py:400
  48.8 9.5 %collective-permute-start.8 = (f32[32,256]{1,0:T(8,128)S(1)}, f32[32,256]{1,0:T(8,128)S(1)}, u32[]{:S(2)}, u32[]{:S(2)}) collective-permute-start(f32[32,256]{1,0:T(8,128)S(1)} %get-tuple-element.71), channel_id=1, source_target_pairs={{0,480},{32,64},{64,32},{96,128},{128,96},{160,192},{192,160},{224... | collective-permute-start | bytes 98312 | tf_op jit(solution)/shard_map/ppermute | solution.py:392
  52.3 6.1 %collective-permute-start.9 = (f32[32,256]{1,0:T(8,128)S(1)}, f32[32,256]{1,0:T(8,128)S(1)}, u32[]{:S(2)}, u32[]{:S(2)}) collective-permute-start(f32[32,256]{1,0:T(8,128)S(1)} %get-tuple-element.72), channel_id=1, source_target_pairs={{0,32},{32,0},{64,96},{96,64},{128,160},{160,128},{192,224},{224,1... | collective-permute-start | bytes 98312 | tf_op jit(solution)/shard_map/ppermute | solution.py:393
  54.2 4.1 %collective-permute-start.10 = (f32[8,256]{1,0:T(8,128)S(1)}, f32[8,256]{1,0:T(8,128)S(1)}, u32[]{:S(2)}, u32[]{:S(2)}) collective-permute-start(f32[8,256]{1,0:T(8,128)S(1)} %get-tuple-element.73), channel_id=1, source_target_pairs={{1,0},{2,1},{3,2},{4,3},{5,4},{6,5},{7,6},{8,7},{9,8},{10,9},{11,1... | collective-permute-start | bytes 24584 | tf_op jit(solution)/shard_map/ppermute | solution.py:401
  57.1 1.2 %collective-permute-start.11 = (f32[8,256]{1,0:T(8,128)S(1)}, f32[8,256]{1,0:T(8,128)S(1)}, u32[]{:S(2)}, u32[]{:S(2)}) collective-permute-start(f32[8,256]{1,0:T(8,128)S(1)} %get-tuple-element.74), channel_id=1, source_target_pairs={{0,1},{1,2},{2,3},{3,4},{4,5},{5,6},{6,7},{7,8},{8,9},{9,10},{10,1... | collective-permute-start | bytes 24584 | tf_op jit(solution)/shard_map/ppermute | solution.py:400

commit v7 on v6

--- a/solution.py
+++ b/solution.py
@@ -307,7 +307,7 @@
     t = table[...]
     members = t.shape[0]
     lane = lax.broadcasted_iota(jnp.int32, t.shape, 1)
-    mine = (rows_of(t.shape) == my_sub()) & (lane == lax.axis_index("group"))
+    mine = (rows_of(t.shape) == (my_sub() + members // 2) % members) & (lane == lax.axis_index("group"))
 
     def column(at):
         return shift(t, -at * groups, 1)
@@ -402,10 +402,11 @@
     return north, south
 
 
-def gather(row, axis):
+def gather(row, axis, first=0):
     peers = lax.axis_size(axis)
+    order = [[(first + i) % peers for i in range(peers)]] if first else None
     rows = jnp.broadcast_to(row, (peers, row.shape[1]))[:, None]
-    return lax.all_to_all(rows, axis, 0, 0).reshape(peers, row.shape[1])
+    return lax.all_to_all(rows, axis, 0, 0, axis_index_groups=order).reshape(peers, row.shape[1])
 
 
 def shards(source, perm, storage):
@@ -453,9 +454,9 @@
         [wide],
         *halos, f1, dots, storage, *inner, *outer,
     )
-    scalars = gather(scalars, ("group", "core"))
+    scalars = gather(scalars, ("group", "core"), groups * 5 // 8 * cores)
     scalars = sum(scalars[i : i + 1] for i in range(groups * cores))
-    table = gather(scalars, "z").reshape(members, LANES)
+    table = gather(scalars, "z", lax.axis_size("z") // 2).reshape(members, LANES)
     return tuple(
         call(
             functools.partial(last_kernel, steps, groups),

time: 97.3 us -> 87.4 us (0.90)
  blocking collectives: 35.9 us -> 26 us
    all_to_all x2, blocking collectives: 35.9 us -> 26 us  [gather(): lax.all_to_all(rows, axis, 0, 0, axis_index_groups=order)]
where the time goes in v7:
time: 87.4 us; the launch traced here: 86.8 us
  starting transfers between devices  44.4 us (51%)
  blocking collectives  26 us (30%)
  waiting for transfers between devices  6.38 us (7%)
  Pallas kernels  5.44 us (6%)
  local copies, waits for them, and re-layouts  3.78 us (4%)
    all_to_all x2, blocking collectives, gather(): lax.all_to_all(rows, axis, 0, 0, axis_index_groups=order)  26 us
    ppermute x3, starting transfers between devices, over_group(): lax.ppermute(to_a, 'group', [(i, ((i + 1 ^ 1) - 1) % groups) for i in ran...  17 us
    ppermute x3, starting transfers between devices, over_sub(): north = lax.ppermute(to_south, SUB, [(j, i) for i, j in up])  11 us
    all_to_all x1, starting transfers between devices, gather(): lax.all_to_all(rows, axis, 0, 0, axis_index_groups=order)  10.1 us
    ppermute x3, starting transfers between devices, over_group(): b = lax.ppermute(to_b, 'group', [(i, i ^ 1) for i in range(groups)])  5.76 us
    pallas_call x8, Pallas kernels, call(): pl.pallas_call(body, out_shape=[jax.ShapeDtypeStruct(s, jnp.float32) for...  5.44 us
    ppermute x3, waiting for transfers between devices, over_group(): b = lax.ppermute(to_b, 'group', [(i, i ^ 1) for i in range(groups)])  3.02 us
    unnamed x8, local copies, waits for them, and re-layouts  2.85 us
  transfers between devices with their start and end apart: 13, of which 4 were waited for; matrix products, arithmetic and copies ran while one was open for 0% of the time, Pallas kernels for 1%

profile of v7, /device:TPU:1, one launch (start us, length us, event | category | flops | bytes accessed | tf_op | source)
XLA Modules:
  0.0 86.8 jit_solution(1869057196539130027)
XLA Ops:
  0.6 0.9 %fusion = (f32[8,1,256]{2,1,0:T(1,128)S(1)}, f32[8,1,256]{2,1,0:T(1,128)S(1)}) fusion(f32[8,32,256]{2,1,0:T(8,128)} %perm.1), kind=kLoop, calls=%fused_computation.19 | loop fusion | bytes 32768 | tf_op jit(solution)/shard_map/slice | solution.py:418
  1.5 6.9 %collective-permute-start = (f32[8,256]{1,0:T(8,128)S(1)}, f32[8,256]{1,0:T(8,128)S(1)}, u32[]{:S(2)}, u32[]{:S(2)}) collective-permute-start(f32[8,256]{1,0:T(8,128)S(1)} %bitcast.30), channel_id=1, source_target_pairs={{1,0},{2,1},{3,2},{4,3},{5,4},{6,5},{7,6},{8,7},{9,8},{10,9},{11,1... | collective-permute-start | bytes 24584 | tf_op jit(solution)/shard_map/ppermute | solution.py:401
  8.4 0.9 %copy-done = f32[8,32,256]{2,1,0:T(8,128)S(1)} copy-done((f32[8,32,256]{2,1,0:T(8,128)S(1)}, f32[8,32,256]{2,1,0:T(8,128)}, u32[]{:S(2)}) %copy-start) | copy-done | bytes 262168
  9.4 0.9 %copy-done.1 = f32[8,32,256]{2,1,0:T(8,128)S(1)} copy-done((f32[8,32,256]{2,1,0:T(8,128)S(1)}, f32[8,32,256]{2,1,0:T(8,128)}, u32[]{:S(2)}) %copy-start.1) | copy-done | bytes 262168
  10.3 0.9 %copy-done.2 = f32[8,32,256]{2,1,0:T(8,128)S(1)} copy-done((f32[8,32,256]{2,1,0:T(8,128)S(1)}, f32[8,32,256]{2,1,0:T(8,128)}, u32[]{:S(2)}) %copy-start.2) | copy-done | bytes 262168
  11.3 0.4 shard_map.50
  11.6 0.0 collective-permute-done.perm_north
  11.7 1.0 %collective-permute-done.1.perm_south = f32[8,256]{1,0:T(8,128)S(1)} collective-permute-done((f32[8,256]{1,0:T(8,128)S(1)}, f32[8,256]{1,0:T(8,128)S(1)}, u32[]{:S(2)}, u32[]{:S(2)}) %collective-permute-start.1) | collective-permute-done | bytes 8224 | tf_op jit(solution)/shard_map/ppermute | solution.py:400
  12.7 0.7 shard_map.51
  13.4 10.1 %all-to-all-start = ((f32[32,1,128]{2,1,0:T(1,128)}), f32[32,1,128]{2,1,0:T(1,128)S(1)}, u32[]{:S(2)}, u32[]{:S(2)}) async-start(f32[32,1,128]{2,1,0:T(1,128)} %bitcast.3), calls=%async_computation | async-start | bytes 32768 | tf_op jit(solution)/shard_map/all_to_all | solution.py:409
  23.5 6.8 %collective-permute-start.2 = (f32[32,256]{1,0:T(8,128)S(1)}, f32[32,256]{1,0:T(8,128)S(1)}, u32[]{:S(2)}, u32[]{:S(2)}) collective-permute-start(f32[32,256]{1,0:T(8,128)S(1)} %get-tuple-element.43), channel_id=1, source_target_pairs={{0,480},{32,64},{64,32},{96,128},{128,96},{160,192},{192,160},{224... | collective-permute-start | bytes 98312 | tf_op jit(solution)/shard_map/ppermute | solution.py:392
  30.3 1.9 %collective-permute-start.3 = (f32[32,256]{1,0:T(8,128)S(1)}, f32[32,256]{1,0:T(8,128)S(1)}, u32[]{:S(2)}, u32[]{:S(2)}) collective-permute-start(f32[32,256]{1,0:T(8,128)S(1)} %get-tuple-element.44), channel_id=1, source_target_pairs={{0,32},{32,0},{64,96},{96,64},{128,160},{160,128},{192,224},{224,1... | collective-permute-start | bytes 98312 | tf_op jit(solution)/shard_map/ppermute | solution.py:393
  32.3 3.0 %collective-permute-done.3.perm_b = f32[32,256]{1,0:T(8,128)S(1)} collective-permute-done((f32[32,256]{1,0:T(8,128)S(1)}, f32[32,256]{1,0:T(8,128)S(1)}, u32[]{:S(2)}, u32[]{:S(2)}) %collective-permute-start.3) | collective-permute-done | bytes 32800 | tf_op jit(solution)/shard_map/ppermute | solution.py:393
  35.3 0.0 all-to-all-done
  35.3 0.8 shard_map.52
  36.1 6.8 %collective-permute-start.4 = (f32[32,256]{1,0:T(8,128)S(1)}, f32[32,256]{1,0:T(8,128)S(1)}, u32[]{:S(2)}, u32[]{:S(2)}) collective-permute-start(f32[32,256]{1,0:T(8,128)S(1)} %get-tuple-element.55), channel_id=1, source_target_pairs={{0,480},{32,64},{64,32},{96,128},{128,96},{160,192},{192,160},{224... | collective-permute-start | bytes 98312 | tf_op jit(solution)/shard_map/ppermute | solution.py:392
  42.9 1.9 %collective-permute-start.5 = (f32[32,256]{1,0:T(8,128)S(1)}, f32[32,256]{1,0:T(8,128)S(1)}, u32[]{:S(2)}, u32[]{:S(2)}) collective-permute-start(f32[32,256]{1,0:T(8,128)S(1)} %get-tuple-element.56), channel_id=1, source_target_pairs={{0,32},{32,0},{64,96},{96,64},{128,160},{160,128},{192,224},{224,1... | collective-permute-start | bytes 98312 | tf_op jit(solution)/shard_map/ppermute | solution.py:393
  44.8 1.2 %collective-permute-start.6 = (f32[8,256]{1,0:T(8,128)S(1)}, f32[8,256]{1,0:T(8,128)S(1)}, u32[]{:S(2)}, u32[]{:S(2)}) collective-permute-start(f32[8,256]{1,0:T(8,128)S(1)} %get-tuple-element.57), channel_id=1, source_target_pairs={{1,0},{2,1},{3,2},{4,3},{5,4},{6,5},{7,6},{8,7},{9,8},{10,9},{11,1... | collective-permute-start | bytes 24584 | tf_op jit(solution)/shard_map/ppermute | solution.py:401
  46.0 0.6 collective-permute-start.7
  46.6 1.3 %collective-permute-done.6.halo_north = f32[8,256]{1,0:T(8,128)S(1)} collective-permute-done((f32[8,256]{1,0:T(8,128)S(1)}, f32[8,256]{1,0:T(8,128)S(1)}, u32[]{:S(2)}, u32[]{:S(2)}) %collective-permute-start.6) | collective-permute-done | bytes 8224 | tf_op jit(solution)/shard_map/ppermute | solution.py:401
  47.9 0.0 collective-permute-done.7.halo_south
  47.9 0.9 %shard_map.53 = (f32[8,32,256]{2,1,0:T(8,128)S(1)}, f32[8,32,256]{2,1,0:T(8,128)S(1)}, f32[8,256]{1,0:T(8,128)S(1)}, f32[8,256]{1,0:T(8,128)S(1)}) custom-call(f32[32,256]{1,0:T(8,128)S(1)} %collective-permute-done.4.halo_a, f32[32,256]{1,0:T(8,128)S(1)} %collective-permute-done.5.halo_b, f32[8,256]{1,0:T(8,128)S(1)} %collective-permute-done.6.halo_north, ...), custom_call_target="tpu_custom_call" | custom-call | tf_op jit(solution)/shard_map/pallas_call | solution.py:379
  48.8 3.5 %collective-permute-start.8 = (f32[32,256]{1,0:T(8,128)S(1)}, f32[32,256]{1,0:T(8,128)S(1)}, u32[]{:S(2)}, u32[]{:S(2)}) collective-permute-start(f32[32,256]{1,0:T(8,128)S(1)} %get-tuple-element.71), channel_id=1, source_target_pairs={{0,480},{32,64},{64,32},{96,128},{128,96},{160,192},{192,160},{224... | collective-permute-start | bytes 98312 | tf_op jit(solution)/shard_map/ppermute | solution.py:392
  52.3 1.9 %collective-permute-start.9 = (f32[32,256]{1,0:T(8,128)S(1)}, f32[32,256]{1,0:T(8,128)S(1)}, u32[]{:S(2)}, u32[]{:S(2)}) collective-permute-start(f32[32,256]{1,0:T(8,128)S(1)} %get-tuple-element.72), channel_id=1, source_target_pairs={{0,32},{32,0},{64,96},{96,64},{128,160},{160,128},{192,224},{224,1... | collective-permute-start | bytes 98312 | tf_op jit(solution)/shard_map/ppermute | solution.py:393
  54.2 2.9 %collective-permute-start.10 = (f32[8,256]{1,0:T(8,128)S(1)}, f32[8,256]{1,0:T(8,128)S(1)}, u32[]{:S(2)}, u32[]{:S(2)}) collective-permute-start(f32[8,256]{1,0:T(8,128)S(1)} %get-tuple-element.73), channel_id=1, source_target_pairs={{1,0},{2,1},{3,2},{4,3},{5,4},{6,5},{7,6},{8,7},{9,8},{10,9},{11,1... | collective-permute-start | bytes 24584 | tf_op jit(solution)/shard_map/ppermute | solution.py:401
  57.1 0.0 collective-permute-start.11
  57.1 0.2 shard_map.55.dots
  57.3 1.0 %collective-permute-done.10.halo_north = f32[8,256]{1,0:T(8,128)S(1)} collective-permute-done((f32[8,256]{1,0:T(8,128)S(1)}, f32[8,256]{1,0:T(8,128)S(1)}, u32[]{:S(2)}, u32[]{:S(2)}) %collective-permute-start.10) | collective-permute-done | bytes 8224 | tf_op jit(solution)/shard_map/ppermute | solution.py:401
  58.4 0.4 shard_map.56
  58.8 12.7 %all_to_all.15 = f32[32,1,256]{2,1,0:T(1,128)S(1)} all-to-all(f32[32,1,256]{2,1,0:T(1,128)S(1)} %broadcast_in_dim_broadcast_in_dim.4), channel_id=1, replica_groups={{320,321,352,353,384,385,416,417,448,449,480,481,0,1,32,33,64,65,96,97,..., dimensions={0} | all-to-all | bytes 65536 | tf_op jit(solution)/shard_map/all_to_all | solution.py:409
  71.6 13.3 %all_to_all.16 = f32[16,1,256]{2,1,0:T(1,128)S(1)} all-to-all(f32[16,1,256]{2,1,0:T(1,128)S(1)} %broadcast_in_dim_broadcast_in_dim.5), channel_id=1, replica_groups={{16,18,20,22,24,26,28,30,0,2,4,6,8,10,12,14},{17,19,21,23,25,27,29,31,1..., dimensions={0} | all-to-all | bytes 32768 | tf_op jit(solution)/shard_map/all_to_all | solution.py:409
  84.9 1.9 %shard_map.57 = (f32[8,32,256]{2,1,0:T(8,128)}, f32[8,32,256]{2,1,0:T(8,128)}) custom-call(f32[32,128]{1,0:T(8,128)S(1)} %bitcast.29, f32[8,32,256]{2,1,0:T(8,128)S(1)} %get-tuple-element.59.u0_ref, f32[8,32,256]{2,1,0:T(8,128)S(1)} %get-tuple-element.70.field.f1_ref, f32[8,32,256]{2,1,0:T(8,128)S(1)} %get-tuple-element.77.image, ...), custom_call_target="tpu_custom_call" | custom-call | tf_op jit(solution)/shard_map/pallas_call | solution.py:379
  (18 shorter events, 0.1 us)
Async XLA Ops:
  1.5 10.1 %collective-permute-start = (f32[8,256]{1,0:T(8,128)S(1)}, f32[8,256]{1,0:T(8,128)S(1)}, u32[]{:S(2)}, u32[]{:S(2)}) collective-permute-start(f32[8,256]{1,0:T(8,128)S(1)} %bitcast.30), channel_id=1, source_target_pairs={{1,0},{2,1},{3,2},{4,3},{5,4},{6,5},{7,6},{8,7},{9,8},{10,9},{11,1... | collective-permute-start | bytes 24584 | tf_op jit(solution)/shard_map/ppermute | solution.py:401
  8.4 4.2 %collective-permute-start.1 = (f32[8,256]{1,0:T(8,128)S(1)}, f32[8,256]{1,0:T(8,128)S(1)}, u32[]{:S(2)}, u32[]{:S(2)}) collective-permute-start(f32[8,256]{1,0:T(8,128)S(1)} %bitcast.32), channel_id=1, source_target_pairs={{0,1},{1,2},{2,3},{3,4},{4,5},{5,6},{6,7},{7,8},{8,9},{9,10},{10,1... | collective-permute-start | bytes 24584 | tf_op jit(solution)/shard_map/ppermute | solution.py:400
  8.4 1.0 %copy-start = (f32[8,32,256]{2,1,0:T(8,128)S(1)}, f32[8,32,256]{2,1,0:T(8,128)}, u32[]{:S(2)}) copy-start(f32[8,32,256]{2,1,0:T(8,128)} %perm.1) | copy-start | bytes 786436
  9.4 0.9 %copy-start.1 = (f32[8,32,256]{2,1,0:T(8,128)S(1)}, f32[8,32,256]{2,1,0:T(8,128)}, u32[]{:S(2)}) copy-start(f32[8,32,256]{2,1,0:T(8,128)} %source.1) | copy-start | bytes 786436
  10.3 0.9 %copy-start.2 = (f32[8,32,256]{2,1,0:T(8,128)S(1)}, f32[8,32,256]{2,1,0:T(8,128)}, u32[]{:S(2)}) copy-start(f32[8,32,256]{2,1,0:T(8,128)} %storage.1) | copy-start | bytes 786436
  13.4 21.9 %all-to-all-start = ((f32[32,1,128]{2,1,0:T(1,128)}), f32[32,1,128]{2,1,0:T(1,128)S(1)}, u32[]{:S(2)}, u32[]{:S(2)}) async-start(f32[32,1,128]{2,1,0:T(1,128)} %bitcast.3), calls=%async_computation | async-start | bytes 32768 | tf_op jit(solution)/shard_map/all_to_all | solution.py:409
  23.5 8.8 %collective-permute-start.2 = (f32[32,256]{1,0:T(8,128)S(1)}, f32[32,256]{1,0:T(8,128)S(1)}, u32[]{:S(2)}, u32[]{:S(2)}) collective-permute-start(f32[32,256]{1,0:T(8,128)S(1)} %get-tuple-element.43), channel_id=1, source_target_pairs={{0,480},{32,64},{64,32},{96,128},{128,96},{160,192},{192,160},{224... | collective-permute-start | bytes 98312 | tf_op jit(solution)/shard_map/ppermute | solution.py:392
  30.3 5.0 %collective-permute-start.3 = (f32[32,256]{1,0:T(8,128)S(1)}, f32[32,256]{1,0:T(8,128)S(1)}, u32[]{:S(2)}, u32[]{:S(2)}) collective-permute-start(f32[32,256]{1,0:T(8,128)S(1)} %get-tuple-element.44), channel_id=1, source_target_pairs={{0,32},{32,0},{64,96},{96,64},{128,160},{160,128},{192,224},{224,1... | collective-permute-start | bytes 98312 | tf_op jit(solution)/shard_map/ppermute | solution.py:393
  36.1 11.8 %collective-permute-start.4 = (f32[32,256]{1,0:T(8,128)S(1)}, f32[32,256]{1,0:T(8,128)S(1)}, u32[]{:S(2)}, u32[]{:S(2)}) collective-permute-start(f32[32,256]{1,0:T(8,128)S(1)} %get-tuple-element.55), channel_id=1, source_target_pairs={{0,480},{32,64},{64,32},{96,128},{128,96},{160,192},{192,160},{224... | collective-permute-start | bytes 98312 | tf_op jit(solution)/shard_map/ppermute | solution.py:392
  42.9 5.0 %collective-permute-start.5 = (f32[32,256]{1,0:T(8,128)S(1)}, f32[32,256]{1,0:T(8,128)S(1)}, u32[]{:S(2)}, u32[]{:S(2)}) collective-permute-start(f32[32,256]{1,0:T(8,128)S(1)} %get-tuple-element.56), channel_id=1, source_target_pairs={{0,32},{32,0},{64,96},{96,64},{128,160},{160,128},{192,224},{224,1... | collective-permute-start | bytes 98312 | tf_op jit(solution)/shard_map/ppermute | solution.py:393
  44.8 3.1 %collective-permute-start.6 = (f32[8,256]{1,0:T(8,128)S(1)}, f32[8,256]{1,0:T(8,128)S(1)}, u32[]{:S(2)}, u32[]{:S(2)}) collective-permute-start(f32[8,256]{1,0:T(8,128)S(1)} %get-tuple-element.57), channel_id=1, source_target_pairs={{1,0},{2,1},{3,2},{4,3},{5,4},{6,5},{7,6},{8,7},{9,8},{10,9},{11,1... | collective-permute-start | bytes 24584 | tf_op jit(solution)/shard_map/ppermute | solution.py:401
  46.0 1.9 %collective-permute-start.7 = (f32[8,256]{1,0:T(8,128)S(1)}, f32[8,256]{1,0:T(8,128)S(1)}, u32[]{:S(2)}, u32[]{:S(2)}) collective-permute-start(f32[8,256]{1,0:T(8,128)S(1)} %get-tuple-element.58), channel_id=1, source_target_pairs={{0,1},{1,2},{2,3},{3,4},{4,5},{5,6},{6,7},{7,8},{8,9},{9,10},{10,1... | collective-permute-start | bytes 24584 | tf_op jit(solution)/shard_map/ppermute | solution.py:400
  48.8 9.5 %collective-permute-start.8 = (f32[32,256]{1,0:T(8,128)S(1)}, f32[32,256]{1,0:T(8,128)S(1)}, u32[]{:S(2)}, u32[]{:S(2)}) collective-permute-start(f32[32,256]{1,0:T(8,128)S(1)} %get-tuple-element.71), channel_id=1, source_target_pairs={{0,480},{32,64},{64,32},{96,128},{128,96},{160,192},{192,160},{224... | collective-permute-start | bytes 98312 | tf_op jit(solution)/shard_map/ppermute | solution.py:392
  52.3 6.1 %collective-permute-start.9 = (f32[32,256]{1,0:T(8,128)S(1)}, f32[32,256]{1,0:T(8,128)S(1)}, u32[]{:S(2)}, u32[]{:S(2)}) collective-permute-start(f32[32,256]{1,0:T(8,128)S(1)} %get-tuple-element.72), channel_id=1, source_target_pairs={{0,32},{32,0},{64,96},{96,64},{128,160},{160,128},{192,224},{224,1... | collective-permute-start | bytes 98312 | tf_op jit(solution)/shard_map/ppermute | solution.py:393
  54.2 4.1 %collective-permute-start.10 = (f32[8,256]{1,0:T(8,128)S(1)}, f32[8,256]{1,0:T(8,128)S(1)}, u32[]{:S(2)}, u32[]{:S(2)}) collective-permute-start(f32[8,256]{1,0:T(8,128)S(1)} %get-tuple-element.73), channel_id=1, source_target_pairs={{1,0},{2,1},{3,2},{4,3},{5,4},{6,5},{7,6},{8,7},{9,8},{10,9},{11,1... | collective-permute-start | bytes 24584 | tf_op jit(solution)/shard_map/ppermute | solution.py:401
  57.1 1.2 %collective-permute-start.11 = (f32[8,256]{1,0:T(8,128)S(1)}, f32[8,256]{1,0:T(8,128)S(1)}, u32[]{:S(2)}, u32[]{:S(2)}) collective-permute-start(f32[8,256]{1,0:T(8,128)S(1)} %get-tuple-element.74), channel_id=1, source_target_pairs={{0,1},{1,2},{2,3},{3,4},{4,5},{5,6},{6,7},{7,8},{8,9},{9,10},{10,1... | collective-permute-start | bytes 24584 | tf_op jit(solution)/shard_map/ppermute | solution.py:400

commit v8 on v7

--- a/solution.py
+++ b/solution.py
@@ -101,6 +101,12 @@
     lax.fori_loop(0, cx, slab, 0, unroll=UNROLL)
     out[0] = out[0] + edge_west[...] * (padded[1] - padded[0])
     out[cx - 1] = out[cx - 1] + edge_east[...] * (padded[cx] - padded[cx + 1])
+
+
+def strips_kernel(field, to_north, to_south):
+    for x in range(field.shape[0]):
+        to_north[x : x + 1] = field[x, field.shape[1] - 1 :]
+        to_south[x : x + 1] = field[x, 0:1]
 
 
 def inner_kernel(
@@ -215,7 +221,7 @@
     factors, last = reduce_rows(t / members, shift(t, -1, 1) * members, steps)
     c0 = solve_rows(factors, last, shift(t, -2, 1))
     lane = lax.broadcasted_iota(jnp.int32, t.shape, 1)
-    c0 = total_of(jnp.where((rows_of(t.shape) == my_sub()) & (lane == 0), c0, 0.0))
+    c0 = total_of(jnp.where((rows_of(t.shape) == (my_sub() + members - 28) % members) & (lane == 0), c0, 0.0))
     for x in range(cx):
         u = work[1, x + 1] + c0
         u0_ref[x] = u
@@ -307,7 +313,7 @@
     t = table[...]
     members = t.shape[0]
     lane = lax.broadcasted_iota(jnp.int32, t.shape, 1)
-    mine = (rows_of(t.shape) == (my_sub() + members // 2) % members) & (lane == lax.axis_index("group"))
+    mine = (rows_of(t.shape) == (my_sub() + members - 14) % members) & (lane == lax.axis_index("group"))
 
     def column(at):
         return shift(t, -at * groups, 1)
@@ -415,7 +421,7 @@
     steps = members.bit_length() - 1
     full, wide, layer, edge, row = (cx, cy, cz), (cx + 2, cy, cz), (cy, cz), (cx, cz), (1, LANES)
     rounds = [full, (2,) + wide]
-    strip_north, strip_south = perm[:, -1], perm[:, 0]
+    strip_north, strip_south = call(strips_kernel, [edge, edge], [], perm)
     halos = over_sub(strip_north, strip_south)
     source, storage, west, east, *inner, diagonal, sums = call(
         inner_kernel,
@@ -429,7 +435,7 @@
         [],
         *halos, strip_north, strip_south, west, east, sums,
     )
-    table = gather(scalars, SUB)
+    table = gather(scalars, SUB, 28)
     edge_east, edge_west, *weights, u0, to_a, to_b, to_north, to_south = call(
         functools.partial(assemble_kernel, steps),
         [layer, layer] + [full] * 8 + [layer, layer, edge, edge],
@@ -456,7 +462,7 @@
     )
     scalars = gather(scalars, ("group", "core"), groups * 5 // 8 * cores)
     scalars = sum(scalars[i : i + 1] for i in range(groups * cores))
-    table = gather(scalars, "z", lax.axis_size("z") // 2).reshape(members, LANES)
+    table = gather(scalars, "z", 7).reshape(members, LANES)
     return tuple(
         call(
             functools.partial(last_kernel, steps, groups),

time: 87.4 us -> 86.2 us (0.986)
  waiting for transfers between devices: 6.38 us -> 8.62 us
  local copies, waits for them, and re-layouts: 3.78 us -> 1.93 us
  blocking collectives: 26 us -> 24.9 us
    ppermute x3, waiting for transfers between devices: 1 us -> 2.89 us  [over_sub(): south = lax.ppermute(to_north, SUB, up)]
    ppermute x3, starting transfers between devices: 0.56 us -> 1.74 us  [over_sub(): south = lax.ppermute(to_north, SUB, up)]
    all_to_all x2, blocking collectives: 26 us -> 24.9 us  [gather(): lax.all_to_all(rows, axis, 0, 0, axis_index_groups=order)]
    unnamed x8 -> x6, local copies, waits for them, and re-layouts: 2.85 us -> 1.9 us
    ppermute x3, starting transfers between devices: 17 us -> 16.1 us  [over_group(): lax.ppermute(to_a, 'group', [(i, ((i + 1 ^ 1) - 1) % groups) for i in ran...]
    slice x1 -> x0, local copies, waits for them, and re-layouts: 0.89 us -> none  [shards(): strip_north, strip_south = (perm[:, -1], perm[:, 0])]
    pallas_call x8 -> x9, Pallas kernels: 5.44 us -> 5.45 us  [call(): pl.pallas_call(body, out_shape=[jax.ShapeDtypeStruct(s, jnp.float32) for...]
where the time goes in v8:
time: 86.2 us; the launch traced here: 85.7 us
  starting transfers between devices  44 us (51%)
  blocking collectives  24.9 us (29%)
  waiting for transfers between devices  8.62 us (10%)
  Pallas kernels  5.45 us (6%)
  local copies, waits for them, and re-layouts  1.93 us (2%)
    all_to_all x2, blocking collectives, gather(): lax.all_to_all(rows, axis, 0, 0, axis_index_groups=order)  24.9 us
    ppermute x3, starting transfers between devices, over_group(): lax.ppermute(to_a, 'group', [(i, ((i + 1 ^ 1) - 1) % groups) for i in ran...  16.1 us
    ppermute x3, starting transfers between devices, over_sub(): north = lax.ppermute(to_south, SUB, [(j, i) for i, j in up])  10.2 us
    all_to_all x1, starting transfers between devices, gather(): lax.all_to_all(rows, axis, 0, 0, axis_index_groups=order)  10.2 us
    ppermute x3, starting transfers between devices, over_group(): b = lax.ppermute(to_b, 'group', [(i, i ^ 1) for i in range(groups)])  5.76 us
    pallas_call x9, Pallas kernels, call(): pl.pallas_call(body, out_shape=[jax.ShapeDtypeStruct(s, jnp.float32) for...  5.45 us
    ppermute x3, waiting for transfers between devices, over_sub(): north = lax.ppermute(to_south, SUB, [(j, i) for i, j in up])  2.99 us
    ppermute x3, waiting for transfers between devices, over_sub(): south = lax.ppermute(to_north, SUB, up)  2.89 us
  transfers between devices with their start and end apart: 13, of which 4 were waited for; matrix products, arithmetic and copies ran while one was open for 0% of the time, Pallas kernels for 1%

profile of v8, /device:TPU:1, one launch (start us, length us, event | category | flops | bytes accessed | tf_op | source)
XLA Modules:
  0.0 85.7 jit_solution(14089834156382117777)
XLA Ops:
  0.6 0.9 %copy-done = f32[8,32,256]{2,1,0:T(8,128)S(1)} copy-done((f32[8,32,256]{2,1,0:T(8,128)S(1)}, f32[8,32,256]{2,1,0:T(8,128)}, u32[]{:S(2)}) %copy-start) | copy-done | bytes 262168
  1.6 6.9 %collective-permute-start = (f32[8,256]{1,0:T(8,128)S(1)}, f32[8,256]{1,0:T(8,128)S(1)}, u32[]{:S(2)}, u32[]{:S(2)}) collective-permute-start(f32[8,256]{1,0:T(8,128)S(1)} %get-tuple-element.42.strip_south), channel_id=1, source_target_pairs={{1,0},{2,1},{3,2},{4,3},{5,4},{6,5},{7,6},{8,7},{9,8},{10,9},{11,1... | collective-permute-start | bytes 24584 | tf_op jit(solution)/shard_map/ppermute | solution.py:407
  8.5 0.0 collective-permute-start.1
  8.5 0.9 %copy-done.2 = f32[8,32,256]{2,1,0:T(8,128)S(1)} copy-done((f32[8,32,256]{2,1,0:T(8,128)S(1)}, f32[8,32,256]{2,1,0:T(8,128)}, u32[]{:S(2)}) %copy-start.2) | copy-done | bytes 262168
  9.4 0.4 shard_map.51
  9.8 0.0 collective-permute-done.perm_north
  9.8 2.9 %collective-permute-done.1.perm_south = f32[8,256]{1,0:T(8,128)S(1)} collective-permute-done((f32[8,256]{1,0:T(8,128)S(1)}, f32[8,256]{1,0:T(8,128)S(1)}, u32[]{:S(2)}, u32[]{:S(2)}) %collective-permute-start.1) | collective-permute-done | bytes 8224 | tf_op jit(solution)/shard_map/ppermute | solution.py:406
  12.7 0.7 shard_map.52
  13.4 10.2 %all-to-all-start = ((f32[32,1,128]{2,1,0:T(1,128)}), f32[32,1,128]{2,1,0:T(1,128)S(1)}, u32[]{:S(2)}, u32[]{:S(2)}) async-start(f32[32,1,128]{2,1,0:T(1,128)} %bitcast.1), calls=%async_computation | async-start | bytes 32768 | tf_op jit(solution)/shard_map/all_to_all | solution.py:415
  23.6 6.8 %collective-permute-start.2 = (f32[32,256]{1,0:T(8,128)S(1)}, f32[32,256]{1,0:T(8,128)S(1)}, u32[]{:S(2)}, u32[]{:S(2)}) collective-permute-start(f32[32,256]{1,0:T(8,128)S(1)} %get-tuple-element.47), channel_id=1, source_target_pairs={{0,480},{32,64},{64,32},{96,128},{128,96},{160,192},{192,160},{224... | collective-permute-start | bytes 98312 | tf_op jit(solution)/shard_map/ppermute | solution.py:398
  30.5 1.9 %collective-permute-start.3 = (f32[32,256]{1,0:T(8,128)S(1)}, f32[32,256]{1,0:T(8,128)S(1)}, u32[]{:S(2)}, u32[]{:S(2)}) collective-permute-start(f32[32,256]{1,0:T(8,128)S(1)} %get-tuple-element.48), channel_id=1, source_target_pairs={{0,32},{32,0},{64,96},{96,64},{128,160},{160,128},{192,224},{224,1... | collective-permute-start | bytes 98312 | tf_op jit(solution)/shard_map/ppermute | solution.py:399
  32.4 0.0 collective-permute-done.2.perm_a
  32.4 2.7 %collective-permute-done.3.perm_b = f32[32,256]{1,0:T(8,128)S(1)} collective-permute-done((f32[32,256]{1,0:T(8,128)S(1)}, f32[32,256]{1,0:T(8,128)S(1)}, u32[]{:S(2)}, u32[]{:S(2)}) %collective-permute-start.3) | collective-permute-done | bytes 32800 | tf_op jit(solution)/shard_map/ppermute | solution.py:399
  35.1 0.8 shard_map.53
  36.0 4.0 %collective-permute-start.4 = (f32[32,256]{1,0:T(8,128)S(1)}, f32[32,256]{1,0:T(8,128)S(1)}, u32[]{:S(2)}, u32[]{:S(2)}) collective-permute-start(f32[32,256]{1,0:T(8,128)S(1)} %get-tuple-element.59), channel_id=1, source_target_pairs={{0,480},{32,64},{64,32},{96,128},{128,96},{160,192},{192,160},{224... | collective-permute-start | bytes 98312 | tf_op jit(solution)/shard_map/ppermute | solution.py:398
  40.0 1.9 %collective-permute-start.5 = (f32[32,256]{1,0:T(8,128)S(1)}, f32[32,256]{1,0:T(8,128)S(1)}, u32[]{:S(2)}, u32[]{:S(2)}) collective-permute-start(f32[32,256]{1,0:T(8,128)S(1)} %get-tuple-element.60), channel_id=1, source_target_pairs={{0,32},{32,0},{64,96},{96,64},{128,160},{160,128},{192,224},{224,1... | collective-permute-start | bytes 98312 | tf_op jit(solution)/shard_map/ppermute | solution.py:399
  41.9 1.1 %collective-permute-start.6 = (f32[8,256]{1,0:T(8,128)S(1)}, f32[8,256]{1,0:T(8,128)S(1)}, u32[]{:S(2)}, u32[]{:S(2)}) collective-permute-start(f32[8,256]{1,0:T(8,128)S(1)} %get-tuple-element.61), channel_id=1, source_target_pairs={{1,0},{2,1},{3,2},{4,3},{5,4},{6,5},{7,6},{8,7},{9,8},{10,9},{11,1... | collective-permute-start | bytes 24584 | tf_op jit(solution)/shard_map/ppermute | solution.py:407
  43.0 1.1 %collective-permute-start.7 = (f32[8,256]{1,0:T(8,128)S(1)}, f32[8,256]{1,0:T(8,128)S(1)}, u32[]{:S(2)}, u32[]{:S(2)}) collective-permute-start(f32[8,256]{1,0:T(8,128)S(1)} %get-tuple-element.62), channel_id=1, source_target_pairs={{0,1},{1,2},{2,3},{3,4},{4,5},{5,6},{6,7},{7,8},{8,9},{9,10},{10,1... | collective-permute-start | bytes 24584 | tf_op jit(solution)/shard_map/ppermute | solution.py:406
  44.1 1.6 %collective-permute-done.6.halo_north = f32[8,256]{1,0:T(8,128)S(1)} collective-permute-done((f32[8,256]{1,0:T(8,128)S(1)}, f32[8,256]{1,0:T(8,128)S(1)}, u32[]{:S(2)}, u32[]{:S(2)}) %collective-permute-start.6) | collective-permute-done | bytes 8224 | tf_op jit(solution)/shard_map/ppermute | solution.py:407
  45.7 0.9 %shard_map.54 = (f32[8,32,256]{2,1,0:T(8,128)S(1)}, f32[8,32,256]{2,1,0:T(8,128)S(1)}, f32[8,256]{1,0:T(8,128)S(1)}, f32[8,256]{1,0:T(8,128)S(1)}) custom-call(f32[32,256]{1,0:T(8,128)S(1)} %collective-permute-done.4.halo_a, f32[32,256]{1,0:T(8,128)S(1)} %collective-permute-done.5.halo_b, f32[8,256]{1,0:T(8,128)S(1)} %collective-permute-done.6.halo_north, ...), custom_call_target="tpu_custom_call" | custom-call | tf_op jit(solution)/shard_map/pallas_call | solution.py:385
  46.7 5.3 %collective-permute-start.8 = (f32[32,256]{1,0:T(8,128)S(1)}, f32[32,256]{1,0:T(8,128)S(1)}, u32[]{:S(2)}, u32[]{:S(2)}) collective-permute-start(f32[32,256]{1,0:T(8,128)S(1)} %get-tuple-element.75), channel_id=1, source_target_pairs={{0,480},{32,64},{64,32},{96,128},{128,96},{160,192},{192,160},{224... | collective-permute-start | bytes 98312 | tf_op jit(solution)/shard_map/ppermute | solution.py:398
  51.9 1.9 %collective-permute-start.9 = (f32[32,256]{1,0:T(8,128)S(1)}, f32[32,256]{1,0:T(8,128)S(1)}, u32[]{:S(2)}, u32[]{:S(2)}) collective-permute-start(f32[32,256]{1,0:T(8,128)S(1)} %get-tuple-element.76), channel_id=1, source_target_pairs={{0,32},{32,0},{64,96},{96,64},{128,160},{160,128},{192,224},{224,1... | collective-permute-start | bytes 98312 | tf_op jit(solution)/shard_map/ppermute | solution.py:399
  53.9 2.2 %collective-permute-start.10 = (f32[8,256]{1,0:T(8,128)S(1)}, f32[8,256]{1,0:T(8,128)S(1)}, u32[]{:S(2)}, u32[]{:S(2)}) collective-permute-start(f32[8,256]{1,0:T(8,128)S(1)} %get-tuple-element.77), channel_id=1, source_target_pairs={{1,0},{2,1},{3,2},{4,3},{5,4},{6,5},{7,6},{8,7},{9,8},{10,9},{11,1... | collective-permute-start | bytes 24584 | tf_op jit(solution)/shard_map/ppermute | solution.py:407
  56.1 0.6 collective-permute-start.11
  56.7 0.2 shard_map.56.dots
  56.9 1.4 %collective-permute-done.10.halo_north = f32[8,256]{1,0:T(8,128)S(1)} collective-permute-done((f32[8,256]{1,0:T(8,128)S(1)}, f32[8,256]{1,0:T(8,128)S(1)}, u32[]{:S(2)}, u32[]{:S(2)}) %collective-permute-start.10) | collective-permute-done | bytes 8224 | tf_op jit(solution)/shard_map/ppermute | solution.py:407
  58.3 0.0 collective-permute-done.8.halo_a
  58.3 0.0 collective-permute-done.9.halo_b
  58.3 0.4 shard_map.57
  58.8 11.7 %all_to_all.15 = f32[32,1,256]{2,1,0:T(1,128)S(1)} all-to-all(f32[32,1,256]{2,1,0:T(1,128)S(1)} %broadcast_in_dim_broadcast_in_dim.4), channel_id=1, replica_groups={{320,321,352,353,384,385,416,417,448,449,480,481,0,1,32,33,64,65,96,97,..., dimensions={0} | all-to-all | bytes 65536 | tf_op jit(solution)/shard_map/all_to_all | solution.py:415
  70.5 13.2 %all_to_all.16 = f32[16,1,256]{2,1,0:T(1,128)S(1)} all-to-all(f32[16,1,256]{2,1,0:T(1,128)S(1)} %broadcast_in_dim_broadcast_in_dim.5), channel_id=1, replica_groups={{14,16,18,20,22,24,26,28,30,0,2,4,6,8,10,12},{15,17,19,21,23,25,27,29,3..., dimensions={0} | all-to-all | bytes 32768 | tf_op jit(solution)/shard_map/all_to_all | solution.py:415
  83.8 1.9 %shard_map.58 = (f32[8,32,256]{2,1,0:T(8,128)}, f32[8,32,256]{2,1,0:T(8,128)}) custom-call(f32[32,128]{1,0:T(8,128)S(1)} %bitcast.23, f32[8,32,256]{2,1,0:T(8,128)S(1)} %get-tuple-element.63.u0_ref, f32[8,32,256]{2,1,0:T(8,128)S(1)} %get-tuple-element.74.field.f1_ref, f32[8,32,256]{2,1,0:T(8,128)S(1)} %get-tuple-element.81.image, ...), custom_call_target="tpu_custom_call" | custom-call | tf_op jit(solution)/shard_map/pallas_call | solution.py:385
  (16 shorter events, 0.1 us)
Async XLA Ops:
  0.6 1.0 %copy-start = (f32[8,32,256]{2,1,0:T(8,128)S(1)}, f32[8,32,256]{2,1,0:T(8,128)}, u32[]{:S(2)}) copy-start(f32[8,32,256]{2,1,0:T(8,128)} %perm.1) | copy-start | bytes 786436
  1.6 6.9 %copy-start.1 = (f32[8,32,256]{2,1,0:T(8,128)S(1)}, f32[8,32,256]{2,1,0:T(8,128)}, u32[]{:S(2)}) copy-start(f32[8,32,256]{2,1,0:T(8,128)} %source.1) | copy-start | bytes 786436
  1.6 8.2 %collective-permute-start = (f32[8,256]{1,0:T(8,128)S(1)}, f32[8,256]{1,0:T(8,128)S(1)}, u32[]{:S(2)}, u32[]{:S(2)}) collective-permute-start(f32[8,256]{1,0:T(8,128)S(1)} %get-tuple-element.42.strip_south), channel_id=1, source_target_pairs={{1,0},{2,1},{3,2},{4,3},{5,4},{6,5},{7,6},{8,7},{9,8},{10,9},{11,1... | collective-permute-start | bytes 24584 | tf_op jit(solution)/shard_map/ppermute | solution.py:407
  8.5 4.2 %collective-permute-start.1 = (f32[8,256]{1,0:T(8,128)S(1)}, f32[8,256]{1,0:T(8,128)S(1)}, u32[]{:S(2)}, u32[]{:S(2)}) collective-permute-start(f32[8,256]{1,0:T(8,128)S(1)} %get-tuple-element.43.strip_north), channel_id=1, source_target_pairs={{0,1},{1,2},{2,3},{3,4},{4,5},{5,6},{6,7},{7,8},{8,9},{9,10},{10,1... | collective-permute-start | bytes 24584 | tf_op jit(solution)/shard_map/ppermute | solution.py:406
  8.5 1.0 %copy-start.2 = (f32[8,32,256]{2,1,0:T(8,128)S(1)}, f32[8,32,256]{2,1,0:T(8,128)}, u32[]{:S(2)}) copy-start(f32[8,32,256]{2,1,0:T(8,128)} %storage.1) | copy-start | bytes 786436
  13.4 21.7 %all-to-all-start = ((f32[32,1,128]{2,1,0:T(1,128)}), f32[32,1,128]{2,1,0:T(1,128)S(1)}, u32[]{:S(2)}, u32[]{:S(2)}) async-start(f32[32,1,128]{2,1,0:T(1,128)} %bitcast.1), calls=%async_computation | async-start | bytes 32768 | tf_op jit(solution)/shard_map/all_to_all | solution.py:415
  23.6 8.8 %collective-permute-start.2 = (f32[32,256]{1,0:T(8,128)S(1)}, f32[32,256]{1,0:T(8,128)S(1)}, u32[]{:S(2)}, u32[]{:S(2)}) collective-permute-start(f32[32,256]{1,0:T(8,128)S(1)} %get-tuple-element.47), channel_id=1, source_target_pairs={{0,480},{32,64},{64,32},{96,128},{128,96},{160,192},{192,160},{224... | collective-permute-start | bytes 98312 | tf_op jit(solution)/shard_map/ppermute | solution.py:398
  30.5 4.7 %collective-permute-start.3 = (f32[32,256]{1,0:T(8,128)S(1)}, f32[32,256]{1,0:T(8,128)S(1)}, u32[]{:S(2)}, u32[]{:S(2)}) collective-permute-start(f32[32,256]{1,0:T(8,128)S(1)} %get-tuple-element.48), channel_id=1, source_target_pairs={{0,32},{32,0},{64,96},{96,64},{128,160},{160,128},{192,224},{224,1... | collective-permute-start | bytes 98312 | tf_op jit(solution)/shard_map/ppermute | solution.py:399
  36.0 9.8 %collective-permute-start.4 = (f32[32,256]{1,0:T(8,128)S(1)}, f32[32,256]{1,0:T(8,128)S(1)}, u32[]{:S(2)}, u32[]{:S(2)}) collective-permute-start(f32[32,256]{1,0:T(8,128)S(1)} %get-tuple-element.59), channel_id=1, source_target_pairs={{0,480},{32,64},{64,32},{96,128},{128,96},{160,192},{192,160},{224... | collective-permute-start | bytes 98312 | tf_op jit(solution)/shard_map/ppermute | solution.py:398
  40.0 5.8 %collective-permute-start.5 = (f32[32,256]{1,0:T(8,128)S(1)}, f32[32,256]{1,0:T(8,128)S(1)}, u32[]{:S(2)}, u32[]{:S(2)}) collective-permute-start(f32[32,256]{1,0:T(8,128)S(1)} %get-tuple-element.60), channel_id=1, source_target_pairs={{0,32},{32,0},{64,96},{96,64},{128,160},{160,128},{192,224},{224,1... | collective-permute-start | bytes 98312 | tf_op jit(solution)/shard_map/ppermute | solution.py:399
  41.9 3.8 %collective-permute-start.6 = (f32[8,256]{1,0:T(8,128)S(1)}, f32[8,256]{1,0:T(8,128)S(1)}, u32[]{:S(2)}, u32[]{:S(2)}) collective-permute-start(f32[8,256]{1,0:T(8,128)S(1)} %get-tuple-element.61), channel_id=1, source_target_pairs={{1,0},{2,1},{3,2},{4,3},{5,4},{6,5},{7,6},{8,7},{9,8},{10,9},{11,1... | collective-permute-start | bytes 24584 | tf_op jit(solution)/shard_map/ppermute | solution.py:407
  43.0 2.7 %collective-permute-start.7 = (f32[8,256]{1,0:T(8,128)S(1)}, f32[8,256]{1,0:T(8,128)S(1)}, u32[]{:S(2)}, u32[]{:S(2)}) collective-permute-start(f32[8,256]{1,0:T(8,128)S(1)} %get-tuple-element.62), channel_id=1, source_target_pairs={{0,1},{1,2},{2,3},{3,4},{4,5},{5,6},{6,7},{7,8},{8,9},{9,10},{10,1... | collective-permute-start | bytes 24584 | tf_op jit(solution)/shard_map/ppermute | solution.py:406
  46.7 11.6 %collective-permute-start.8 = (f32[32,256]{1,0:T(8,128)S(1)}, f32[32,256]{1,0:T(8,128)S(1)}, u32[]{:S(2)}, u32[]{:S(2)}) collective-permute-start(f32[32,256]{1,0:T(8,128)S(1)} %get-tuple-element.75), channel_id=1, source_target_pairs={{0,480},{32,64},{64,32},{96,128},{128,96},{160,192},{192,160},{224... | collective-permute-start | bytes 98312 | tf_op jit(solution)/shard_map/ppermute | solution.py:398
  51.9 6.4 %collective-permute-start.9 = (f32[32,256]{1,0:T(8,128)S(1)}, f32[32,256]{1,0:T(8,128)S(1)}, u32[]{:S(2)}, u32[]{:S(2)}) collective-permute-start(f32[32,256]{1,0:T(8,128)S(1)} %get-tuple-element.76), channel_id=1, source_target_pairs={{0,32},{32,0},{64,96},{96,64},{128,160},{160,128},{192,224},{224,1... | collective-permute-start | bytes 98312 | tf_op jit(solution)/shard_map/ppermute | solution.py:399
  53.9 4.4 %collective-permute-start.10 = (f32[8,256]{1,0:T(8,128)S(1)}, f32[8,256]{1,0:T(8,128)S(1)}, u32[]{:S(2)}, u32[]{:S(2)}) collective-permute-start(f32[8,256]{1,0:T(8,128)S(1)} %get-tuple-element.77), channel_id=1, source_target_pairs={{1,0},{2,1},{3,2},{4,3},{5,4},{6,5},{7,6},{8,7},{9,8},{10,9},{11,1... | collective-permute-start | bytes 24584 | tf_op jit(solution)/shard_map/ppermute | solution.py:407
  56.1 2.2 %collective-permute-start.11 = (f32[8,256]{1,0:T(8,128)S(1)}, f32[8,256]{1,0:T(8,128)S(1)}, u32[]{:S(2)}, u32[]{:S(2)}) collective-permute-start(f32[8,256]{1,0:T(8,128)S(1)} %get-tuple-element.78), channel_id=1, source_target_pairs={{0,1},{1,2},{2,3},{3,4},{4,5},{5,6},{6,7},{7,8},{8,9},{9,10},{10,1... | collective-permute-start | bytes 24584 | tf_op jit(solution)/shard_map/ppermute | solution.py:406

commit v9 on v8

--- a/solution.py
+++ b/solution.py
@@ -12,6 +12,7 @@
 VMEM = 16 * 2**20
 UNROLL = True
 SUB = ("z", "core")
+LEAD_COARSE, LEAD_GROUP, LEAD_LAST = 28, 10, 7
 AGAINST, IMAGE, STORED, COUPLING, EAST = range(5)
 DOTS = 120
 
@@ -142,12 +143,9 @@
     sums[...] = placed(((0, total_of(stored)), (2, total_of(total_r))))
 
 
-def edge_kernel(
-    perm_north, perm_south, strip_north, strip_south, west, east, sums, edge_north, edge_south, to_a, to_b, out
-):
+def edge_kernel(perm_north, strip_north, west, east, sums, edge_north, to_a, to_b, out):
     north = harmonic(strip_north[...], perm_north[...])
     edge_north[...] = north
-    edge_south[...] = harmonic(perm_south[...], strip_south[...])
     out[...] = jnp.broadcast_to(sums[...] + placed(((1, total_of(north)),)), out.shape)
     by_side(west[...], east[...], to_a, to_b)
 
@@ -185,8 +183,8 @@
 
 def assemble_kernel(
     steps, perm_a, perm_b, table, source, perm_west, perm_east,
-    east_in, north_in, south_in, upper_t, lower_t, diagonal, edge_north, edge_south,
-    edge_east, edge_west, scale, w_east, w_west, w_north, w_south, w_upper, w_lower,
+    east_in, north_in, south_in, upper_t, lower_t, diagonal, edge_north, perm_south, strip_south,
+    edge_east, edge_west, edge_south, scale, w_east, w_west, w_north, w_south, w_upper, w_lower,
     u0_ref, to_a, to_b, to_north, to_south, first, work,
 ):
     cx, cy, cz = source.shape
@@ -195,6 +193,7 @@
     a, b = perm_a[...], perm_b[...]
     edge_east[...] = harmonic(perm_east[...], jnp.where(odd, a, b))
     edge_west[...] = harmonic(jnp.where(odd, b, a), perm_west[...])
+    edge_south[...] = harmonic(perm_south[...], strip_south[...])
     for x in range(cx):
         d = diagonal[x]
         d = d + jnp.where(row == cy - 1, edge_north[x : x + 1], jnp.where(row == 0, edge_south[x : x + 1], 0.0))
@@ -221,7 +220,7 @@
     factors, last = reduce_rows(t / members, shift(t, -1, 1) * members, steps)
     c0 = solve_rows(factors, last, shift(t, -2, 1))
     lane = lax.broadcasted_iota(jnp.int32, t.shape, 1)
-    c0 = total_of(jnp.where((rows_of(t.shape) == (my_sub() + members - 28) % members) & (lane == 0), c0, 0.0))
+    c0 = total_of(jnp.where((rows_of(t.shape) == (my_sub() + members - LEAD_COARSE) % members) & (lane == 0), c0, 0.0))
     for x in range(cx):
         u = work[1, x + 1] + c0
         u0_ref[x] = u
@@ -313,7 +312,7 @@
     t = table[...]
     members = t.shape[0]
     lane = lax.broadcasted_iota(jnp.int32, t.shape, 1)
-    mine = (rows_of(t.shape) == (my_sub() + members - 14) % members) & (lane == lax.axis_index("group"))
+    mine = (rows_of(t.shape) == (my_sub() + members - LEAD_LAST * lax.axis_size("core")) % members) & (lane == lax.axis_index("group"))
 
     def column(at):
         return shift(t, -at * groups, 1)
@@ -410,7 +409,7 @@
 
 def gather(row, axis, first=0):
     peers = lax.axis_size(axis)
-    order = [[(first + i) % peers for i in range(peers)]] if first else None
+    order = [[(first + i) % peers for i in range(peers)]]
     rows = jnp.broadcast_to(row, (peers, row.shape[1]))[:, None]
     return lax.all_to_all(rows, axis, 0, 0, axis_index_groups=order).reshape(peers, row.shape[1])
 
@@ -422,25 +421,25 @@
     full, wide, layer, edge, row = (cx, cy, cz), (cx + 2, cy, cz), (cy, cz), (cx, cz), (1, LANES)
     rounds = [full, (2,) + wide]
     strip_north, strip_south = call(strips_kernel, [edge, edge], [], perm)
-    halos = over_sub(strip_north, strip_south)
+    perm_north, perm_south = over_sub(strip_north, strip_south)
     source, storage, west, east, *inner, diagonal, sums = call(
         inner_kernel,
         [full, full, layer, layer, (cx + 1, cy, cz)] + [full] * 5 + [row],
         [],
         source, perm, storage, cost=2**21,
     )
-    edge_north, edge_south, to_a, to_b, scalars = call(
+    edge_north, to_a, to_b, scalars = call(
         edge_kernel,
-        [edge, edge, layer, layer, (members, LANES)],
+        [edge, layer, layer, (members, LANES)],
         [],
-        *halos, strip_north, strip_south, west, east, sums,
-    )
-    table = gather(scalars, SUB, 28)
-    edge_east, edge_west, *weights, u0, to_a, to_b, to_north, to_south = call(
+        perm_north, strip_north, west, east, sums,
+    )
+    table = gather(scalars, SUB, LEAD_COARSE)
+    edge_east, edge_west, edge_south, *weights, u0, to_a, to_b, to_north, to_south = call(
         functools.partial(assemble_kernel, steps),
-        [layer, layer] + [full] * 8 + [layer, layer, edge, edge],
+        [layer, layer, edge] + [full] * 7 + [full, layer, layer, edge, edge],
         rounds,
-        *over_group(to_a, to_b), table, source, west, east, *inner, diagonal, edge_north, edge_south,
+        *over_group(to_a, to_b), table, source, west, east, *inner, diagonal, edge_north, perm_south, strip_south,
     )
     outer = [edge_east, edge_west, edge_north, edge_south]
     halos = over_group(to_a, to_b) + over_sub(to_north, to_south)
@@ -460,9 +459,9 @@
         [wide],
         *halos, f1, dots, storage, *inner, *outer,
     )
-    scalars = gather(scalars, ("group", "core"), groups * 5 // 8 * cores)
+    scalars = gather(scalars, ("group", "core"), LEAD_GROUP * cores)
     scalars = sum(scalars[i : i + 1] for i in range(groups * cores))
-    table = gather(scalars, "z", 7).reshape(members, LANES)
+    table = gather(scalars, "z", LEAD_LAST).reshape(members, LANES)
     return tuple(
         call(
             functools.partial(last_kernel, steps, groups),

time: 86.2 us -> 86.1 us (level)
  waiting for transfers between devices: 8.62 us -> 4.01 us
  starting transfers between devices: 44 us -> 48 us
    ppermute x3, waiting for transfers between devices: 2.73 us -> 0.22 us  [over_group(): b = lax.ppermute(to_b, 'group', [(i, i ^ 1) for i in range(groups)])]
    all_to_all x1, starting transfers between devices: 10.2 us -> 12.5 us  [gather(): lax.all_to_all(rows, axis, 0, 0, axis_index_groups=order)]
    ppermute x3, waiting for transfers between devices: 2.89 us -> 0.8 us  [over_sub(): south = lax.ppermute(to_north, SUB, up)]
    ppermute x3, starting transfers between devices: 10.2 us -> 11.7 us  [over_sub(): north = lax.ppermute(to_south, SUB, [(j, i) for i, j in up])]
where the time goes in v9:
time: 86.1 us; the launch traced here: 85.6 us
  starting transfers between devices  48 us (56%)
  blocking collectives  25.4 us (30%)
  Pallas kernels  5.44 us (6%)
  waiting for transfers between devices  4.01 us (5%)
  local copies, waits for them, and re-layouts  1.93 us (2%)
    all_to_all x2, blocking collectives, gather(): lax.all_to_all(rows, axis, 0, 0, axis_index_groups=order)  25.4 us
    ppermute x3, starting transfers between devices, over_group(): lax.ppermute(to_a, 'group', [(i, ((i + 1 ^ 1) - 1) % groups) for i in ran...  16.1 us
    all_to_all x1, starting transfers between devices, gather(): lax.all_to_all(rows, axis, 0, 0, axis_index_groups=order)  12.5 us
    ppermute x3, starting transfers between devices, over_sub(): north = lax.ppermute(to_south, SUB, [(j, i) for i, j in up])  11.7 us
    ppermute x3, starting transfers between devices, over_group(): b = lax.ppermute(to_b, 'group', [(i, i ^ 1) for i in range(groups)])  5.76 us
    pallas_call x9, Pallas kernels, call(): pl.pallas_call(body, out_shape=[jax.ShapeDtypeStruct(s, jnp.float32) for...  5.44 us
    ppermute x3, waiting for transfers between devices, over_sub(): north = lax.ppermute(to_south, SUB, [(j, i) for i, j in up])  2.99 us
    ppermute x3, starting transfers between devices, over_sub(): south = lax.ppermute(to_north, SUB, up)  1.96 us
  transfers between devices with their start and end apart: 13, of which 4 were waited for; matrix products, arithmetic and copies ran while one was open for 0% of the time, Pallas kernels for 1%

profile of v9, /device:TPU:1, one launch (start us, length us, event | category | flops | bytes accessed | tf_op | source)
XLA Modules:
  0.0 85.6 jit_solution(18384634014334980726)
XLA Ops:
  0.6 0.9 %copy-done = f32[8,32,256]{2,1,0:T(8,128)S(1)} copy-done((f32[8,32,256]{2,1,0:T(8,128)S(1)}, f32[8,32,256]{2,1,0:T(8,128)}, u32[]{:S(2)}) %copy-start) | copy-done | bytes 262168
  1.6 6.9 %collective-permute-start = (f32[8,256]{1,0:T(8,128)S(1)}, f32[8,256]{1,0:T(8,128)S(1)}, u32[]{:S(2)}, u32[]{:S(2)}) collective-permute-start(f32[8,256]{1,0:T(8,128)S(1)} %get-tuple-element.42.strip_south), channel_id=1, source_target_pairs={{1,0},{2,1},{3,2},{4,3},{5,4},{6,5},{7,6},{8,7},{9,8},{10,9},{11,1... | collective-permute-start | bytes 24584 | tf_op jit(solution)/shard_map/ppermute | solution.py:406
  8.5 0.9 %copy-done.2 = f32[8,32,256]{2,1,0:T(8,128)S(1)} copy-done((f32[8,32,256]{2,1,0:T(8,128)S(1)}, f32[8,32,256]{2,1,0:T(8,128)}, u32[]{:S(2)}) %copy-start.2) | copy-done | bytes 262168
  9.4 0.4 shard_map.51
  9.8 0.7 shard_map.52
  10.6 12.5 %all-to-all-start = ((f32[32,1,128]{2,1,0:T(1,128)}), f32[32,1,128]{2,1,0:T(1,128)S(1)}, u32[]{:S(2)}, u32[]{:S(2)}) async-start(f32[32,1,128]{2,1,0:T(1,128)} %bitcast.1), calls=%async_computation | async-start | bytes 32768 | tf_op jit(solution)/shard_map/all_to_all | solution.py:414
  23.0 6.8 %collective-permute-start.1 = (f32[32,256]{1,0:T(8,128)S(1)}, f32[32,256]{1,0:T(8,128)S(1)}, u32[]{:S(2)}, u32[]{:S(2)}) collective-permute-start(f32[32,256]{1,0:T(8,128)S(1)} %get-tuple-element.47), channel_id=1, source_target_pairs={{0,480},{32,64},{64,32},{96,128},{128,96},{160,192},{192,160},{224... | collective-permute-start | bytes 98312 | tf_op jit(solution)/shard_map/ppermute | solution.py:397
  29.9 1.9 %collective-permute-start.2 = (f32[32,256]{1,0:T(8,128)S(1)}, f32[32,256]{1,0:T(8,128)S(1)}, u32[]{:S(2)}, u32[]{:S(2)}) collective-permute-start(f32[32,256]{1,0:T(8,128)S(1)} %get-tuple-element.48), channel_id=1, source_target_pairs={{0,32},{32,0},{64,96},{96,64},{128,160},{160,128},{192,224},{224,1... | collective-permute-start | bytes 98312 | tf_op jit(solution)/shard_map/ppermute | solution.py:398
  31.8 1.7 %collective-permute-start.3 = (f32[8,256]{1,0:T(8,128)S(1)}, f32[8,256]{1,0:T(8,128)S(1)}, u32[]{:S(2)}, u32[]{:S(2)}) collective-permute-start(f32[8,256]{1,0:T(8,128)S(1)} %get-tuple-element.43.strip_north), channel_id=1, source_target_pairs={{0,1},{1,2},{2,3},{3,4},{4,5},{5,6},{6,7},{7,8},{8,9},{9,10},{10,1... | collective-permute-start | bytes 24584 | tf_op jit(solution)/shard_map/ppermute | solution.py:405
  33.5 0.8 collective-permute-done.3.perm_south
  34.3 0.0 collective-permute-done.1.perm_a
  34.3 0.2 collective-permute-done.2.perm_b
  34.5 0.8 shard_map.53
  35.4 4.0 %collective-permute-start.4 = (f32[32,256]{1,0:T(8,128)S(1)}, f32[32,256]{1,0:T(8,128)S(1)}, u32[]{:S(2)}, u32[]{:S(2)}) collective-permute-start(f32[32,256]{1,0:T(8,128)S(1)} %get-tuple-element.58), channel_id=1, source_target_pairs={{0,480},{32,64},{64,32},{96,128},{128,96},{160,192},{192,160},{224... | collective-permute-start | bytes 98312 | tf_op jit(solution)/shard_map/ppermute | solution.py:397
  39.4 1.9 %collective-permute-start.5 = (f32[32,256]{1,0:T(8,128)S(1)}, f32[32,256]{1,0:T(8,128)S(1)}, u32[]{:S(2)}, u32[]{:S(2)}) collective-permute-start(f32[32,256]{1,0:T(8,128)S(1)} %get-tuple-element.59), channel_id=1, source_target_pairs={{0,32},{32,0},{64,96},{96,64},{128,160},{160,128},{192,224},{224,1... | collective-permute-start | bytes 98312 | tf_op jit(solution)/shard_map/ppermute | solution.py:398
  41.3 2.2 %collective-permute-start.6 = (f32[8,256]{1,0:T(8,128)S(1)}, f32[8,256]{1,0:T(8,128)S(1)}, u32[]{:S(2)}, u32[]{:S(2)}) collective-permute-start(f32[8,256]{1,0:T(8,128)S(1)} %get-tuple-element.60), channel_id=1, source_target_pairs={{1,0},{2,1},{3,2},{4,3},{5,4},{6,5},{7,6},{8,7},{9,8},{10,9},{11,1... | collective-permute-start | bytes 24584 | tf_op jit(solution)/shard_map/ppermute | solution.py:406
  43.5 0.0 collective-permute-start.7
  43.5 1.6 %collective-permute-done.6.halo_north = f32[8,256]{1,0:T(8,128)S(1)} collective-permute-done((f32[8,256]{1,0:T(8,128)S(1)}, f32[8,256]{1,0:T(8,128)S(1)}, u32[]{:S(2)}, u32[]{:S(2)}) %collective-permute-start.6) | collective-permute-done | bytes 8224 | tf_op jit(solution)/shard_map/ppermute | solution.py:406
  45.1 0.0 collective-permute-done.7.halo_south
  45.2 0.0 collective-permute-done.4.halo_a
  45.2 0.0 collective-permute-done.5.halo_b
  45.2 0.9 %shard_map.54 = (f32[8,32,256]{2,1,0:T(8,128)S(1)}, f32[8,32,256]{2,1,0:T(8,128)S(1)}, f32[8,256]{1,0:T(8,128)S(1)}, f32[8,256]{1,0:T(8,128)S(1)}) custom-call(f32[32,256]{1,0:T(8,128)S(1)} %collective-permute-done.4.halo_a, f32[32,256]{1,0:T(8,128)S(1)} %collective-permute-done.5.halo_b, f32[8,256]{1,0:T(8,128)S(1)} %collective-permute-done.6.halo_north, ...), custom_call_target="tpu_custom_call" | custom-call | tf_op jit(solution)/shard_map/pallas_call | solution.py:384
  46.1 5.3 %collective-permute-start.8 = (f32[32,256]{1,0:T(8,128)S(1)}, f32[32,256]{1,0:T(8,128)S(1)}, u32[]{:S(2)}, u32[]{:S(2)}) collective-permute-start(f32[32,256]{1,0:T(8,128)S(1)} %get-tuple-element.75), channel_id=1, source_target_pairs={{0,480},{32,64},{64,32},{96,128},{128,96},{160,192},{192,160},{224... | collective-permute-start | bytes 98312 | tf_op jit(solution)/shard_map/ppermute | solution.py:397
  51.4 1.9 %collective-permute-start.9 = (f32[32,256]{1,0:T(8,128)S(1)}, f32[32,256]{1,0:T(8,128)S(1)}, u32[]{:S(2)}, u32[]{:S(2)}) collective-permute-start(f32[32,256]{1,0:T(8,128)S(1)} %get-tuple-element.76), channel_id=1, source_target_pairs={{0,32},{32,0},{64,96},{96,64},{128,160},{160,128},{192,224},{224,1... | collective-permute-start | bytes 98312 | tf_op jit(solution)/shard_map/ppermute | solution.py:398
  53.3 2.6 %collective-permute-start.10 = (f32[8,256]{1,0:T(8,128)S(1)}, f32[8,256]{1,0:T(8,128)S(1)}, u32[]{:S(2)}, u32[]{:S(2)}) collective-permute-start(f32[8,256]{1,0:T(8,128)S(1)} %get-tuple-element.77), channel_id=1, source_target_pairs={{1,0},{2,1},{3,2},{4,3},{5,4},{6,5},{7,6},{8,7},{9,8},{10,9},{11,1... | collective-permute-start | bytes 24584 | tf_op jit(solution)/shard_map/ppermute | solution.py:406
  55.9 0.2 collective-permute-start.11
  56.1 0.2 shard_map.56.dots
  56.3 1.4 %collective-permute-done.10.halo_north = f32[8,256]{1,0:T(8,128)S(1)} collective-permute-done((f32[8,256]{1,0:T(8,128)S(1)}, f32[8,256]{1,0:T(8,128)S(1)}, u32[]{:S(2)}, u32[]{:S(2)}) %collective-permute-start.10) | collective-permute-done | bytes 8224 | tf_op jit(solution)/shard_map/ppermute | solution.py:406
  57.7 0.4 shard_map.57
  58.2 12.1 %all_to_all.15 = f32[32,1,256]{2,1,0:T(1,128)S(1)} all-to-all(f32[32,1,256]{2,1,0:T(1,128)S(1)} %broadcast_in_dim_broadcast_in_dim.4), channel_id=1, replica_groups={{320,321,352,353,384,385,416,417,448,449,480,481,0,1,32,33,64,65,96,97,..., dimensions={0} | all-to-all | bytes 65536 | tf_op jit(solution)/shard_map/all_to_all | solution.py:414
  70.4 13.2 %all_to_all.16 = f32[16,1,256]{2,1,0:T(1,128)S(1)} all-to-all(f32[16,1,256]{2,1,0:T(1,128)S(1)} %broadcast_in_dim_broadcast_in_dim.5), channel_id=1, replica_groups={{14,16,18,20,22,24,26,28,30,0,2,4,6,8,10,12},{15,17,19,21,23,25,27,29,3..., dimensions={0} | all-to-all | bytes 32768 | tf_op jit(solution)/shard_map/all_to_all | solution.py:414
  83.6 1.9 %shard_map.58 = (f32[8,32,256]{2,1,0:T(8,128)}, f32[8,32,256]{2,1,0:T(8,128)}) custom-call(f32[32,128]{1,0:T(8,128)S(1)} %bitcast.23, f32[8,32,256]{2,1,0:T(8,128)S(1)} %get-tuple-element.62.u0_ref, f32[8,32,256]{2,1,0:T(8,128)S(1)} %get-tuple-element.74.field.f1_ref, f32[8,32,256]{2,1,0:T(8,128)S(1)} %get-tuple-element.81.image, ...), custom_call_target="tpu_custom_call" | custom-call | tf_op jit(solution)/shard_map/pallas_call | solution.py:384
  (16 shorter events, 0.1 us)
Async XLA Ops:
  0.6 1.0 %copy-start = (f32[8,32,256]{2,1,0:T(8,128)S(1)}, f32[8,32,256]{2,1,0:T(8,128)}, u32[]{:S(2)}) copy-start(f32[8,32,256]{2,1,0:T(8,128)} %perm.1) | copy-start | bytes 786436
  1.6 6.9 %copy-start.1 = (f32[8,32,256]{2,1,0:T(8,128)S(1)}, f32[8,32,256]{2,1,0:T(8,128)}, u32[]{:S(2)}) copy-start(f32[8,32,256]{2,1,0:T(8,128)} %source.1) | copy-start | bytes 786436
  1.6 8.2 %collective-permute-start = (f32[8,256]{1,0:T(8,128)S(1)}, f32[8,256]{1,0:T(8,128)S(1)}, u32[]{:S(2)}, u32[]{:S(2)}) collective-permute-start(f32[8,256]{1,0:T(8,128)S(1)} %get-tuple-element.42.strip_south), channel_id=1, source_target_pairs={{1,0},{2,1},{3,2},{4,3},{5,4},{6,5},{7,6},{8,7},{9,8},{10,9},{11,1... | collective-permute-start | bytes 24584 | tf_op jit(solution)/shard_map/ppermute | solution.py:406
  8.5 1.0 %copy-start.2 = (f32[8,32,256]{2,1,0:T(8,128)S(1)}, f32[8,32,256]{2,1,0:T(8,128)}, u32[]{:S(2)}) copy-start(f32[8,32,256]{2,1,0:T(8,128)} %storage.1) | copy-start | bytes 786436
  10.6 24.0 %all-to-all-start = ((f32[32,1,128]{2,1,0:T(1,128)}), f32[32,1,128]{2,1,0:T(1,128)S(1)}, u32[]{:S(2)}, u32[]{:S(2)}) async-start(f32[32,1,128]{2,1,0:T(1,128)} %bitcast.1), calls=%async_computation | async-start | bytes 32768 | tf_op jit(solution)/shard_map/all_to_all | solution.py:414
  23.0 11.3 %collective-permute-start.1 = (f32[32,256]{1,0:T(8,128)S(1)}, f32[32,256]{1,0:T(8,128)S(1)}, u32[]{:S(2)}, u32[]{:S(2)}) collective-permute-start(f32[32,256]{1,0:T(8,128)S(1)} %get-tuple-element.47), channel_id=1, source_target_pairs={{0,480},{32,64},{64,32},{96,128},{128,96},{160,192},{192,160},{224... | collective-permute-start | bytes 98312 | tf_op jit(solution)/shard_map/ppermute | solution.py:397
  29.9 4.7 %collective-permute-start.2 = (f32[32,256]{1,0:T(8,128)S(1)}, f32[32,256]{1,0:T(8,128)S(1)}, u32[]{:S(2)}, u32[]{:S(2)}) collective-permute-start(f32[32,256]{1,0:T(8,128)S(1)} %get-tuple-element.48), channel_id=1, source_target_pairs={{0,32},{32,0},{64,96},{96,64},{128,160},{160,128},{192,224},{224,1... | collective-permute-start | bytes 98312 | tf_op jit(solution)/shard_map/ppermute | solution.py:398
  31.8 2.5 %collective-permute-start.3 = (f32[8,256]{1,0:T(8,128)S(1)}, f32[8,256]{1,0:T(8,128)S(1)}, u32[]{:S(2)}, u32[]{:S(2)}) collective-permute-start(f32[8,256]{1,0:T(8,128)S(1)} %get-tuple-element.43.strip_north), channel_id=1, source_target_pairs={{0,1},{1,2},{2,3},{3,4},{4,5},{5,6},{6,7},{7,8},{8,9},{9,10},{10,1... | collective-permute-start | bytes 24584 | tf_op jit(solution)/shard_map/ppermute | solution.py:405
  35.4 9.8 %collective-permute-start.4 = (f32[32,256]{1,0:T(8,128)S(1)}, f32[32,256]{1,0:T(8,128)S(1)}, u32[]{:S(2)}, u32[]{:S(2)}) collective-permute-start(f32[32,256]{1,0:T(8,128)S(1)} %get-tuple-element.58), channel_id=1, source_target_pairs={{0,480},{32,64},{64,32},{96,128},{128,96},{160,192},{192,160},{224... | collective-permute-start | bytes 98312 | tf_op jit(solution)/shard_map/ppermute | solution.py:397
  39.4 5.8 %collective-permute-start.5 = (f32[32,256]{1,0:T(8,128)S(1)}, f32[32,256]{1,0:T(8,128)S(1)}, u32[]{:S(2)}, u32[]{:S(2)}) collective-permute-start(f32[32,256]{1,0:T(8,128)S(1)} %get-tuple-element.59), channel_id=1, source_target_pairs={{0,32},{32,0},{64,96},{96,64},{128,160},{160,128},{192,224},{224,1... | collective-permute-start | bytes 98312 | tf_op jit(solution)/shard_map/ppermute | solution.py:398
  41.3 3.8 %collective-permute-start.6 = (f32[8,256]{1,0:T(8,128)S(1)}, f32[8,256]{1,0:T(8,128)S(1)}, u32[]{:S(2)}, u32[]{:S(2)}) collective-permute-start(f32[8,256]{1,0:T(8,128)S(1)} %get-tuple-element.60), channel_id=1, source_target_pairs={{1,0},{2,1},{3,2},{4,3},{5,4},{6,5},{7,6},{8,7},{9,8},{10,9},{11,1... | collective-permute-start | bytes 24584 | tf_op jit(solution)/shard_map/ppermute | solution.py:406
  43.5 1.7 %collective-permute-start.7 = (f32[8,256]{1,0:T(8,128)S(1)}, f32[8,256]{1,0:T(8,128)S(1)}, u32[]{:S(2)}, u32[]{:S(2)}) collective-permute-start(f32[8,256]{1,0:T(8,128)S(1)} %get-tuple-element.61), channel_id=1, source_target_pairs={{0,1},{1,2},{2,3},{3,4},{4,5},{5,6},{6,7},{7,8},{8,9},{9,10},{10,1... | collective-permute-start | bytes 24584 | tf_op jit(solution)/shard_map/ppermute | solution.py:405
  46.1 11.6 %collective-permute-start.8 = (f32[32,256]{1,0:T(8,128)S(1)}, f32[32,256]{1,0:T(8,128)S(1)}, u32[]{:S(2)}, u32[]{:S(2)}) collective-permute-start(f32[32,256]{1,0:T(8,128)S(1)} %get-tuple-element.75), channel_id=1, source_target_pairs={{0,480},{32,64},{64,32},{96,128},{128,96},{160,192},{192,160},{224... | collective-permute-start | bytes 98312 | tf_op jit(solution)/shard_map/ppermute | solution.py:397
  51.4 6.4 %collective-permute-start.9 = (f32[32,256]{1,0:T(8,128)S(1)}, f32[32,256]{1,0:T(8,128)S(1)}, u32[]{:S(2)}, u32[]{:S(2)}) collective-permute-start(f32[32,256]{1,0:T(8,128)S(1)} %get-tuple-element.76), channel_id=1, source_target_pairs={{0,32},{32,0},{64,96},{96,64},{128,160},{160,128},{192,224},{224,1... | collective-permute-start | bytes 98312 | tf_op jit(solution)/shard_map/ppermute | solution.py:398
  53.3 4.4 %collective-permute-start.10 = (f32[8,256]{1,0:T(8,128)S(1)}, f32[8,256]{1,0:T(8,128)S(1)}, u32[]{:S(2)}, u32[]{:S(2)}) collective-permute-start(f32[8,256]{1,0:T(8,128)S(1)} %get-tuple-element.77), channel_id=1, source_target_pairs={{1,0},{2,1},{3,2},{4,3},{5,4},{6,5},{7,6},{8,7},{9,8},{10,9},{11,1... | collective-permute-start | bytes 24584 | tf_op jit(solution)/shard_map/ppermute | solution.py:406
  55.9 1.8 %collective-permute-start.11 = (f32[8,256]{1,0:T(8,128)S(1)}, f32[8,256]{1,0:T(8,128)S(1)}, u32[]{:S(2)}, u32[]{:S(2)}) collective-permute-start(f32[8,256]{1,0:T(8,128)S(1)} %get-tuple-element.78), channel_id=1, source_target_pairs={{0,1},{1,2},{2,3},{3,4},{4,5},{5,6},{6,7},{7,8},{8,9},{9,10},{10,1... | collective-permute-start | bytes 24584 | tf_op jit(solution)/shard_map/ppermute | solution.py:405

commit v10 on v9

--- a/solution.py
+++ b/solution.py
@@ -83,7 +83,7 @@
 
 def apply(padded, north_halo, south_halo, storage, inner, edges, out):
     cx, cy = storage.shape[:2]
-    east_t, north_t, south_t, upper_t, lower_t = inner
+    east_t, north_t, _, upper_t, _ = inner
     edge_east, edge_west, edge_north, edge_south = edges
 
     def slab(x, carry):
@@ -91,8 +91,10 @@
         row = rows_of(u.shape)
         total = storage[x] * u
         total = total + east_t[x + 1] * (u - padded[x + 2]) + east_t[x] * (u - padded[x])
-        total = total + north_t[x] * (u - shift(u, -1, 0)) + south_t[x] * (u - shift(u, 1, 0))
-        total = total + upper_t[x] * (u - shift(u, -1, 1)) + lower_t[x] * (u - shift(u, 1, 1))
+        flux = north_t[x] * (u - shift(u, -1, 0))
+        total = total + flux - shift(flux, 1, 0)
+        flux = upper_t[x] * (u - shift(u, -1, 1))
+        total = total + flux - shift(flux, 1, 1)
         one = pl.ds(x, 1)
         north = jnp.where(row == cy - 1, edge_north[one] * (u - north_halo[one]), 0.0)
         total = total + jnp.where(row == 0, edge_south[one] * (u - south_halo[one]), north)
@@ -334,20 +336,8 @@
         stored * c1 + after * (c1 - c_north) + shift(after, 1, 0) * (c1 - c_south)
         + right * (c1 - c_east) + to_the_west(right) * (c1 - c_west)
     )
-    c2 = solve_rows(factors, last, image_sum + coupled)
-    valid = lane < groups
-    sums = jnp.sum(t, axis=0, keepdims=True)
-    r_u0, u0_v0, v0_u1, u1_v1 = (sums[:, DOTS + at : DOTS + at + 1] for at in range(4))
-    v0_u1 = v0_u1 + total_of(jnp.where(valid, c1 * against, 0.0))
-    u1_v1 = u1_v1 + total_of(jnp.where(valid, c1 * (2.0 * image_sum + coupled), 0.0))
-    c1, c_east, c_west, c_north, c_south, c2 = (pick(c) for c in (c1, c_east, c_west, c_north, c_south, c2))
-
-    a0 = r_u0 / u0_v0
-    rz = a0 * a0 * v0_u1 - r_u0
-    keep = 1.0 + rz / r_u0
-    a1 = rz / (keep * keep * u0_v0 - 2.0 * keep * a0 * v0_u1 + a0 * a0 * u1_v1)
-    p0, p1 = a0 + a1 * keep, a1 * a0
-
+    c1_all = c1
+    c1, c_east, c_west, c_north, c_south = (pick(c) for c in (c1, c_east, c_west, c_north, c_south))
     def send(at, x):
         src, dst = ((pressure, pressure_out), (precond, precond_out))[at]
         copy = pltpu.make_async_copy(src.at[x], dst.at[x], sems.at[at, x])
@@ -357,8 +347,6 @@
     copies = []
     row = rows_of((cy, cz))
     for x in range(cx):
-        pressure[x] = p0 * u0_ref[x] - p1 * (f1_ref[x] + c1)
-        copies.append(send(0, x))
         one = slice(x, x + 1)
         edge = jnp.where(row == 0, edge_south[one] * (c1 - c_south), 0.0)
         edge = jnp.where(row == cy - 1, edge_north[one] * (c1 - c_north), edge)
@@ -372,7 +360,23 @@
         work[0, x + 1] = s
     clear_ends(work)
     smooth(first, work, (w_east, w_west, w_north, w_south, w_upper, w_lower))
-    for x in range(cx):
+    c2 = solve_rows(factors, last, image_sum + coupled)
+    valid = lane < groups
+    sums = jnp.sum(t, axis=0, keepdims=True)
+    r_u0, u0_v0, v0_u1, u1_v1 = (sums[:, DOTS + at : DOTS + at + 1] for at in range(4))
+    v0_u1 = v0_u1 + total_of(jnp.where(valid, c1_all * against, 0.0))
+    u1_v1 = u1_v1 + total_of(jnp.where(valid, c1_all * (2.0 * image_sum + coupled), 0.0))
+
+    c2 = pick(c2)
+    a0 = r_u0 / u0_v0
+    rz = a0 * a0 * v0_u1 - r_u0
+    keep = 1.0 + rz / r_u0
+    a1 = rz / (keep * keep * u0_v0 - 2.0 * keep * a0 * v0_u1 + a0 * a0 * u1_v1)
+    p0, p1 = a0 + a1 * keep, a1 * a0
+
+    for x in range(cx):
+        pressure[x] = p0 * u0_ref[x] - p1 * (f1_ref[x] + c1)
+        copies.append(send(0, x))
         precond[x] = u0_ref[x] - p0 * (f1_ref[x] + c1) + p1 * (work[1, x + 1] + c2)
         copies.append(send(1, x))
     for copy in copies:

time: 86.1 us -> 86.2 us (level)
  no operation moved by 1% of the time
where the time goes in v10:
time: 86.2 us; the launch traced here: 85.7 us
  starting transfers between devices  48 us (56%)
  blocking collectives  25.4 us (29%)
  Pallas kernels  5.56 us (6%)
  waiting for transfers between devices  4.01 us (5%)
  local copies, waits for them, and re-layouts  1.93 us (2%)
    all_to_all x2, blocking collectives, gather(): lax.all_to_all(rows, axis, 0, 0, axis_index_groups=order)  25.4 us
    ppermute x3, starting transfers between devices, over_group(): lax.ppermute(to_a, 'group', [(i, ((i + 1 ^ 1) - 1) % groups) for i in ran...  16.1 us
    all_to_all x1, starting transfers between devices, gather(): lax.all_to_all(rows, axis, 0, 0, axis_index_groups=order)  12.5 us
    ppermute x3, starting transfers between devices, over_sub(): north = lax.ppermute(to_south, SUB, [(j, i) for i, j in up])  11.7 us
    ppermute x3, starting transfers between devices, over_group(): b = lax.ppermute(to_b, 'group', [(i, i ^ 1) for i in range(groups)])  5.76 us
    pallas_call x9, Pallas kernels, call(): pl.pallas_call(body, out_shape=[jax.ShapeDtypeStruct(s, jnp.float32) for...  5.56 us
    ppermute x3, waiting for transfers between devices, over_sub(): north = lax.ppermute(to_south, SUB, [(j, i) for i, j in up])  2.99 us
    ppermute x3, starting transfers between devices, over_sub(): south = lax.ppermute(to_north, SUB, up)  1.96 us
  transfers between devices with their start and end apart: 13, of which 4 were waited for; matrix products, arithmetic and copies ran while one was open for 0% of the time, Pallas kernels for 1%

profile of v10, /device:TPU:1, one launch (start us, length us, event | category | flops | bytes accessed | tf_op | source)
XLA Modules:
  0.0 85.7 jit_solution(4541695365216214391)
XLA Ops:
  0.6 0.9 %copy-done = f32[8,32,256]{2,1,0:T(8,128)S(1)} copy-done((f32[8,32,256]{2,1,0:T(8,128)S(1)}, f32[8,32,256]{2,1,0:T(8,128)}, u32[]{:S(2)}) %copy-start) | copy-done | bytes 262168
  1.6 6.9 %collective-permute-start = (f32[8,256]{1,0:T(8,128)S(1)}, f32[8,256]{1,0:T(8,128)S(1)}, u32[]{:S(2)}, u32[]{:S(2)}) collective-permute-start(f32[8,256]{1,0:T(8,128)S(1)} %get-tuple-element.42.strip_south), channel_id=1, source_target_pairs={{1,0},{2,1},{3,2},{4,3},{5,4},{6,5},{7,6},{8,7},{9,8},{10,9},{11,1... | collective-permute-start | bytes 24584 | tf_op jit(solution)/shard_map/ppermute | solution.py:410
  8.5 0.9 %copy-done.2 = f32[8,32,256]{2,1,0:T(8,128)S(1)} copy-done((f32[8,32,256]{2,1,0:T(8,128)S(1)}, f32[8,32,256]{2,1,0:T(8,128)}, u32[]{:S(2)}) %copy-start.2) | copy-done | bytes 262168
  9.4 0.4 shard_map.51
  9.8 0.7 shard_map.52
  10.6 12.5 %all-to-all-start = ((f32[32,1,128]{2,1,0:T(1,128)}), f32[32,1,128]{2,1,0:T(1,128)S(1)}, u32[]{:S(2)}, u32[]{:S(2)}) async-start(f32[32,1,128]{2,1,0:T(1,128)} %bitcast.1), calls=%async_computation | async-start | bytes 32768 | tf_op jit(solution)/shard_map/all_to_all | solution.py:418
  23.0 6.8 %collective-permute-start.1 = (f32[32,256]{1,0:T(8,128)S(1)}, f32[32,256]{1,0:T(8,128)S(1)}, u32[]{:S(2)}, u32[]{:S(2)}) collective-permute-start(f32[32,256]{1,0:T(8,128)S(1)} %get-tuple-element.47), channel_id=1, source_target_pairs={{0,480},{32,64},{64,32},{96,128},{128,96},{160,192},{192,160},{224... | collective-permute-start | bytes 98312 | tf_op jit(solution)/shard_map/ppermute | solution.py:401
  29.9 1.9 %collective-permute-start.2 = (f32[32,256]{1,0:T(8,128)S(1)}, f32[32,256]{1,0:T(8,128)S(1)}, u32[]{:S(2)}, u32[]{:S(2)}) collective-permute-start(f32[32,256]{1,0:T(8,128)S(1)} %get-tuple-element.48), channel_id=1, source_target_pairs={{0,32},{32,0},{64,96},{96,64},{128,160},{160,128},{192,224},{224,1... | collective-permute-start | bytes 98312 | tf_op jit(solution)/shard_map/ppermute | solution.py:402
  31.8 1.7 %collective-permute-start.3 = (f32[8,256]{1,0:T(8,128)S(1)}, f32[8,256]{1,0:T(8,128)S(1)}, u32[]{:S(2)}, u32[]{:S(2)}) collective-permute-start(f32[8,256]{1,0:T(8,128)S(1)} %get-tuple-element.43.strip_north), channel_id=1, source_target_pairs={{0,1},{1,2},{2,3},{3,4},{4,5},{5,6},{6,7},{7,8},{8,9},{9,10},{10,1... | collective-permute-start | bytes 24584 | tf_op jit(solution)/shard_map/ppermute | solution.py:409
  33.5 0.8 collective-permute-done.3.perm_south
  34.3 0.0 collective-permute-done.1.perm_a
  34.3 0.2 collective-permute-done.2.perm_b
  34.5 0.8 shard_map.53
  35.4 4.0 %collective-permute-start.4 = (f32[32,256]{1,0:T(8,128)S(1)}, f32[32,256]{1,0:T(8,128)S(1)}, u32[]{:S(2)}, u32[]{:S(2)}) collective-permute-start(f32[32,256]{1,0:T(8,128)S(1)} %get-tuple-element.58), channel_id=1, source_target_pairs={{0,480},{32,64},{64,32},{96,128},{128,96},{160,192},{192,160},{224... | collective-permute-start | bytes 98312 | tf_op jit(solution)/shard_map/ppermute | solution.py:401
  39.4 1.9 %collective-permute-start.5 = (f32[32,256]{1,0:T(8,128)S(1)}, f32[32,256]{1,0:T(8,128)S(1)}, u32[]{:S(2)}, u32[]{:S(2)}) collective-permute-start(f32[32,256]{1,0:T(8,128)S(1)} %get-tuple-element.59), channel_id=1, source_target_pairs={{0,32},{32,0},{64,96},{96,64},{128,160},{160,128},{192,224},{224,1... | collective-permute-start | bytes 98312 | tf_op jit(solution)/shard_map/ppermute | solution.py:402
  41.3 2.2 %collective-permute-start.6 = (f32[8,256]{1,0:T(8,128)S(1)}, f32[8,256]{1,0:T(8,128)S(1)}, u32[]{:S(2)}, u32[]{:S(2)}) collective-permute-start(f32[8,256]{1,0:T(8,128)S(1)} %get-tuple-element.60), channel_id=1, source_target_pairs={{1,0},{2,1},{3,2},{4,3},{5,4},{6,5},{7,6},{8,7},{9,8},{10,9},{11,1... | collective-permute-start | bytes 24584 | tf_op jit(solution)/shard_map/ppermute | solution.py:410
  43.5 0.0 collective-permute-start.7
  43.5 1.6 %collective-permute-done.6.halo_north = f32[8,256]{1,0:T(8,128)S(1)} collective-permute-done((f32[8,256]{1,0:T(8,128)S(1)}, f32[8,256]{1,0:T(8,128)S(1)}, u32[]{:S(2)}, u32[]{:S(2)}) %collective-permute-start.6) | collective-permute-done | bytes 8224 | tf_op jit(solution)/shard_map/ppermute | solution.py:410
  45.1 0.0 collective-permute-done.7.halo_south
  45.2 0.0 collective-permute-done.4.halo_a
  45.2 0.0 collective-permute-done.5.halo_b
  45.2 1.0 %shard_map.54 = (f32[8,32,256]{2,1,0:T(8,128)S(1)}, f32[8,32,256]{2,1,0:T(8,128)S(1)}, f32[8,256]{1,0:T(8,128)S(1)}, f32[8,256]{1,0:T(8,128)S(1)}) custom-call(f32[32,256]{1,0:T(8,128)S(1)} %collective-permute-done.4.halo_a, f32[32,256]{1,0:T(8,128)S(1)} %collective-permute-done.5.halo_b, f32[8,256]{1,0:T(8,128)S(1)} %collective-permute-done.6.halo_north, ...), custom_call_target="tpu_custom_call" | custom-call | tf_op jit(solution)/shard_map/pallas_call | solution.py:388
  46.2 5.3 %collective-permute-start.8 = (f32[32,256]{1,0:T(8,128)S(1)}, f32[32,256]{1,0:T(8,128)S(1)}, u32[]{:S(2)}, u32[]{:S(2)}) collective-permute-start(f32[32,256]{1,0:T(8,128)S(1)} %get-tuple-element.75), channel_id=1, source_target_pairs={{0,480},{32,64},{64,32},{96,128},{128,96},{160,192},{192,160},{224... | collective-permute-start | bytes 98312 | tf_op jit(solution)/shard_map/ppermute | solution.py:401
  51.5 1.9 %collective-permute-start.9 = (f32[32,256]{1,0:T(8,128)S(1)}, f32[32,256]{1,0:T(8,128)S(1)}, u32[]{:S(2)}, u32[]{:S(2)}) collective-permute-start(f32[32,256]{1,0:T(8,128)S(1)} %get-tuple-element.76), channel_id=1, source_target_pairs={{0,32},{32,0},{64,96},{96,64},{128,160},{160,128},{192,224},{224,1... | collective-permute-start | bytes 98312 | tf_op jit(solution)/shard_map/ppermute | solution.py:402
  53.4 2.6 %collective-permute-start.10 = (f32[8,256]{1,0:T(8,128)S(1)}, f32[8,256]{1,0:T(8,128)S(1)}, u32[]{:S(2)}, u32[]{:S(2)}) collective-permute-start(f32[8,256]{1,0:T(8,128)S(1)} %get-tuple-element.77), channel_id=1, source_target_pairs={{1,0},{2,1},{3,2},{4,3},{5,4},{6,5},{7,6},{8,7},{9,8},{10,9},{11,1... | collective-permute-start | bytes 24584 | tf_op jit(solution)/shard_map/ppermute | solution.py:410
  56.1 0.2 collective-permute-start.11
  56.3 0.2 shard_map.56.dots
  56.5 1.4 %collective-permute-done.10.halo_north = f32[8,256]{1,0:T(8,128)S(1)} collective-permute-done((f32[8,256]{1,0:T(8,128)S(1)}, f32[8,256]{1,0:T(8,128)S(1)}, u32[]{:S(2)}, u32[]{:S(2)}) %collective-permute-start.10) | collective-permute-done | bytes 8224 | tf_op jit(solution)/shard_map/ppermute | solution.py:410
  57.9 0.4 shard_map.57
  58.3 12.1 %all_to_all.15 = f32[32,1,256]{2,1,0:T(1,128)S(1)} all-to-all(f32[32,1,256]{2,1,0:T(1,128)S(1)} %broadcast_in_dim_broadcast_in_dim.4), channel_id=1, replica_groups={{320,321,352,353,384,385,416,417,448,449,480,481,0,1,32,33,64,65,96,97,..., dimensions={0} | all-to-all | bytes 65536 | tf_op jit(solution)/shard_map/all_to_all | solution.py:418
  70.6 13.2 %all_to_all.16 = f32[16,1,256]{2,1,0:T(1,128)S(1)} all-to-all(f32[16,1,256]{2,1,0:T(1,128)S(1)} %broadcast_in_dim_broadcast_in_dim.5), channel_id=1, replica_groups={{14,16,18,20,22,24,26,28,30,0,2,4,6,8,10,12},{15,17,19,21,23,25,27,29,3..., dimensions={0} | all-to-all | bytes 32768 | tf_op jit(solution)/shard_map/all_to_all | solution.py:418
  83.8 1.9 %shard_map.58 = (f32[8,32,256]{2,1,0:T(8,128)}, f32[8,32,256]{2,1,0:T(8,128)}) custom-call(f32[32,128]{1,0:T(8,128)S(1)} %bitcast.23, f32[8,32,256]{2,1,0:T(8,128)S(1)} %get-tuple-element.62.u0_ref, f32[8,32,256]{2,1,0:T(8,128)S(1)} %get-tuple-element.74.field.f1_ref, f32[8,32,256]{2,1,0:T(8,128)S(1)} %get-tuple-element.81.image, ...), custom_call_target="tpu_custom_call" | custom-call | tf_op jit(solution)/shard_map/pallas_call | solution.py:388
  (16 shorter events, 0.1 us)
Async XLA Ops:
  0.6 1.0 %copy-start = (f32[8,32,256]{2,1,0:T(8,128)S(1)}, f32[8,32,256]{2,1,0:T(8,128)}, u32[]{:S(2)}) copy-start(f32[8,32,256]{2,1,0:T(8,128)} %perm.1) | copy-start | bytes 786436
  1.6 6.9 %copy-start.1 = (f32[8,32,256]{2,1,0:T(8,128)S(1)}, f32[8,32,256]{2,1,0:T(8,128)}, u32[]{:S(2)}) copy-start(f32[8,32,256]{2,1,0:T(8,128)} %source.1) | copy-start | bytes 786436
  1.6 8.2 %collective-permute-start = (f32[8,256]{1,0:T(8,128)S(1)}, f32[8,256]{1,0:T(8,128)S(1)}, u32[]{:S(2)}, u32[]{:S(2)}) collective-permute-start(f32[8,256]{1,0:T(8,128)S(1)} %get-tuple-element.42.strip_south), channel_id=1, source_target_pairs={{1,0},{2,1},{3,2},{4,3},{5,4},{6,5},{7,6},{8,7},{9,8},{10,9},{11,1... | collective-permute-start | bytes 24584 | tf_op jit(solution)/shard_map/ppermute | solution.py:410
  8.5 1.0 %copy-start.2 = (f32[8,32,256]{2,1,0:T(8,128)S(1)}, f32[8,32,256]{2,1,0:T(8,128)}, u32[]{:S(2)}) copy-start(f32[8,32,256]{2,1,0:T(8,128)} %storage.1) | copy-start | bytes 786436
  10.6 24.0 %all-to-all-start = ((f32[32,1,128]{2,1,0:T(1,128)}), f32[32,1,128]{2,1,0:T(1,128)S(1)}, u32[]{:S(2)}, u32[]{:S(2)}) async-start(f32[32,1,128]{2,1,0:T(1,128)} %bitcast.1), calls=%async_computation | async-start | bytes 32768 | tf_op jit(solution)/shard_map/all_to_all | solution.py:418
  23.0 11.3 %collective-permute-start.1 = (f32[32,256]{1,0:T(8,128)S(1)}, f32[32,256]{1,0:T(8,128)S(1)}, u32[]{:S(2)}, u32[]{:S(2)}) collective-permute-start(f32[32,256]{1,0:T(8,128)S(1)} %get-tuple-element.47), channel_id=1, source_target_pairs={{0,480},{32,64},{64,32},{96,128},{128,96},{160,192},{192,160},{224... | collective-permute-start | bytes 98312 | tf_op jit(solution)/shard_map/ppermute | solution.py:401
  29.9 4.7 %collective-permute-start.2 = (f32[32,256]{1,0:T(8,128)S(1)}, f32[32,256]{1,0:T(8,128)S(1)}, u32[]{:S(2)}, u32[]{:S(2)}) collective-permute-start(f32[32,256]{1,0:T(8,128)S(1)} %get-tuple-element.48), channel_id=1, source_target_pairs={{0,32},{32,0},{64,96},{96,64},{128,160},{160,128},{192,224},{224,1... | collective-permute-start | bytes 98312 | tf_op jit(solution)/shard_map/ppermute | solution.py:402
  31.8 2.5 %collective-permute-start.3 = (f32[8,256]{1,0:T(8,128)S(1)}, f32[8,256]{1,0:T(8,128)S(1)}, u32[]{:S(2)}, u32[]{:S(2)}) collective-permute-start(f32[8,256]{1,0:T(8,128)S(1)} %get-tuple-element.43.strip_north), channel_id=1, source_target_pairs={{0,1},{1,2},{2,3},{3,4},{4,5},{5,6},{6,7},{7,8},{8,9},{9,10},{10,1... | collective-permute-start | bytes 24584 | tf_op jit(solution)/shard_map/ppermute | solution.py:409
  35.4 9.8 %collective-permute-start.4 = (f32[32,256]{1,0:T(8,128)S(1)}, f32[32,256]{1,0:T(8,128)S(1)}, u32[]{:S(2)}, u32[]{:S(2)}) collective-permute-start(f32[32,256]{1,0:T(8,128)S(1)} %get-tuple-element.58), channel_id=1, source_target_pairs={{0,480},{32,64},{64,32},{96,128},{128,96},{160,192},{192,160},{224... | collective-permute-start | bytes 98312 | tf_op jit(solution)/shard_map/ppermute | solution.py:401
  39.4 5.8 %collective-permute-start.5 = (f32[32,256]{1,0:T(8,128)S(1)}, f32[32,256]{1,0:T(8,128)S(1)}, u32[]{:S(2)}, u32[]{:S(2)}) collective-permute-start(f32[32,256]{1,0:T(8,128)S(1)} %get-tuple-element.59), channel_id=1, source_target_pairs={{0,32},{32,0},{64,96},{96,64},{128,160},{160,128},{192,224},{224,1... | collective-permute-start | bytes 98312 | tf_op jit(solution)/shard_map/ppermute | solution.py:402
  41.3 3.8 %collective-permute-start.6 = (f32[8,256]{1,0:T(8,128)S(1)}, f32[8,256]{1,0:T(8,128)S(1)}, u32[]{:S(2)}, u32[]{:S(2)}) collective-permute-start(f32[8,256]{1,0:T(8,128)S(1)} %get-tuple-element.60), channel_id=1, source_target_pairs={{1,0},{2,1},{3,2},{4,3},{5,4},{6,5},{7,6},{8,7},{9,8},{10,9},{11,1... | collective-permute-start | bytes 24584 | tf_op jit(solution)/shard_map/ppermute | solution.py:410
  43.5 1.7 %collective-permute-start.7 = (f32[8,256]{1,0:T(8,128)S(1)}, f32[8,256]{1,0:T(8,128)S(1)}, u32[]{:S(2)}, u32[]{:S(2)}) collective-permute-start(f32[8,256]{1,0:T(8,128)S(1)} %get-tuple-element.61), channel_id=1, source_target_pairs={{0,1},{1,2},{2,3},{3,4},{4,5},{5,6},{6,7},{7,8},{8,9},{9,10},{10,1... | collective-permute-start | bytes 24584 | tf_op jit(solution)/shard_map/ppermute | solution.py:409
  46.2 11.6 %collective-permute-start.8 = (f32[32,256]{1,0:T(8,128)S(1)}, f32[32,256]{1,0:T(8,128)S(1)}, u32[]{:S(2)}, u32[]{:S(2)}) collective-permute-start(f32[32,256]{1,0:T(8,128)S(1)} %get-tuple-element.75), channel_id=1, source_target_pairs={{0,480},{32,64},{64,32},{96,128},{128,96},{160,192},{192,160},{224... | collective-permute-start | bytes 98312 | tf_op jit(solution)/shard_map/ppermute | solution.py:401
  51.5 6.4 %collective-permute-start.9 = (f32[32,256]{1,0:T(8,128)S(1)}, f32[32,256]{1,0:T(8,128)S(1)}, u32[]{:S(2)}, u32[]{:S(2)}) collective-permute-start(f32[32,256]{1,0:T(8,128)S(1)} %get-tuple-element.76), channel_id=1, source_target_pairs={{0,32},{32,0},{64,96},{96,64},{128,160},{160,128},{192,224},{224,1... | collective-permute-start | bytes 98312 | tf_op jit(solution)/shard_map/ppermute | solution.py:402
  53.4 4.4 %collective-permute-start.10 = (f32[8,256]{1,0:T(8,128)S(1)}, f32[8,256]{1,0:T(8,128)S(1)}, u32[]{:S(2)}, u32[]{:S(2)}) collective-permute-start(f32[8,256]{1,0:T(8,128)S(1)} %get-tuple-element.77), channel_id=1, source_target_pairs={{1,0},{2,1},{3,2},{4,3},{5,4},{6,5},{7,6},{8,7},{9,8},{10,9},{11,1... | collective-permute-start | bytes 24584 | tf_op jit(solution)/shard_map/ppermute | solution.py:410
  56.1 1.8 %collective-permute-start.11 = (f32[8,256]{1,0:T(8,128)S(1)}, f32[8,256]{1,0:T(8,128)S(1)}, u32[]{:S(2)}, u32[]{:S(2)}) collective-permute-start(f32[8,256]{1,0:T(8,128)S(1)} %get-tuple-element.78), channel_id=1, source_target_pairs={{0,1},{1,2},{2,3},{3,4},{4,5},{5,6},{6,7},{7,8},{8,9},{9,10},{10,1... | collective-permute-start | bytes 24584 | tf_op jit(solution)/shard_map/ppermute | solution.py:409
